TPU v7x, 128 devices: a whole 4x4x4 slice. The times are simulated.
128 devices in a mesh: grp: 4 (over x), scan: 32 (over z, y, core).
Axes of the slice: x: 4, y: 4, z: 4, core: 2. Of those that a mesh axis runs over, the one named last changes fastest.
Arguments:
- amplitude: float32 [512, 256, 256], P(('grp', 'scan')), may hold values from 0 to 3
- positions: int32 [512, 2], P(('grp', 'scan')), may hold values from 0 to 7936, as said below
- owner_perm: int32 [4, 32], replicated, may hold values from 0 to 31, each once within a row
- object_tiles: float32 [8192, 2, 4096], P(('grp', 'scan')), may hold values from -6 to 6
- probe: float32 [4, 2, 256, 256], P('grp'), may hold values from -6 to 6
Outputs:
- object_out: float32 [8192, 2, 4096], P(('grp', 'scan'))
- probe_out: float32 [4, 2, 256, 256], P('grp')
Inputs may be any that keep to these rules, and one draw needn't show every extreme that they name: `positions`: each row is a pattern's top-left pixel (row, column), both multiples of 128. The 4 patterns of one device (consecutive rows) share their row and stand 2 * 64 pixels apart in column, the first leftmost. The patterns of group g of the grp axis lie inside tile rows g * 32 to (g + 1) * 32 - 1, and every window lies inside the object. `owner_perm`: row g maps the 32 owner classes of band g one to one onto the devices of the scan axis.
All inputs are finite; a program needn't handle non-finite values.
Results may differ from a plain program's by a relative error of at most 0.0003.
Values sent between devices are 32-bit elements; how exact they have to be, the bound alone decides.
No kernel may reach another device: no remote copies, remote signals or barrier semaphores. Data moves between devices by JAX's collectives and lax.ppermute only.
A program may use at most 128 MiB of HBM per device.

v0:
```python
import math

import jax
import jax.numpy as jnp
from jax import lax
from jax.sharding import PartitionSpec as P

OBJ_COLS = 64
ITERS = 2


PROBE_STEP = 0.03125


def dft_tables(patch_side):
    counter = lax.iota(jnp.int32, patch_side)
    phase_index = counter[:, None] * counter[None, :] % patch_side
    angles = phase_index.astype(jnp.float32) * (2.0 * math.pi / patch_side)
    factor = 1.0 / math.sqrt(patch_side)
    return (jnp.cos(angles) * factor, -jnp.sin(angles) * factor)


def product(spec, first, second):
    return jnp.einsum(spec, first, second, precision=lax.Precision.HIGHEST)


def both_sides(real_part, imag_part, table_re, table_im):
    left_re = product("mn,...np->...mp", table_re, real_part) - product(
        "mn,...np->...mp", table_im, imag_part
    )
    left_im = product("mn,...np->...mp", table_re, imag_part) + product(
        "mn,...np->...mp", table_im, real_part
    )
    right_re = product("...mn,np->...mp", left_re, table_re) - product(
        "...mn,np->...mp", left_im, table_im
    )
    right_im = product("...mn,np->...mp", left_re, table_im) + product(
        "...mn,np->...mp", left_im, table_re
    )
    return (right_re, right_im)


def body(amplitude, positions, owner_perm, object_tiles, probe):
    n_scan = lax.axis_size("scan")
    band_index = lax.axis_index("grp")
    pat_count = amplitude.shape[0]
    patch_side = amplitude.shape[-1]
    tile_side = patch_side // 4
    tile_area = tile_side * tile_side
    tiles_dev = object_tiles.shape[0]
    col_classes = n_scan // 8
    strip_cols = 2 * pat_count + 2
    capacity = (strip_cols + col_classes - 1) // col_classes
    band_rows = n_scan * tiles_dev // OBJ_COLS
    slot_count = n_scan * capacity
    needed = 4 * strip_cols
    row_first = positions[0, 0] // tile_side - band_index * band_rows
    col_first = positions[0, 1] // tile_side
    rows_in = row_first + jnp.repeat(jnp.arange(4, dtype=jnp.int32), strip_cols)
    cols_in = col_first + jnp.tile(jnp.arange(strip_cols, dtype=jnp.int32), 4)
    classes = rows_in % 8 * col_classes + cols_in % col_classes
    perm_row = lax.dynamic_index_in_dim(owner_perm, band_index, 0, keepdims=False)
    owner_dev = jnp.sum(
        jnp.where(
            classes[:, None] == jnp.arange(n_scan, dtype=jnp.int32)[None, :], perm_row[None, :], 0
        ),
        axis=1,
    )
    slot_ids = rows_in // 8 * (OBJ_COLS // col_classes) + cols_in // col_classes
    request_order = jnp.arange(needed, dtype=jnp.int32)
    earlier = (owner_dev[None, :] == owner_dev[:, None]) & (
        request_order[None, :] < request_order[:, None]
    )
    rank_within = jnp.sum(earlier.astype(jnp.int32), axis=1)
    target = owner_dev * capacity + rank_within
    matches = target[None, :] == jnp.arange(slot_count, dtype=jnp.int32)[:, None]
    request = jnp.sum(jnp.where(matches, slot_ids[None, :], 0), axis=1).reshape(n_scan, capacity)
    source = jnp.sum(jnp.where(matches, request_order[None, :] + 1, 0), axis=1) - 1
    source = jnp.where(source < 0, needed, source)
    served = lax.all_to_all(request, "scan", split_axis=0, concat_axis=0, tiled=True).reshape(
        slot_count
    )
    placing = (served[:, None] == jnp.arange(tiles_dev, dtype=jnp.int32)[None, :]).astype(
        jnp.float32
    )
    table_re, table_im = dft_tables(patch_side)
    current = object_tiles
    own_probe = probe
    for iteration in range(ITERS):
        modes_all = lax.all_gather(own_probe, "grp", axis=0, tiled=True)
        probe_re = modes_all[:, 0]
        probe_im = modes_all[:, 1]
        probe_peak = jnp.max(jnp.sum(probe_re * probe_re + probe_im * probe_im, axis=0)) + 1e-06
        outgoing = jnp.take(current, served, axis=0).reshape(n_scan, capacity, 2, tile_area)
        arrived = lax.all_to_all(outgoing, "scan", split_axis=0, concat_axis=0, tiled=True).reshape(
            slot_count, 2, tile_area
        )
        mine = jnp.take(arrived, target, axis=0).reshape(4, strip_cols, 2, tile_side, tile_side)
        strip = mine.transpose(2, 0, 3, 1, 4).reshape(2, patch_side, strip_cols * tile_side)
        windows = jnp.stack(
            [
                strip[:, :, 2 * p * tile_side : 2 * p * tile_side + patch_side]
                for p in range(pat_count)
            ],
            axis=0,
        )
        patch_re = windows[:, 0]
        patch_im = windows[:, 1]
        exit_re = probe_re[None] * patch_re[:, None] - probe_im[None] * patch_im[:, None]
        exit_im = probe_re[None] * patch_im[:, None] + probe_im[None] * patch_re[:, None]
        far_re, far_im = both_sides(exit_re, exit_im, table_re, table_im)
        intensity = jnp.sum(far_re * far_re + far_im * far_im, axis=1)
        keeping = (1.0 - amplitude / jnp.sqrt(intensity + 1.0))[:, None]
        chi_re, chi_im = both_sides(far_re * keeping, far_im * keeping, table_re, -table_im)
        grad_re = jnp.sum(probe_re[None] * chi_re + probe_im[None] * chi_im, axis=1)
        grad_im = jnp.sum(probe_re[None] * chi_im - probe_im[None] * chi_re, axis=1)
        probe_grad_re = jnp.sum(patch_re[:, None] * chi_re + patch_im[:, None] * chi_im, axis=0)
        probe_grad_im = jnp.sum(patch_re[:, None] * chi_im - patch_im[:, None] * chi_re, axis=0)
        probe_grad = jnp.stack([probe_grad_re, probe_grad_im], axis=1)
        strip_grad = jnp.zeros((2, patch_side, strip_cols * tile_side), jnp.float32)
        for p in range(pat_count):
            start_col = 2 * p * tile_side
            pattern_grad = jnp.stack([grad_re[p], grad_im[p]], axis=0)
            strip_grad = strip_grad.at[:, :, start_col : start_col + patch_side].add(pattern_grad)
        grad_tiles = strip_grad.reshape(2, 4, tile_side, strip_cols, tile_side).transpose(
            1, 3, 0, 2, 4
        )
        grad_tiles = grad_tiles.reshape(needed, 2, tile_area)
        padded = jnp.concatenate([grad_tiles, jnp.zeros((1, 2, tile_area), jnp.float32)], axis=0)
        returning = jnp.take(padded, source, axis=0).reshape(n_scan, capacity, 2, tile_area)
        received = lax.all_to_all(
            returning, "scan", split_axis=0, concat_axis=0, tiled=True
        ).reshape(slot_count, 2 * tile_area)
        object_grad = jnp.dot(placing.T, received, precision=lax.Precision.HIGHEST).reshape(
            tiles_dev, 2, tile_area
        )
        current = current - object_grad / probe_peak
        owned_sum = lax.psum_scatter(probe_grad, "grp", scatter_dimension=0, tiled=True)
        owned_sum = lax.psum(owned_sum, "scan")
        own_probe = own_probe - owned_sum * PROBE_STEP
    return (current, own_probe)


def solution(mesh):
    in_specs = (
        P(("grp", "scan"), None, None),
        P(("grp", "scan"), None),
        P(),
        P(("grp", "scan"), None, None),
        P("grp", None, None, None),
    )
    out_specs = (P(("grp", "scan"), None, None), P("grp", None, None, None))
    return jax.shard_map(body, mesh=mesh, in_specs=in_specs, out_specs=out_specs, check_vma=False)
```

profile of v0, /device:TPU:1, one launch (start us, length us, event | category | flops | bytes accessed | tf_op | source)
XLA Modules:
  0.0 811.2 jit_solution(12842025136307305710)
XLA Ops:
  14.4 16.3 %all_to_all.29 = s32[32,1,3]{2,1,0:T(1,128)S(1)} all-to-all(s32[32,1,3]{2,1,0:T(1,128)S(1)} %bitcast.260), channel_id=1, replica_groups=mesh['grp'=4,'scan'=32] {'scan'}, dimensions={0} | all-to-all | bytes 768 | tf_op jit(solution)/shard_map/all_to_all | solution.py:80
  32.1 9.4 %gather_fusion = f32[96,2,4096]{2,1,0:T(2,128)S(1)} fusion(f32[64,2,4096]{2,1,0:T(2,128)} %param.30, s32[1024]{0:T(1024)S(1)} %pad_clamp_fusion.2), kind=kCustom, calls=%fused_computation.clone | custom fusion | bytes 6291840 | tf_op jit(solution)/shard_map/jit(_take)/gather | solution.py:94
  41.4 3.7 broadcast_select_fusion.3
  45.1 4.4 all-to-all-start.1
  50.3 38.5 %all-to-all-done.1 = f32[32,3,2,4096]{3,2,1,0:T(2,128)S(1)} async-done(((f32[32,3,2,4096]{3,2,1,0:T(2,128)}), f32[32,3,2,4096]{3,2,1,0:T(2,128)S(1)}, u32[]{:S(2)}, u32[]{:S(2)}) %all-to-all-start.1) | async-done | bytes 3145760 | tf_op jit(solution)/shard_map/all_to_all | solution.py:95
  88.7 3.2 gather_fusion.1
  100.7 2.9 reshape.410
  106.6 8.2 %fusion.39 = f32[4,4,256,256]{3,2,1,0:T(8,128)S(1)} fusion(f32[4,256,256]{2,1,0:T(8,128)S(1)} %copy.207, f32[4,256,256]{2,1,0:T(8,128)S(1)} %get-tuple-element.134, f32[4,256,256]{2,1,0:T(8,128)S(1)} %copy.206, f32[4,256,256]{2,1,0:T(8,128)S(1)} %get-tuple-element.133), kind=kOutput, calls=%fused_computation.60 | convolution fusion | flops 3225419776 | bytes 8388608 | tf_op jit(solution)/shard_map/mn,...np->...mp/dot_general | solution.py:24
  114.7 8.4 %fusion.38 = f32[4,4,256,256]{3,2,1,0:T(8,128)S(1)} fusion(f32[4,256,256]{2,1,0:T(8,128)S(1)} %copy.207, f32[4,256,256]{2,1,0:T(8,128)S(1)} %get-tuple-element.134, f32[4,256,256]{2,1,0:T(8,128)S(1)} %copy.206, f32[4,256,256]{2,1,0:T(8,128)S(1)} %get-tuple-element.133), kind=kOutput, calls=%fused_computation.59 | convolution fusion | flops 3225354240 | bytes 8388608 | tf_op jit(solution)/shard_map/mn,...np->...mp/dot_general | solution.py:24
  123.1 8.4 %fusion.129 = f32[4,4,256,256]{3,2,1,0:T(8,128)S(1)} fusion(f32[4,4,256,256]{3,2,1,0:T(8,128)S(1)} %fusion.38, f32[4,256,256]{2,1,0:T(8,128)S(1)} %copy.207, f32[4,256,256]{2,1,0:T(8,128)S(1)} %get-tuple-element.134, f32[4,256,256]{2,1,0:T(8,128)S(1)} %copy.206, f32[4,256,256]{2,1,0:T(8,128)S(1)} %get-tuple-element.133), kind=kOutput, calls=%fused_computation.135 | convolution fusion | flops 3226468352 | bytes 12582912 | tf_op jit(solution)/shard_map/mn,...np->...mp/dot_general | solution.py:24
  131.6 8.2 %fusion.26 = f32[4,4,256,256]{3,2,1,0:T(8,128)S(1)} fusion(f32[4,4,256,256]{3,2,1,0:T(8,128)S(1)} %fusion.129), kind=kOutput, calls=%fused_computation.34 | convolution fusion | flops 3222208512 | bytes 8388608 | tf_op jit(solution)/shard_map/...mn,np->...mp/dot_general | solution.py:24
  139.7 8.3 %fusion.28 = f32[4,4,256,256]{3,2,1,0:T(8,128)S(1)} fusion(f32[4,4,256,256]{3,2,1,0:T(8,128)S(1)} %fusion.129), kind=kOutput, calls=%fused_computation.36 | convolution fusion | flops 3222274048 | bytes 8388608 | tf_op jit(solution)/shard_map/...mn,np->...mp/dot_general | solution.py:24
  148.1 8.5 %fusion.128 = f32[4,4,256,256]{3,2,1,0:T(8,128)S(1)} fusion(f32[4,4,256,256]{3,2,1,0:T(8,128)S(1)} %fusion.39, f32[4,256,256]{2,1,0:T(8,128)S(1)} %copy.207, f32[4,256,256]{2,1,0:T(8,128)S(1)} %get-tuple-element.134, f32[4,256,256]{2,1,0:T(8,128)S(1)} %copy.206, f32[4,256,256]{2,1,0:T(8,128)S(1)} %get-tuple-element.133), kind=kOutput, calls=%fused_computation.134 | convolution fusion | flops 3226402816 | bytes 12582912 | tf_op jit(solution)/shard_map/mn,...np->...mp/dot_general | solution.py:24
  156.5 8.0 fusion.74
  164.6 9.0 %add_reduce_fusion.5 = (f32[4,256,256]{2,1,0:T(8,128)S(1)}, f32[4,4,256,256]{3,2,1,0:T(8,128)S(1)}) fusion(f32[4,4,256,256]{3,2,1,0:T(8,128)S(1)} %fusion.74, f32[4,4,256,256]{3,2,1,0:T(8,128)S(1)} %fusion.26, f32[4,4,256,256]{3,2,1,0:T(8,128)S(1)} %fusion.128), kind=kOutput, calls=%fused_computation.57 | convolution fusion | flops 3227254784 | bytes 17825792 | tf_op jit(solution)/shard_map/...mn,np->...mp/dot_general | solution.py:24
  173.7 8.2 %fusion.52 = f32[4,4,256,256]{3,2,1,0:T(8,128)S(1)} fusion(f32[4,4,256,256]{3,2,1,0:T(8,128)S(1)} %get-tuple-element.166, f32[4,256,256]{2,1,0:T(8,128)S(1)} %multiply_subtract_fusion.15), kind=kOutput, calls=%fused_computation.74 | convolution fusion | flops 3223388160 | bytes 9437184 | tf_op jit(solution)/shard_map/mn,...np->...mp/dot_general | solution.py:24
  181.9 8.1 fusion.50
  190.0 8.3 %fusion.65 = f32[4,4,256,256]{3,2,1,0:T(8,128)S(1)} fusion(f32[4,4,256,256]{3,2,1,0:T(8,128)S(1)} %fusion.50, f32[4,4,256,256]{3,2,1,0:T(8,128)S(1)} %fusion.74, f32[4,256,256]{2,1,0:T(8,128)S(1)} %multiply_subtract_fusion.15), kind=kOutput, calls=%fused_computation.89 | convolution fusion | flops 3224436736 | bytes 13631488 | tf_op jit(solution)/shard_map/mn,...np->...mp/dot_general | solution.py:24
  198.3 8.0 fusion.18
  206.3 8.4 %fusion.20 = f32[4,4,256,256]{3,2,1,0:T(8,128)S(1)} fusion(f32[4,4,256,256]{3,2,1,0:T(8,128)S(1)} %fusion.65), kind=kOutput, calls=%fused_computation.28 | convolution fusion | flops 3222339584 | bytes 8388608 | tf_op jit(solution)/shard_map/...mn,np->...mp/dot_general | solution.py:24
  214.7 8.3 %fusion.62 = f32[4,4,256,256]{3,2,1,0:T(8,128)S(1)} fusion(f32[4,4,256,256]{3,2,1,0:T(8,128)S(1)} %fusion.52, f32[4,4,256,256]{3,2,1,0:T(8,128)S(1)} %fusion.74, f32[4,256,256]{2,1,0:T(8,128)S(1)} %multiply_subtract_fusion.15), kind=kOutput, calls=%fused_computation.88 | convolution fusion | flops 3224305664 | bytes 13631488 | tf_op jit(solution)/shard_map/mn,...np->...mp/dot_general | solution.py:24
  223.1 8.0 fusion.80
  231.1 12.4 %add_reduce_fusion.3 = (f32[4,256,256]{2,1,0:T(8,128)}, f32[4,256,256]{2,1,0:T(8,128)}, f32[4,256,256]{2,1,0:T(8,128)S(1)}, f32[4,256,256]{2,1,0:T(8,128)S(1)}) fusion(f32[4,4,256,256]{3,2,1,0:T(8,128)S(1)} %fusion.80, f32[4,256,256]{2,1,0:T(8,128)S(1)} %copy.207, f32[4,256,256]{2,1,0:T(8,128)S(1)} %copy.206, f32[4,256,256]{2,1,0:T(8,128)S(1)} %get-tuple-element.134, ...), kind=kOutput, calls=%fused_computation.54 | convolution fusion | flops 3239116800 | bytes 20971520 | tf_op jit(solution)/shard_map/...mn,np->...mp/dot_general | solution.py:24
  247.9 2.9 copy.290
  250.8 3.1 reshape.493
  254.7 8.1 gather_fusion.2
  262.8 6.5 broadcast_select_fusion.1
  269.3 7.4 all-to-all-start.2
  277.0 2.9 pad_maximum_fusion.1
  281.4 34.6 %all-to-all-done.2 = f32[32,3,2,4096]{3,2,1,0:T(2,128)} async-done(((f32[32,3,2,4096]{3,2,1,0:T(2,128)}), f32[32,3,2,4096]{3,2,1,0:T(2,128)}, u32[]{:S(2)}, u32[]{:S(2)}) %all-to-all-start.2) | async-done | bytes 3145760 | tf_op jit(solution)/shard_map/all_to_all | solution.py:131
  316.0 6.8 fusion
  325.8 8.1 gather_fusion.3
  333.9 6.5 broadcast_select_fusion.2
  340.4 7.1 all-to-all-start.3
  348.3 123.4 %all-reduce.7.cloned.1.call-done = f32[1,2,256,256]{3,2,1,0:T(8,128)} async-done(((f32[1,2,256,256]{3,2,1,0:T(8,128)}), f32[1,2,256,256]{3,2,1,0:T(8,128)}) %all-reduce.7.cloned.1.call-update) | async-done | bytes 524304 | tf_op jit(solution)/shard_map/psum | solution.py:139
  473.8 3.2 gather_fusion.4
  477.0 3.4 broadcast_select_fusion.4
  489.6 14.5 %all-gather.5.cloned.1.call-done = f32[4,2,256,256]{3,2,1,0:T(8,128)} async-done(((f32[1,2,256,256]{3,2,1,0:T(8,128)}), f32[4,2,256,256]{3,2,1,0:T(8,128)}) %all-gather.5.cloned.1.call-update) | async-done | bytes 2097168 | tf_op jit(solution)/shard_map/all_gather | solution.py:90
  505.9 8.2 %fusion.35 = f32[4,4,256,256]{3,2,1,0:T(8,128)S(1)} fusion(f32[4,256,256]{2,1,0:T(8,128)S(1)} %copy.233, f32[4,256,256]{2,1,0:T(8,128)S(1)} %get-tuple-element.130, f32[4,256,256]{2,1,0:T(8,128)S(1)} %copy.232, f32[4,256,256]{2,1,0:T(8,128)S(1)} %get-tuple-element.129), kind=kOutput, calls=%fused_computation.49 | convolution fusion | flops 3225419776 | bytes 8388608 | tf_op jit(solution)/shard_map/mn,...np->...mp/dot_general | solution.py:24
  514.1 8.3 %fusion.34 = f32[4,4,256,256]{3,2,1,0:T(8,128)S(1)} fusion(f32[4,256,256]{2,1,0:T(8,128)S(1)} %copy.233, f32[4,256,256]{2,1,0:T(8,128)S(1)} %get-tuple-element.130, f32[4,256,256]{2,1,0:T(8,128)S(1)} %copy.232, f32[4,256,256]{2,1,0:T(8,128)S(1)} %get-tuple-element.129), kind=kOutput, calls=%fused_computation.48 | convolution fusion | flops 3225354240 | bytes 8388608 | tf_op jit(solution)/shard_map/mn,...np->...mp/dot_general | solution.py:24
  522.4 8.2 %fusion.107 = f32[4,4,256,256]{3,2,1,0:T(8,128)S(1)} fusion(f32[4,4,256,256]{3,2,1,0:T(8,128)S(1)} %fusion.34, f32[4,256,256]{2,1,0:T(8,128)S(1)} %copy.233, f32[4,256,256]{2,1,0:T(8,128)S(1)} %get-tuple-element.130, f32[4,256,256]{2,1,0:T(8,128)S(1)} %copy.232, f32[4,256,256]{2,1,0:T(8,128)S(1)} %get-tuple-element.129), kind=kOutput, calls=%fused_computation.113 | convolution fusion | flops 3226468352 | bytes 12582912 | tf_op jit(solution)/shard_map/mn,...np->...mp/dot_general | solution.py:24
  530.7 8.2 %fusion.10 = f32[4,4,256,256]{3,2,1,0:T(8,128)S(1)} fusion(f32[4,4,256,256]{3,2,1,0:T(8,128)S(1)} %fusion.107), kind=kOutput, calls=%fused_computation.18 | convolution fusion | flops 3222208512 | bytes 8388608 | tf_op jit(solution)/shard_map/...mn,np->...mp/dot_general | solution.py:24
  538.8 8.6 %fusion.12 = f32[4,4,256,256]{3,2,1,0:T(8,128)S(1)} fusion(f32[4,4,256,256]{3,2,1,0:T(8,128)S(1)} %fusion.107), kind=kOutput, calls=%fused_computation.20 | convolution fusion | flops 3222274048 | bytes 8388608 | tf_op jit(solution)/shard_map/...mn,np->...mp/dot_general | solution.py:24
  547.4 8.4 %fusion.106 = f32[4,4,256,256]{3,2,1,0:T(8,128)S(1)} fusion(f32[4,4,256,256]{3,2,1,0:T(8,128)S(1)} %fusion.35, f32[4,256,256]{2,1,0:T(8,128)S(1)} %copy.233, f32[4,256,256]{2,1,0:T(8,128)S(1)} %get-tuple-element.130, f32[4,256,256]{2,1,0:T(8,128)S(1)} %copy.232, f32[4,256,256]{2,1,0:T(8,128)S(1)} %get-tuple-element.129), kind=kOutput, calls=%fused_computation.112 | convolution fusion | flops 3226402816 | bytes 12582912 | tf_op jit(solution)/shard_map/mn,...np->...mp/dot_general | solution.py:24
  555.9 8.0 fusion.86
  563.9 8.8 %add_reduce_fusion.2 = (f32[4,256,256]{2,1,0:T(8,128)S(1)}, f32[4,4,256,256]{3,2,1,0:T(8,128)S(1)}) fusion(f32[4,4,256,256]{3,2,1,0:T(8,128)S(1)} %fusion.86, f32[4,4,256,256]{3,2,1,0:T(8,128)S(1)} %fusion.10, f32[4,4,256,256]{3,2,1,0:T(8,128)S(1)} %fusion.106), kind=kOutput, calls=%fused_computation.46 | convolution fusion | flops 3227254784 | bytes 17825792 | tf_op jit(solution)/shard_map/...mn,np->...mp/dot_general | solution.py:24
  572.9 8.4 %fusion.44 = f32[4,4,256,256]{3,2,1,0:T(8,128)S(1)} fusion(f32[4,4,256,256]{3,2,1,0:T(8,128)S(1)} %get-tuple-element.168, f32[4,256,256]{2,1,0:T(8,128)S(1)} %multiply_subtract_fusion.14), kind=kOutput, calls=%fused_computation.66 | convolution fusion | flops 3223388160 | bytes 9437184 | tf_op jit(solution)/shard_map/mn,...np->...mp/dot_general | solution.py:24
  581.3 8.1 fusion.42
  589.3 8.3 %fusion.71 = f32[4,4,256,256]{3,2,1,0:T(8,128)S(1)} fusion(f32[4,4,256,256]{3,2,1,0:T(8,128)S(1)} %fusion.42, f32[4,4,256,256]{3,2,1,0:T(8,128)S(1)} %fusion.86, f32[4,256,256]{2,1,0:T(8,128)S(1)} %multiply_subtract_fusion.14), kind=kOutput, calls=%fused_computation.91 | convolution fusion | flops 3224436736 | bytes 13631488 | tf_op jit(solution)/shard_map/mn,...np->...mp/dot_general | solution.py:24
  597.6 8.0 fusion.2
  605.6 8.2 %fusion.4 = f32[4,4,256,256]{3,2,1,0:T(8,128)S(1)} fusion(f32[4,4,256,256]{3,2,1,0:T(8,128)S(1)} %fusion.71), kind=kOutput, calls=%fused_computation.12 | convolution fusion | flops 3222339584 | bytes 8388608 | tf_op jit(solution)/shard_map/...mn,np->...mp/dot_general | solution.py:24
  613.8 8.6 %fusion.68 = f32[4,4,256,256]{3,2,1,0:T(8,128)S(1)} fusion(f32[4,4,256,256]{3,2,1,0:T(8,128)S(1)} %fusion.44, f32[4,4,256,256]{3,2,1,0:T(8,128)S(1)} %fusion.86, f32[4,256,256]{2,1,0:T(8,128)S(1)} %multiply_subtract_fusion.14), kind=kOutput, calls=%fused_computation.90 | convolution fusion | flops 3224305664 | bytes 13631488 | tf_op jit(solution)/shard_map/mn,...np->...mp/dot_general | solution.py:24
  622.4 8.0 fusion.92
  630.5 12.3 %add_reduce_fusion = (f32[4,256,256]{2,1,0:T(8,128)S(1)}, f32[4,256,256]{2,1,0:T(8,128)}, f32[4,256,256]{2,1,0:T(8,128)}, f32[4,256,256]{2,1,0:T(8,128)S(1)}) fusion(f32[4,4,256,256]{3,2,1,0:T(8,128)S(1)} %fusion.92, f32[4,256,256]{2,1,0:T(8,128)S(1)} %copy.233, f32[4,256,256]{2,1,0:T(8,128)S(1)} %copy.232, f32[4,256,256]{2,1,0:T(8,128)S(1)} %get-tuple-element.130, ...), kind=kOutput, calls=%fused_computation.43 | convolution fusion | flops 3239116800 | bytes 20971520 | tf_op jit(solution)/shard_map/...mn,np->...mp/dot_general | solution.py:24
  642.8 2.9 pad_maximum_fusion.3
  650.1 2.9 copy.291
  653.1 2.9 reshape.494
  656.8 8.1 gather_fusion.5
  664.9 6.6 broadcast_select_fusion
  671.4 7.9 all-to-all-start.4
  681.1 37.6 %all-to-all-done.4 = f32[32,3,2,4096]{3,2,1,0:T(2,128)} async-done(((f32[32,3,2,4096]{3,2,1,0:T(2,128)}), f32[32,3,2,4096]{3,2,1,0:T(2,128)}, u32[]{:S(2)}, u32[]{:S(2)}) %all-to-all-start.4) | async-done | bytes 3145760 | tf_op jit(solution)/shard_map/all_to_all | solution.py:131
  718.7 5.8 fusion.1
  724.5 2.9 copy.254
  727.4 74.7 %all-reduce.9.cloned.1.call-done = f32[1,2,256,256]{3,2,1,0:T(8,128)} async-done(((f32[1,2,256,256]{3,2,1,0:T(8,128)}), f32[1,2,256,256]{3,2,1,0:T(8,128)}) %all-reduce.9.cloned.1.call-update) | async-done | bytes 524304 | tf_op jit(solution)/shard_map/psum | solution.py:139
  (104 shorter events, 47.2 us)
Async XLA Ops:
  7.2 6.7 copy-start
  45.1 43.6 %all-to-all-start.1 = ((f32[32,3,2,4096]{3,2,1,0:T(2,128)}), f32[32,3,2,4096]{3,2,1,0:T(2,128)S(1)}, u32[]{:S(2)}, u32[]{:S(2)}) async-start(f32[32,3,2,4096]{3,2,1,0:T(2,128)} %bitcast.6), calls=%async_computation.1 | async-start | bytes 6291456 | tf_op jit(solution)/shard_map/all_to_all | solution.py:95
  49.5 55.3 %all-gather.3.cloned.1.call-start = ((), (), s32[]{:S(2)}) async-start(), calls=%async_computation.7 | async-start | bytes 2621440 | tf_op jit(solution)/shard_map/all_gather | solution.py:90
  164.6 9.0 %copy-start.5 = (f32[4,256,256]{2,1,0:T(8,128)S(1)}, f32[4,256,256]{2,1,0:T(8,128)}, u32[]{:S(2)}) copy-start(f32[4,256,256]{2,1,0:T(8,128)} %param.27) | copy-start | bytes 3145732
  269.3 7.6 copy-start.8
  269.3 46.7 %all-to-all-start.2 = ((f32[32,3,2,4096]{3,2,1,0:T(2,128)}), f32[32,3,2,4096]{3,2,1,0:T(2,128)}, u32[]{:S(2)}, u32[]{:S(2)}) async-start(f32[32,3,2,4096]{3,2,1,0:T(2,128)} %bitcast.30), calls=%async_computation.2 | async-start | bytes 6291456 | tf_op jit(solution)/shard_map/all_to_all | solution.py:131
  276.7 3.2 copy-start.2
  276.7 70.8 %reduce-scatter.3.cloned.1.call-start = ((), (), s32[]{:S(2)}) async-start(), calls=%async_computation.8 | async-start | bytes 2621440 | tf_op jit(solution)/shard_map/reduce_scatter | solution.py:138
  322.9 1.3 copy-start.9
  340.4 133.4 %all-to-all-start.3 = ((f32[32,3,2,4096]{3,2,1,0:T(2,128)}), f32[32,3,2,4096]{3,2,1,0:T(2,128)S(1)}, u32[]{:S(2)}, u32[]{:S(2)}) async-start(f32[32,3,2,4096]{3,2,1,0:T(2,128)} %bitcast.35), calls=%async_computation.4 | async-start | bytes 6291456 | tf_op jit(solution)/shard_map/all_to_all | solution.py:95
  347.5 124.2 %all-reduce.7.cloned.1.call-start = ((), (), s32[]{:S(2)}) async-start(), calls=%async_computation.9 | async-start | bytes 1048576 | tf_op jit(solution)/shard_map/psum | solution.py:139
  348.2 155.9 %all-gather.5.cloned.1.call-start = ((), (), s32[]{:S(2)}) async-start(), calls=%async_computation.10 | async-start | bytes 2621440 | tf_op jit(solution)/shard_map/all_gather | solution.py:90
  473.7 207.3 %reduce-scatter.5.cloned.1.call-start = ((), (), s32[]{:S(2)}) async-start(), calls=%async_computation.11 | async-start | bytes 2621440 | tf_op jit(solution)/shard_map/reduce_scatter | solution.py:138
  563.9 8.8 %copy-start.6 = (f32[4,256,256]{2,1,0:T(8,128)S(1)}, f32[4,256,256]{2,1,0:T(8,128)}, u32[]{:S(2)}) copy-start(f32[4,256,256]{2,1,0:T(8,128)} %param.27) | copy-start | bytes 3145732
  642.8 2.9 copy-start.7
  671.4 8.2 %copy-start.3 = (f32[4,2,256,256]{3,2,1,0:T(8,128)S(1)}, f32[4,2,256,256]{3,2,1,0:T(8,128)}, u32[]{:S(2)}) copy-start(f32[4,2,256,256]{3,2,1,0:T(8,128)} %all-gather.5.cloned.1.call-done) | copy-start | bytes 6291460
  671.4 47.2 %all-to-all-start.4 = ((f32[32,3,2,4096]{3,2,1,0:T(2,128)}), f32[32,3,2,4096]{3,2,1,0:T(2,128)}, u32[]{:S(2)}, u32[]{:S(2)}) async-start(f32[32,3,2,4096]{3,2,1,0:T(2,128)} %bitcast.50), calls=%async_computation.5 | async-start | bytes 6291456 | tf_op jit(solution)/shard_map/all_to_all | solution.py:131
  679.3 122.8 %all-reduce.9.cloned.1.call-start = ((), (), s32[]{:S(2)}) async-start(), calls=%async_computation.12 | async-start | bytes 1048576 | tf_op jit(solution)/shard_map/psum | solution.py:139
  718.7 85.4 %copy-start.1 = (s32[4,32]{1,0:T(4,128)S(1)}, s32[4,32]{1,0:T(4,128)}, u32[]{:S(2)}) copy-start(s32[4,32]{1,0:T(4,128)} %param.29) | copy-start | bytes 1540
  724.5 77.7 %copy-start.4 = (f32[1,2,256,256]{3,2,1,0:T(8,128)S(1)}, f32[1,2,256,256]{3,2,1,0:T(8,128)}, u32[]{:S(2)}) copy-start(f32[1,2,256,256]{3,2,1,0:T(8,128)} %multiply_subtract_fusion.17) | copy-start | bytes 1572868
Sparse Core Ops, SparseCore 0:
  52.0 31.8 all-gather.2
  280.0 30.7 reduce-scatter.2
  351.8 119.7 all-reduce.6
  473.9 30.2 all-gather.4
  645.8 29.7 reduce-scatter.4
  683.4 118.7 all-reduce.8
where the time goes:
time: 817 us; the launch traced here: 811 us
  waiting for transfers between devices  324 us (40%)
  matrix products  286 us (35%)
  local copies, waits for them, and re-layouts  92.5 us (11%)
  other arithmetic  42.6 us (5%)
  starting transfers between devices  27.9 us (3%)
  between operations  21.6 us (3%)
  blocking collectives  16.3 us (2%)
    dot_general x32, matrix products, product(): return jnp.einsum(spec, first, second, precision=lax.Precision.HIGHEST)  273 us
    psum x2, waiting for transfers between devices, body(): owned_sum = lax.psum(owned_sum, 'scan')  198 us
    all_to_all x2, waiting for transfers between devices, body(): lax.all_to_all(returning, 'scan', split_axis=0, concat_axis=0, tiled=True)  72.2 us
    all_to_all x2, waiting for transfers between devices, body(): lax.all_to_all(outgoing, 'scan', split_axis=0, concat_axis=0, tiled=True)  38.5 us
    gather x2, local copies, waits for them, and re-layouts, body(): jnp.take(current, served, axis=0).reshape(n_scan, capacity, 2, tile_area)  17.4 us
    all_to_all x1, blocking collectives, body(): lax.all_to_all(request, 'scan', split_axis=0, concat_axis=0, tiled=True)  16.3 us
  transfers between devices with their start and end apart: 10, of which 6 were waited for; matrix products, arithmetic and copies ran while one was open for 12% of the time, Pallas kernels for 0%

commit v1 on v0

v1 whole, which is shorter than its diff:
```python
import functools
import math

import jax
import jax.numpy as jnp
import ml_dtypes
import numpy as np
from jax import lax
from jax.experimental import pallas as pl
from jax.experimental.pallas import tpu as pltpu
from jax.sharding import PartitionSpec as P

SIDE = 256
HALF = 128
TILE = 64
MODES = 4
PATS = 4
N_SCAN = 32
N_GRP = 4
BAND_ROWS = 32
GROUPS = 5
PROBE_STEP = 0.03125
OBJ_ROWS = 2 * GROUPS * 8
PRB_ROWS = 64
SEND_ROWS = OBJ_ROWS + PRB_ROWS
F32 = jnp.float32
BF16 = jnp.bfloat16


def row_of_position():
    return np.array([64 * r + 2 * q + h for r in range(2) for h in range(2) for q in range(32)])


def split_table(table):
    high = table.astype(ml_dtypes.bfloat16)
    low = (table - high.astype(np.float64)).astype(ml_dtypes.bfloat16)
    return high, low


def dft_tables():
    j = np.arange(HALF)[None, :]

    def real_form(n, odd):
        angle = 2.0 * math.pi * ((n[:, None] * (2 * j + odd)) % SIDE) / SIDE
        c, s = np.cos(angle) / 16.0, np.sin(angle) / 16.0
        return np.block([[c, -s], [s, c]])

    lanes = np.arange(HALF)
    rows = row_of_position()
    right, left = [], []
    for odd in (0, 1):
        for table in (real_form(lanes, odd), real_form(lanes, odd).T):
            high, low = split_table(table)
            right.append(np.concatenate([high, low, high], axis=0))
        for table in (real_form(rows, odd).T, real_form(rows, odd)):
            high, low = split_table(table)
            left.append(np.concatenate([high, low, high], axis=1))
    return np.stack(right), np.stack(left)


def split(x):
    high = x.astype(BF16)
    return high, (x - high.astype(F32)).astype(BF16)


def from_right(x, table):
    high, low = split(x)
    return jnp.dot(jnp.concatenate([high, high, low], axis=1), table, preferred_element_type=F32)


def from_left(table, x):
    high, low = split(x)
    return jnp.dot(table, jnp.concatenate([high, high, low], axis=0), preferred_element_type=F32)


def gradients(strip, probe, amp, right, left, far, sgrad, pgrad, weight):
    sgrad[...] = jnp.zeros_like(sgrad)
    pgrad[...] = jnp.zeros_like(pgrad)
    weight[...] = jnp.zeros_like(weight)

    def patch_block(p, c, rh, u):
        return strip[c, p + u, rh * HALF : (rh + 1) * HALF, :]

    def one_pattern(p, carry):
        bright = [None, None]
        for k in range(MODES):
            sums, diffs = [], []
            for rh in range(2):
                wave = []
                for u in range(2):
                    o_re, o_im = patch_block(p, 0, rh, u), patch_block(p, 1, rh, u)
                    p_re, p_im = probe[k, rh, 0, u], probe[k, rh, 1, u]
                    wave.append((p_re * o_re - p_im * o_im, p_re * o_im + p_im * o_re))
                sums.append(jnp.concatenate([wave[0][0] + wave[1][0], wave[0][1] + wave[1][1]], axis=1))
                diffs.append(jnp.concatenate([wave[0][0] - wave[1][0], wave[0][1] - wave[1][1]], axis=1))
            even = from_right(jnp.concatenate(sums, axis=0), right[0])
            odd = from_right(jnp.concatenate(diffs, axis=0), right[2])
            for eo in range(2):
                if eo == 0:
                    e, o = even[:HALF] + even[HALF:], odd[:HALF] + odd[HALF:]
                else:
                    e, o = even[:HALF] - even[HALF:], odd[:HALF] - odd[HALF:]
                stacked = jnp.concatenate(
                    [
                        jnp.concatenate([e[:, :HALF], o[:, :HALF]], axis=1),
                        jnp.concatenate([e[:, HALF:], o[:, HALF:]], axis=1),
                    ],
                    axis=0,
                )
                wave = from_left(left[2 * eo], stacked)
                far[k, eo] = wave
                power = wave[:HALF] * wave[:HALF] + wave[HALF:] * wave[HALF:]
                bright[eo] = power if k == 0 else bright[eo] + power
        scale = [amp[p, eo] * lax.rsqrt(bright[eo] + 1.0) for eo in range(2)]
        obj = {}
        for k in range(MODES):
            part = []
            for eo in range(2):
                wave = far[k, eo]
                cut = jnp.concatenate([wave[:HALF] * scale[eo], wave[HALF:] * scale[eo]], axis=0)
                part.append(from_left(left[2 * eo + 1], cut))
            top, low = part[0] + part[1], part[0] - part[1]
            rows_e = jnp.concatenate(
                [jnp.concatenate([w[:HALF, :HALF], w[HALF:, :HALF]], axis=1) for w in (top, low)], axis=0
            )
            rows_o = jnp.concatenate(
                [jnp.concatenate([w[:HALF, HALF:], w[HALF:, HALF:]], axis=1) for w in (top, low)], axis=0
            )
            even = from_right(rows_e, right[1])
            odd = from_right(rows_o, right[3])
            for u in range(2):
                psi = even + odd if u == 0 else even - odd
                for rh in range(2):
                    rows = slice(rh * HALF, (rh + 1) * HALF)
                    s_re, s_im = psi[rows, :HALF], psi[rows, HALF:]
                    o_re, o_im = patch_block(p, 0, rh, u), patch_block(p, 1, rh, u)
                    p_re, p_im = probe[k, rh, 0, u], probe[k, rh, 1, u]
                    g_re = p_re * s_re + p_im * s_im
                    g_im = p_re * s_im - p_im * s_re
                    if k == 0:
                        obj[u, rh] = (g_re, g_im)
                    else:
                        obj[u, rh] = (obj[u, rh][0] + g_re, obj[u, rh][1] + g_im)
                    pgrad[rh, k, 0, u] -= o_re * s_re + o_im * s_im
                    pgrad[rh, k, 1, u] -= o_re * s_im - o_im * s_re
        for u in range(2):
            for rh in range(2):
                o_re, o_im = patch_block(p, 0, rh, u), patch_block(p, 1, rh, u)
                power = 0.0
                for k in range(MODES):
                    p_re, p_im = probe[k, rh, 0, u], probe[k, rh, 1, u]
                    power = power + (p_re * p_re + p_im * p_im)
                rows = slice(rh * HALF, (rh + 1) * HALF)
                sgrad[0, p + u, rows, :] += power * o_re - obj[u, rh][0]
                sgrad[1, p + u, rows, :] += power * o_im - obj[u, rh][1]
                weight[rh, u] += o_re * o_re + o_im * o_im
        return carry

    lax.fori_loop(0, PATS, one_pattern, 0)
    for k in range(MODES):
        for rh in range(2):
            for c in range(2):
                for u in range(2):
                    pgrad[rh, k, c, u] += weight[rh, u] * probe[k, rh, c, u]


def peak_of(probe):
    most = None
    for rh in range(2):
        for u in range(2):
            power = 0.0
            for k in range(MODES):
                p_re, p_im = probe[k, rh, 0, u], probe[k, rh, 1, u]
                power = power + (p_re * p_re + p_im * p_im)
            most = power if most is None else jnp.maximum(most, power)
    return jnp.max(most) + 1e-6


def swap_halves(first, second):
    lane = lax.broadcasted_iota(jnp.int32, first.shape, 1)
    low = lane < TILE
    return (
        jnp.where(low, first, pltpu.roll(second, TILE, 1)),
        jnp.where(low, pltpu.roll(first, TILE, 1), second),
    )


def slot_of(info, perm, r, c):
    row, col = info[0] + r, info[1] + c
    return perm[(row % 8) * 4 + col % 4] * 3 + c // 4


def chunk_of(info, r, h, block):
    return ((info[0] + r) % 4) * 8 + h * 4 + block


def first_kernel(info, perm, tiles, probe, amp, right, left, strip, send, pgrad, peak, far, sgrad, weight):
    for r in range(4):
        for g in range(GROUPS):
            a, b = slot_of(info, perm, r, 2 * g), slot_of(info, perm, r, 2 * g + 1)
            for c in range(2):
                one = tiles[a, pl.ds(c, 32, stride=2), :]
                two = tiles[b, pl.ds(c, 32, stride=2), :]
                top, low = swap_halves(one, two)
                strip[c, g, 64 * r : 64 * r + 32, :] = top
                strip[c, g, 64 * r + 32 : 64 * r + 64, :] = low
    gradients(strip, probe, amp, right, left, far, sgrad, pgrad, weight)
    peak[0, 0] = peak_of(probe)
    for r in range(4):
        for h in range(2):
            for block in range(4):
                at = chunk_of(info, r, h, block)
                start = 64 * r + 32 * h + 8 * block
                for c in range(2):
                    for g in range(GROUPS):
                        line = (c * GROUPS + g) * 8
                        send[at, line : line + 8, :] = sgrad[c, g, start : start + 8, :]


def second_kernel(
    info, perm, peak, old_strip, first_send, total, other, old_probe, amp, right, left,
    out_tiles, pgrad, strip, probe, far, sgrad, weight
):
    inverse = 1.0 / peak[0, 0]
    for r in range(4):
        for h in range(2):
            for block in range(4):
                at = chunk_of(info, r, h, block)
                start = 64 * r + 32 * h + 8 * block
                for c in range(2):
                    for g in range(GROUPS):
                        line = (c * GROUPS + g) * 8
                        strip[c, g, start : start + 8, :] = (
                            old_strip[c, g, start : start + 8, :] - total[at, line : line + 8, :] * inverse
                        )
    mine = info[2]
    for k in range(MODES):
        for c in range(2):
            for u in range(2):
                for part in range(2):
                    piece = ((k * 2 + c) * 2 + u) * 2 + part
                    rows = slice(part * 64, part * 64 + 64)
                    probe[k, mine, c, u, rows, :] = (
                        old_probe[k, mine, c, u, rows, :] - total[piece, OBJ_ROWS:, :] * PROBE_STEP
                    )
                    probe[k, 1 - mine, c, u, rows, :] = (
                        old_probe[k, 1 - mine, c, u, rows, :] - other[piece] * PROBE_STEP
                    )
    gradients(strip, probe, amp, right, left, far, sgrad, pgrad, weight)
    inverse_now = 1.0 / peak_of(probe)
    for r in range(4):
        for g in range(GROUPS):
            a, b = slot_of(info, perm, r, 2 * g), slot_of(info, perm, r, 2 * g + 1)
            for c in range(2):
                lines = []
                for h in range(2):
                    start = 64 * r + 32 * h
                    line = (c * GROUPS + g) * 8
                    before = jnp.concatenate(
                        [first_send[chunk_of(info, r, h, block), line : line + 8, :] for block in range(4)], axis=0
                    )
                    lines.append(sgrad[c, g, start : start + 32, :] * inverse_now + before * inverse)
                one, two = swap_halves(lines[0], lines[1])
                out_tiles[a, pl.ds(c, 32, stride=2), :] = one
                out_tiles[b, pl.ds(c, 32, stride=2), :] = two


def served_slot(spots, mine, t, k):
    row, col = spots[t, 0], spots[t, 1]
    cls = mine[0]
    r = (cls // 4 - row + BAND_ROWS) % 8
    c = (cls % 4 - col + TILE) % 4 + 4 * k
    valid = jnp.logical_and(r < 4, c < 2 * GROUPS)
    slot = ((row + r) // 8) * 16 + (col + c) // 4
    return valid, jnp.where(valid, slot, 0)


def pack_kernel(spots, mine, tiles, out):
    def one(t, carry):
        for k in range(3):
            valid, slot = served_slot(spots, mine, t, k)
            out[t * 3 + k] = tiles[slot]
        return carry

    lax.fori_loop(0, N_SCAN, one, 0)


def unpack_kernel(spots, mine, tiles, arrived, out):
    out[...] = tiles[...]

    def one(t, carry):
        for k in range(3):
            valid, slot = served_slot(spots, mine, t, k)

            @pl.when(valid)
            def _():
                out[slot] -= arrived[t * 3 + k]

        return carry

    lax.fori_loop(0, N_SCAN, one, 0)


def owner_kernel(spots, me, arrived, out, band):
    band[...] = jnp.zeros_like(band)
    rho = me[0] // 8

    def place(t):
        row = spots[t, 0]
        r = row + (rho - row + BAND_ROWS) % 4
        return r // 4, spots[t, 1] // 2

    def add(t, carry):
        tr, lg = place(t)
        for c in range(2):
            for g in range(GROUPS):
                line = (c * GROUPS + g) * 8
                band[tr, c, lg + g] += arrived[t, line : line + 8, :]
        return carry

    def give(t, carry):
        tr, lg = place(t)
        for c in range(2):
            for g in range(GROUPS):
                line = (c * GROUPS + g) * 8
                out[t, line : line + 8, :] = band[tr, c, lg + g]
        return carry

    lax.fori_loop(0, N_SCAN, add, 0)
    lax.fori_loop(0, N_SCAN, give, 0)


def amplitude_kernel(amp, shuffle, out, moved):
    for p in range(PATS):
        x = amp[p]
        first = x.astype(BF16)
        rest = x - first.astype(F32)
        second = rest.astype(BF16)
        third = (rest - second.astype(F32)).astype(BF16)
        total = None
        for piece in (third, second, first):
            part = jnp.dot(piece, shuffle[...], preferred_element_type=F32)
            total = part if total is None else total + part
        for half in range(2):
            moved[half] = total[:, half * HALF : (half + 1) * HALF]
            for eo in range(2):
                out[p, eo, :, half * HALF : (half + 1) * HALF] = moved[half, pl.ds(eo, HALF, stride=2), :]


SMEM = pl.BlockSpec(memory_space=pltpu.SMEM)
VMEM = pl.BlockSpec(memory_space=pltpu.VMEM)


def kernel(body, outs, ins, scratch=(), out_specs=None, name=None):
    return pl.pallas_call(
        body,
        out_shape=outs,
        in_specs=ins,
        out_specs=out_specs if out_specs is not None else jax.tree.map(lambda _: VMEM, outs),
        scratch_shapes=list(scratch),
        compiler_params=pltpu.CompilerParams(vmem_limit_bytes=52 * 1024 * 1024),
        name=name,
    )


def shaped(*shape, dtype=F32):
    return jax.ShapeDtypeStruct(shape, dtype)


def shift(n, k):
    return [(i, (i + k) % n) for i in range(n)]


def shift_y(k):
    return [(i, (i & ~6) | ((((i >> 1) & 3) + k) % 4) << 1) for i in range(N_SCAN)]


def shift_z(k):
    return [(i, (i + 8 * k) % N_SCAN) for i in range(N_SCAN)]


SWAP = [(i, i ^ 1) for i in range(N_SCAN)]


def exchange(x):
    return lax.all_to_all(x, "scan", split_axis=0, concat_axis=0, tiled=True)


def scatter_sum(x, at, axis, perm_of):
    own = lax.dynamic_index_in_dim(x, at, 0, keepdims=False)
    for k in (1, 3, 2):
        row = lax.dynamic_index_in_dim(x, (at + k) % 4, 0, keepdims=False)
        own = own + lax.ppermute(row, axis, perm_of(k))
    return own


def gather_rows(x, at, axis, perm_of):
    stacked = jnp.zeros((4,) + x.shape, x.dtype)
    stacked = lax.dynamic_update_index_in_dim(stacked, x, at, 0)
    for k in (1, 3, 2):
        got = lax.ppermute(x, axis, perm_of(k))
        stacked = lax.dynamic_update_index_in_dim(stacked, got, (at - k) % 4, 0)
    return stacked


def body(amplitude, positions, owner_perm, object_tiles, probe):
    band = lax.axis_index("grp")
    me = lax.axis_index("scan")
    core, y_at, z_at = me % 2, me // 2 % 4, me // 8
    right_np, left_np = dft_tables()
    right, left = jnp.asarray(right_np), jnp.asarray(left_np)
    shuffle_np = np.zeros((SIDE, SIDE), np.float32)
    for m in range(SIDE):
        shuffle_np[m, m // 2 + HALF * (m % 2)] = 1.0
    shuffle = jnp.asarray(shuffle_np.astype(ml_dtypes.bfloat16))

    spot = positions[0] // TILE - jnp.array([BAND_ROWS, 0], jnp.int32) * band
    spots = exchange(jnp.broadcast_to(spot[None, None], (N_SCAN, 1, 2))).reshape(N_SCAN, 2)
    perm = lax.dynamic_index_in_dim(owner_perm, band, 0, keepdims=False)
    cls = jnp.sum(jnp.where(perm == me, jnp.arange(N_SCAN, dtype=jnp.int32), 0)).reshape(1)
    info = jnp.concatenate([spot, core.reshape(1).astype(jnp.int32)])
    place = me.reshape(1).astype(jnp.int32)

    tiles = object_tiles.reshape(TILE, 2, 32, HALF).transpose(0, 2, 1, 3).reshape(TILE, TILE, HALF)
    packed = kernel(pack_kernel, shaped(96, TILE, HALF), [SMEM, SMEM, VMEM], name="pack")(spots, cls, tiles)
    arrived = exchange(packed)

    own = probe.reshape(1, 2, 2, 2, 32, 2, 2, HALF).transpose(0, 2, 1, 6, 3, 5, 4, 7).reshape(1, 2, 2, 2, HALF, HALF)
    modes = lax.all_gather(own, "grp", axis=0, tiled=True)
    amp = kernel(amplitude_kernel, shaped(PATS, 2, HALF, SIDE), [VMEM, VMEM], [pltpu.VMEM((2, SIDE, HALF), F32)], name="spread")(amplitude, shuffle)

    scratch = [
        pltpu.VMEM((MODES, 2, SIDE, SIDE), F32),
        pltpu.VMEM((2, GROUPS, SIDE, HALF), F32),
        pltpu.VMEM((2, 2, HALF, HALF), F32),
    ]
    strip, send, pgrad, peak = kernel(
        first_kernel,
        (
            shaped(2, GROUPS, SIDE, HALF),
            shaped(N_SCAN, OBJ_ROWS, HALF),
            shaped(2, MODES, 2, 2, HALF, HALF),
            shaped(1, 1),
        ),
        [SMEM, SMEM] + [VMEM] * 5,
        scratch,
        out_specs=(VMEM, VMEM, VMEM, SMEM),
        name="first",
    )(info, perm, arrived, modes, amp, right, left)

    def chip_sum(x):
        kept = lax.dynamic_index_in_dim(x, core, 0, keepdims=False)
        given = lax.dynamic_index_in_dim(x, 1 - core, 0, keepdims=False)
        return kept + lax.ppermute(given, "scan", SWAP)

    chip = chip_sum(pgrad).reshape(N_SCAN, PRB_ROWS, HALF)
    got = exchange(jnp.concatenate([send, chip], axis=1))
    both = jnp.sum(got[:, OBJ_ROWS:].reshape(16, 2, PRB_ROWS, HALF), axis=0)
    summed = both
    for k in (1, 3, 2):
        summed = summed + lax.ppermute(both, "grp", shift(N_GRP, k))
    totals = kernel(
        owner_kernel,
        shaped(N_SCAN, OBJ_ROWS, HALF),
        [SMEM, SMEM, VMEM],
        [pltpu.VMEM((8, 2, 32, 8, HALF), F32)],
        name="owner",
    )(spots, place, got)
    answer = jnp.broadcast_to(summed[None], (16, 2, PRB_ROWS, HALF)).reshape(N_SCAN, PRB_ROWS, HALF)
    total = exchange(jnp.concatenate([totals, answer], axis=1))
    other = lax.ppermute(total[:, OBJ_ROWS:], "scan", SWAP)

    moved, pgrad = kernel(
        second_kernel,
        (shaped(96, TILE, HALF), shaped(2, MODES, 2, 2, HALF, HALF)),
        [SMEM, SMEM, SMEM] + [VMEM] * 8,
        [
            pltpu.VMEM((2, GROUPS, SIDE, HALF), F32),
            pltpu.VMEM((MODES, 2, 2, 2, HALF, HALF), F32),
        ]
        + scratch,
        name="second",
    )(info, perm, peak, strip, send, total, other, modes, amp, right, left)
    returned = exchange(moved)

    chip = chip_sum(pgrad)
    mine = scatter_sum(chip, band, "grp", lambda k: shift(N_GRP, k))
    mine = mine.reshape(4, 4, 32, HALF)
    mine = scatter_sum(mine, y_at, "scan", shift_y)
    mine = scatter_sum(mine, z_at, "scan", shift_z)
    mine = gather_rows(mine, z_at, "scan", shift_z)
    mine = gather_rows(mine, y_at, "scan", shift_y).reshape(2, 2, HALF, HALF)
    theirs = lax.ppermute(mine, "scan", SWAP)
    second_sum = jnp.where(core == 0, jnp.stack([mine, theirs]), jnp.stack([theirs, mine]))

    half_one = total[:, OBJ_ROWS:].reshape(MODES, 2, 2, HALF, HALF)
    half_one = lax.dynamic_index_in_dim(half_one, band, 0, keepdims=False)
    half_two = lax.dynamic_index_in_dim(other.reshape(MODES, 2, 2, HALF, HALF), band, 0, keepdims=False)
    first_sum = jnp.where(core == 0, jnp.stack([half_one, half_two]), jnp.stack([half_two, half_one]))
    probe_new = own[0] - first_sum * PROBE_STEP - second_sum * PROBE_STEP
    probe_out = (
        probe_new.reshape(2, 2, 2, 2, 2, 32, HALF).transpose(1, 0, 3, 5, 4, 2, 6).reshape(1, 2, SIDE, SIDE)
    )

    object_new = kernel(unpack_kernel, shaped(TILE, TILE, HALF), [SMEM, SMEM, VMEM, VMEM], name="unpack")(
        spots, cls, tiles, returned
    )
    object_out = object_new.reshape(TILE, 32, 2, HALF).transpose(0, 2, 1, 3).reshape(TILE, 2, TILE * TILE)
    return object_out, probe_out


def solution(mesh):
    in_specs = (
        P(("grp", "scan"), None, None),
        P(("grp", "scan"), None),
        P(),
        P(("grp", "scan"), None, None),
        P("grp", None, None, None),
    )
    out_specs = (P(("grp", "scan"), None, None), P("grp", None, None, None))
    return jax.shard_map(body, mesh=mesh, in_specs=in_specs, out_specs=out_specs, check_vma=False)
```

time: 817 us -> 328 us (0.40)
  matrix products: 286 us -> 0 us
  waiting for transfers between devices: 324 us -> 97.3 us
  local copies, waits for them, and re-layouts: 92.5 us -> 11.5 us
  Pallas kernels: 0 us -> 76.7 us
  blocking collectives: 16.3 us -> 71.2 us
  other arithmetic: 42.6 us -> 7.05 us
  starting transfers between devices: 27.9 us -> 48.6 us
    dot_general x34 -> x0, matrix products: 286 us -> none  [the longest x32 273 us: product(): return jnp.einsum(spec, first, second, precision=lax.Precision.HIGHEST)]
    psum x2 -> x0, waiting for transfers between devices: 198 us -> none  [body(): owned_sum = lax.psum(owned_sum, 'scan')]
    pallas_call x0 -> x6, Pallas kernels: none -> 76.7 us  [the longest x1 30.2 us: body(): kernel(second_kernel, (shaped(96, TILE, HALF), shaped(2, MODES, 2, 2, HAL...]
    all_to_all x4 -> x3, waiting for transfers between devices: 111 us -> 40.6 us  [exchange(): return lax.all_to_all(x, 'scan', split_axis=0, concat_axis=0, tiled=True)]
    ppermute x0 -> x22, waiting for transfers between devices: none -> 56.6 us  [the longest x9 40.1 us: scatter_sum(): own = own + lax.ppermute(row, axis, perm_of(k))]
    all_to_all x1 -> x2, blocking collectives: 16.3 us -> 71.2 us  [exchange(): return lax.all_to_all(x, 'scan', split_axis=0, concat_axis=0, tiled=True)]
    gather x6 -> x0, local copies, waits for them, and re-layouts: 40 us -> none  [the longest x2 17.4 us: body(): jnp.take(current, served, axis=0).reshape(n_scan, capacity, 2, tile_area)]
    select_n x8 -> x0, other arithmetic: 28.7 us -> none  [the longest x2 13.1 us: body(): jnp.take(padded, source, axis=0).reshape(n_scan, capacity, 2, tile_area)]
  transfers between devices with their start and end apart: 10 -> 26, of which waited for: 6 -> 16; matrix products, arithmetic and copies ran while one was open for 12% -> 2% of each run, Pallas kernels for 0% -> 3%
where the time goes in v1:
time: 328 us; the launch traced here: 327 us
  waiting for transfers between devices  97.3 us (30%)
  Pallas kernels  76.7 us (23%)
  blocking collectives  71.2 us (22%)
  starting transfers between devices  48.6 us (15%)
  between operations  14.5 us (4%)
  local copies, waits for them, and re-layouts  11.5 us (4%)
  other arithmetic  7.05 us (2%)
    all_to_all x2, blocking collectives, exchange(): return lax.all_to_all(x, 'scan', split_axis=0, concat_axis=0, tiled=True)  71.2 us
    all_to_all x3, waiting for transfers between devices, exchange(): return lax.all_to_all(x, 'scan', split_axis=0, concat_axis=0, tiled=True)  40.6 us
    ppermute x9, waiting for transfers between devices, scatter_sum(): own = own + lax.ppermute(row, axis, perm_of(k))  40.1 us
    pallas_call x1, Pallas kernels, body(): kernel(second_kernel, (shaped(96, TILE, HALF), shaped(2, MODES, 2, 2, HAL...  30.2 us
    pallas_call x1, Pallas kernels, body(): kernel(first_kernel, (shaped(2, GROUPS, SIDE, HALF), shaped(N_SCAN, OBJ_R...  27.8 us
    all_to_all x3, starting transfers between devices, exchange(): return lax.all_to_all(x, 'scan', split_axis=0, concat_axis=0, tiled=True)  19.9 us
    ppermute x9, starting transfers between devices, scatter_sum(): own = own + lax.ppermute(row, axis, perm_of(k))  10.2 us
    ppermute x6, waiting for transfers between devices, gather_rows(): got = lax.ppermute(x, axis, perm_of(k))  8.35 us
  transfers between devices with their start and end apart: 26, of which 16 were waited for; matrix products, arithmetic and copies ran while one was open for 2% of the time, Pallas kernels for 3%

profile of v1, /device:TPU:1, one launch (start us, length us, event | category | flops | bytes accessed | tf_op | source)
XLA Modules:
  0.0 326.9 jit_solution(5958967353149663292)
XLA Ops:
  7.2 0.8 slice_reduce_fusion
  8.0 0.7 multiply_subtract_fusion
  8.6 0.6 broadcast_in_dim.48
  9.2 9.6 %all-to-all-start = ((s32[32,1,2]{2,1,0:T(1,128)}), s32[32,1,2]{2,1,0:T(1,128)S(1)}, u32[]{:S(2)}, u32[]{:S(2)}) async-start(s32[32,1,2]{2,1,0:T(1,128)} %broadcast_in_dim.48), calls=%async_computation | async-start | bytes 32768 | tf_op jit(solution)/shard_map/all_to_all | solution.py:386
  18.9 1.3 reshape.81
  20.2 0.9 copy.21
  21.1 1.3 fusion.11
  22.4 3.3 %all-to-all-done = s32[32,1,2]{2,1,0:T(1,128)S(1)} async-done(((s32[32,1,2]{2,1,0:T(1,128)}), s32[32,1,2]{2,1,0:T(1,128)S(1)}, u32[]{:S(2)}, u32[]{:S(2)}) %all-to-all-start) | async-done | bytes 288 | tf_op jit(solution)/shard_map/all_to_all | solution.py:386
  25.7 6.0 %pack.1 = f32[96,64,128]{2,1,0:T(8,128)} custom-call(s32[32,2]{1,0:T(8,128)S(1)} %bitcast.100, s32[1]{0:T(128)} %bitcast.2.mine, f32[64,64,128]{2,1,0:T(8,128)} %bitcast.103), custom_call_target="tpu_custom_call" | custom-call | tf_op jit(solution)/shard_map/pack/pallas_call | solution.py:425
  31.7 5.2 %all-to-all-start.1 = ((f32[96,64,128]{2,1,0:T(8,128)}), f32[96,64,128]{2,1,0:T(8,128)}, u32[]{:S(2)}, u32[]{:S(2)}) async-start(f32[96,64,128]{2,1,0:T(8,128)} %pack.1), calls=%async_computation.1 | async-start | bytes 6291456 | tf_op jit(solution)/shard_map/all_to_all | solution.py:386
  37.0 1.9 spread.1.amp
  39.0 37.3 %all-to-all-done.1.tiles = f32[96,64,128]{2,1,0:T(8,128)} async-done(((f32[96,64,128]{2,1,0:T(8,128)}), f32[96,64,128]{2,1,0:T(8,128)}, u32[]{:S(2)}, u32[]{:S(2)}) %all-to-all-start.1) | async-done | bytes 3145760 | tf_op jit(solution)/shard_map/all_to_all | solution.py:386
  76.3 27.8 %first.1 = (f32[2,5,256,128]{3,2,1,0:T(8,128)}, f32[32,80,128]{2,1,0:T(8,128)}, f32[2,4,2,2,128,128]{5,4,3,2,1,0:T(8,128)}, f32[1,1]{1,0:T(1,128)}) custom-call(s32[3]{0:T(128)S(1)} %pad_add_fusion.info, s32[32]{0:T(128)S(1)} %get-tuple-element.17.perm, f32[96,64,128]{2,1,0:T(8,128)} %all-to-all-done.1.tiles, ...), custom_call_target="tpu_custom_call" | custom-call | tf_op jit(solution)/shard_map/first/pallas_call | solution.py:437
  104.1 1.3 dynamic-slice_bitcast_fusion.1
  105.4 3.0 collective-permute-start
  108.4 2.4 collective-permute-done
  110.8 1.7 bitcast_add_fusion.1
  112.5 0.2 pad_maximum_fusion
  112.6 34.6 %all_to_all.25.arrived = f32[32,144,128]{2,1,0:T(8,128)S(1)} all-to-all(f32[32,144,128]{2,1,0:T(8,128)S(1)} %pad_maximum_fusion), channel_id=1, replica_groups=mesh['grp'=4,'scan'=32] {'scan'}, dimensions={0} | all-to-all | bytes 4718592 | tf_op jit(solution)/shard_map/all_to_all | solution.py:386
  147.2 1.4 copy-done.3
  148.9 2.8 collective-permute-start.3
  151.7 0.9 collective-permute-start.2
  152.5 0.6 collective-permute-start.1
  153.1 3.2 owner.1
  156.4 0.5 collective-permute-done.1
  157.0 0.2 pad_maximum_fusion.1
  157.2 36.6 %all_to_all.26.total = f32[32,144,128]{2,1,0:T(8,128)S(1)} all-to-all(f32[32,144,128]{2,1,0:T(8,128)S(1)} %pad_maximum_fusion.1), channel_id=1, replica_groups=mesh['grp'=4,'scan'=32] {'scan'}, dimensions={0} | all-to-all | bytes 4718592 | tf_op jit(solution)/shard_map/all_to_all | solution.py:386
  193.8 0.1 slice.14
  194.0 0.4 collective-permute-start.4
  194.4 2.5 collective-permute-done.4.other
  196.9 30.2 %second.1 = (f32[96,64,128]{2,1,0:T(8,128)}, f32[2,4,2,2,128,128]{5,4,3,2,1,0:T(8,128)}) custom-call(s32[3]{0:T(128)S(1)} %pad_add_fusion.info, s32[32]{0:T(128)S(1)} %get-tuple-element.17.perm, f32[1,1]{1,0:T(1,128)} %get-tuple-element.8.peak, f32[2,5,256,128]{3,2,1,0:T(8,128)} %get-tuple-element.9.old_strip, f32[32,80,128]{2,1,0:T(8,128)} %get-tuple-element.10.first_send, ...), custom_call_target="tpu_custom_call" | custom-call | tf_op jit(solution)/shard_map/second/pallas_call | solution.py:473
  227.0 1.3 dynamic-slice_bitcast_fusion
  228.3 0.2 collective-permute-start.5
  228.6 2.6 collective-permute-done.5
  231.2 1.7 bitcast_add_fusion
  232.9 0.8 dynamic-slice_bitcast_fusion.4
  233.7 1.9 collective-permute-start.8
  235.6 0.8 collective-permute-start.7
  236.3 5.1 %all-to-all-start.4 = ((f32[96,64,128]{2,1,0:T(8,128)}), f32[96,64,128]{2,1,0:T(8,128)}, u32[]{:S(2)}, u32[]{:S(2)}) async-start(f32[96,64,128]{2,1,0:T(8,128)} %get-tuple-element.12), calls=%async_computation.4 | async-start | bytes 6291456 | tf_op jit(solution)/shard_map/all_to_all | solution.py:386
  241.5 7.1 %collective-permute-done.6 = f32[2,2,128,128]{3,2,1,0:T(8,128)S(1)} collective-permute-done((f32[2,2,128,128]{3,2,1,0:T(8,128)}, f32[2,2,128,128]{3,2,1,0:T(8,128)S(1)}, u32[]{:S(2)}, u32[]{:S(2)}) %collective-permute-start.6) | collective-permute-done | bytes 262176 | tf_op jit(solution)/shard_map/ppermute | solution.py:393
  248.6 1.1 fusion.6
  249.8 0.5 collective-permute-start.9
  250.2 1.9 collective-permute-start.11
  252.1 0.6 collective-permute-start.10
  252.7 27.5 %collective-permute-done.9 = f32[4,32,128]{2,1,0:T(8,128)S(1)} collective-permute-done((f32[4,32,128]{2,1,0:T(8,128)S(1)}, f32[4,32,128]{2,1,0:T(8,128)S(1)}, u32[]{:S(2)}, u32[]{:S(2)}) %collective-permute-start.9) | collective-permute-done | bytes 65568 | tf_op jit(solution)/shard_map/ppermute | solution.py:393
  280.2 2.9 collective-permute-done.11
  283.1 2.1 collective-permute-start.12
  285.2 2.2 collective-permute-start.14
  287.4 0.3 collective-permute-start.13
  287.7 1.6 collective-permute-done.14
  289.3 1.0 collective-permute-done.13
  290.5 2.5 collective-permute-start.16
  293.1 1.1 collective-permute-done.15
  294.2 3.0 collective-permute-done.17
  297.1 0.2 collective-permute-start.20
  297.3 2.1 collective-permute-start.19
  299.5 4.3 %collective-permute-done.18 = f32[4,32,128]{2,1,0:T(8,128)S(1)} collective-permute-done((f32[4,32,128]{2,1,0:T(8,128)S(1)}, f32[4,32,128]{2,1,0:T(8,128)S(1)}, u32[]{:S(2)}, u32[]{:S(2)}) %collective-permute-start.18) | collective-permute-done | bytes 65568 | tf_op jit(solution)/shard_map/ppermute | solution.py:401
  303.8 5.6 %collective-permute-start.21 = (f32[2,2,128,128]{3,2,1,0:T(8,128)S(1)}, f32[2,2,128,128]{3,2,1,0:T(8,128)S(1)}, u32[]{:S(2)}, u32[]{:S(2)}) collective-permute-start(f32[2,2,128,128]{3,2,1,0:T(8,128)S(1)} %bitcast.115), channel_id=1, source_target_pairs={{0,1},{1,0},{2,3},{3,2},{4,5},{5,4},{6,7},{7,6},{8,9},{9,8},{10,11... | collective-permute-start | bytes 786440 | tf_op jit(solution)/shard_map/ppermute | solution.py:493
  309.4 1.0 constant_dynamic-slice_fusion.1
  310.4 0.2 collective-permute-done.21
  310.6 0.2 fusion.3
  310.8 0.4 copy.25
  311.2 1.2 reshape.93
  312.4 7.6 %unpack.1 = f32[64,64,128]{2,1,0:T(8,128)} custom-call(s32[32,2]{1,0:T(8,128)S(1)} %bitcast.102, s32[1]{0:T(128)} %bitcast.2.mine, f32[64,64,128]{2,1,0:T(8,128)} %bitcast.104, f32[96,64,128]{2,1,0:T(8,128)} %all-to-all-done.4.arrived), custom_call_target="tpu_custom_call" | custom-call | tf_op jit(solution)/shard_map/unpack/pallas_call | solution.py:505
  (47 shorter events, 0.8 us)
Async XLA Ops:
  9.2 16.5 %all-to-all-start = ((s32[32,1,2]{2,1,0:T(1,128)}), s32[32,1,2]{2,1,0:T(1,128)S(1)}, u32[]{:S(2)}, u32[]{:S(2)}) async-start(s32[32,1,2]{2,1,0:T(1,128)} %broadcast_in_dim.48), calls=%async_computation | async-start | bytes 32768 | tf_op jit(solution)/shard_map/all_to_all | solution.py:386
  18.9 57.4 %all-gather.2.cloned.1.call-start = ((), (), s32[]{:S(2)}) async-start(), calls=%async_computation.5 | async-start | bytes 2621440 | tf_op jit(solution)/shard_map/all_gather | solution.py:429
  31.7 5.2 %copy-start.1 = (bf16[256,256]{1,0:T(8,128)(2,1)S(1)}, bf16[256,256]{1,0:T(8,128)(2,1)}, u32[]{:S(2)}) copy-start(bf16[256,256]{1,0:T(8,128)(2,1)} %constant.222.clone.shuffle) | copy-start | bytes 393220
  31.7 44.5 %all-to-all-start.1 = ((f32[96,64,128]{2,1,0:T(8,128)}), f32[96,64,128]{2,1,0:T(8,128)}, u32[]{:S(2)}, u32[]{:S(2)}) async-start(f32[96,64,128]{2,1,0:T(8,128)} %pack.1), calls=%async_computation.1 | async-start | bytes 6291456 | tf_op jit(solution)/shard_map/all_to_all | solution.py:386
  38.9 65.2 %copy-start = (f32[4,2,128,256]{3,2,1,0:T(8,128)}, f32[4,2,128,256]{3,2,1,0:T(8,128)S(1)}, u32[]{:S(2)}) copy-start(f32[4,2,128,256]{3,2,1,0:T(8,128)S(1)} %spread.1.amp) | copy-start | bytes 3145732
  105.4 7.1 %copy-start.4 = (f32[32,80,128]{2,1,0:T(8,128)S(1)}, f32[32,80,128]{2,1,0:T(8,128)}, u32[]{:S(2)}) copy-start(f32[32,80,128]{2,1,0:T(8,128)} %get-tuple-element.10.first_send) | copy-start | bytes 3932164
  105.4 5.4 %collective-permute-start = (f32[4,2,2,128,128]{4,3,2,1,0:T(8,128)S(1)}, f32[4,2,2,128,128]{4,3,2,1,0:T(8,128)}, u32[]{:S(2)}, u32[]{:S(2)}) collective-permute-start(f32[4,2,2,128,128]{4,3,2,1,0:T(8,128)S(1)} %dynamic-slice_bitcast_fusion.1), channel_id=1, source_target_pairs={{0,1},{1,0},{2,3},{3,2},{4,5},{5,4},{6,7},{7,6},{8,9},{9,8},{10,11... | collective-permute-start | bytes 3145736 | tf_op jit(solution)/shard_map/ppermute | solution.py:454
  147.2 1.4 copy-start.3
  148.9 7.5 %collective-permute-start.3 = (f32[2,64,128]{2,1,0:T(8,128)S(1)}, f32[2,64,128]{2,1,0:T(8,128)S(1)}, u32[]{:S(2)}, u32[]{:S(2)}) collective-permute-start(f32[2,64,128]{2,1,0:T(8,128)S(1)} %reduce_sum.19), channel_id=1, source_target_pairs={{0,64},{32,96},{64,0},{96,32},{1,65},{33,97},{65,1},{97,33},{2,66}... | collective-permute-start | bytes 196616 | tf_op jit(solution)/shard_map/ppermute | solution.py:461
  151.7 4.7 %collective-permute-start.2 = (f32[2,64,128]{2,1,0:T(8,128)S(1)}, f32[2,64,128]{2,1,0:T(8,128)S(1)}, u32[]{:S(2)}, u32[]{:S(2)}) collective-permute-start(f32[2,64,128]{2,1,0:T(8,128)S(1)} %reduce_sum.19), channel_id=1, source_target_pairs={{0,96},{32,0},{64,32},{96,64},{1,97},{33,1},{65,33},{97,65},{2,98}... | collective-permute-start | bytes 196616 | tf_op jit(solution)/shard_map/ppermute | solution.py:461
  152.5 4.3 %collective-permute-start.1 = (f32[2,64,128]{2,1,0:T(8,128)S(1)}, f32[2,64,128]{2,1,0:T(8,128)S(1)}, u32[]{:S(2)}, u32[]{:S(2)}) collective-permute-start(f32[2,64,128]{2,1,0:T(8,128)S(1)} %reduce_sum.19), channel_id=1, source_target_pairs={{0,32},{32,64},{64,96},{96,0},{1,33},{33,65},{65,97},{97,1},{2,34}... | collective-permute-start | bytes 196616 | tf_op jit(solution)/shard_map/ppermute | solution.py:461
  193.8 3.1 copy-start.2
  194.0 2.9 copy-start.5
  194.0 2.9 collective-permute-start.4
  228.3 2.9 collective-permute-start.5
  233.6 14.9 %collective-permute-start.6 = (f32[2,2,128,128]{3,2,1,0:T(8,128)}, f32[2,2,128,128]{3,2,1,0:T(8,128)S(1)}, u32[]{:S(2)}, u32[]{:S(2)}) collective-permute-start(f32[2,2,128,128]{3,2,1,0:T(8,128)} %get-tuple-element.18), channel_id=1, source_target_pairs={{0,32},{32,64},{64,96},{96,0},{1,33},{33,65},{65,97},{97,1},{2,34}... | collective-permute-start | bytes 786440 | tf_op jit(solution)/shard_map/ppermute | solution.py:393
  233.7 14.9 %collective-permute-start.8 = (f32[2,2,128,128]{3,2,1,0:T(8,128)S(1)}, f32[2,2,128,128]{3,2,1,0:T(8,128)}, u32[]{:S(2)}, u32[]{:S(2)}) collective-permute-start(f32[2,2,128,128]{3,2,1,0:T(8,128)S(1)} %get-tuple-element.19), channel_id=1, source_target_pairs={{0,64},{32,96},{64,0},{96,32},{1,65},{33,97},{65,1},{97,33},{2,66}... | collective-permute-start | bytes 786440 | tf_op jit(solution)/shard_map/ppermute | solution.py:393
  235.6 13.1 %collective-permute-start.7 = (f32[2,2,128,128]{3,2,1,0:T(8,128)S(1)}, f32[2,2,128,128]{3,2,1,0:T(8,128)}, u32[]{:S(2)}, u32[]{:S(2)}) collective-permute-start(f32[2,2,128,128]{3,2,1,0:T(8,128)S(1)} %get-tuple-element.20), channel_id=1, source_target_pairs={{0,96},{32,0},{64,32},{96,64},{1,97},{33,1},{65,33},{97,65},{2,98}... | collective-permute-start | bytes 786440 | tf_op jit(solution)/shard_map/ppermute | solution.py:393
  236.3 76.1 %all-to-all-start.4 = ((f32[96,64,128]{2,1,0:T(8,128)}), f32[96,64,128]{2,1,0:T(8,128)}, u32[]{:S(2)}, u32[]{:S(2)}) async-start(f32[96,64,128]{2,1,0:T(8,128)} %get-tuple-element.12), calls=%async_computation.4 | async-start | bytes 6291456 | tf_op jit(solution)/shard_map/all_to_all | solution.py:386
  249.8 30.4 %collective-permute-start.9 = (f32[4,32,128]{2,1,0:T(8,128)S(1)}, f32[4,32,128]{2,1,0:T(8,128)S(1)}, u32[]{:S(2)}, u32[]{:S(2)}) collective-permute-start(f32[4,32,128]{2,1,0:T(8,128)S(1)} %get-tuple-element.21), channel_id=1, source_target_pairs={{0,2},{1,3},{2,4},{3,5},{4,6},{5,7},{6,0},{7,1},{8,10},{9,11},{10,... | collective-permute-start | bytes 196616 | tf_op jit(solution)/shard_map/ppermute | solution.py:393
  250.2 32.8 %collective-permute-start.11 = (f32[4,32,128]{2,1,0:T(8,128)S(1)}, f32[4,32,128]{2,1,0:T(8,128)S(1)}, u32[]{:S(2)}, u32[]{:S(2)}) collective-permute-start(f32[4,32,128]{2,1,0:T(8,128)S(1)} %get-tuple-element.22), channel_id=1, source_target_pairs={{0,4},{1,5},{2,6},{3,7},{4,0},{5,1},{6,2},{7,3},{8,12},{9,13},{10,... | collective-permute-start | bytes 196616 | tf_op jit(solution)/shard_map/ppermute | solution.py:393
  252.1 31.0 %collective-permute-start.10 = (f32[4,32,128]{2,1,0:T(8,128)S(1)}, f32[4,32,128]{2,1,0:T(8,128)S(1)}, u32[]{:S(2)}, u32[]{:S(2)}) collective-permute-start(f32[4,32,128]{2,1,0:T(8,128)S(1)} %get-tuple-element.23), channel_id=1, source_target_pairs={{0,6},{1,7},{2,0},{3,1},{4,2},{5,3},{6,4},{7,5},{8,14},{9,15},{10,... | collective-permute-start | bytes 196616 | tf_op jit(solution)/shard_map/ppermute | solution.py:393
  283.1 4.6 %collective-permute-start.12 = (f32[32,128]{1,0:T(8,128)S(1)}, f32[32,128]{1,0:T(8,128)S(1)}, u32[]{:S(2)}, u32[]{:S(2)}) collective-permute-start(f32[32,128]{1,0:T(8,128)S(1)} %get-tuple-element.24), channel_id=1, source_target_pairs={{0,8},{1,9},{2,10},{3,11},{4,12},{5,13},{6,14},{7,15},{8,16},{9,17... | collective-permute-start | bytes 49160 | tf_op jit(solution)/shard_map/ppermute | solution.py:393
  285.2 4.1 %collective-permute-start.14 = (f32[32,128]{1,0:T(8,128)S(1)}, f32[32,128]{1,0:T(8,128)S(1)}, u32[]{:S(2)}, u32[]{:S(2)}) collective-permute-start(f32[32,128]{1,0:T(8,128)S(1)} %get-tuple-element.25), channel_id=1, source_target_pairs={{0,16},{1,17},{2,18},{3,19},{4,20},{5,21},{6,22},{7,23},{8,24},{9,... | collective-permute-start | bytes 49160 | tf_op jit(solution)/shard_map/ppermute | solution.py:393
  287.4 2.9 collective-permute-start.13
  290.3 3.9 %collective-permute-start.15 = (f32[32,128]{1,0:T(8,128)S(1)}, f32[32,128]{1,0:T(8,128)S(1)}, u32[]{:S(2)}, u32[]{:S(2)}) collective-permute-start(f32[32,128]{1,0:T(8,128)S(1)} %get-tuple-element.15), channel_id=1, source_target_pairs={{0,8},{1,9},{2,10},{3,11},{4,12},{5,13},{6,14},{7,15},{8,16},{9,17... | collective-permute-start | bytes 49160 | tf_op jit(solution)/shard_map/ppermute | solution.py:401
  290.5 3.7 %collective-permute-start.16 = (f32[32,128]{1,0:T(8,128)S(1)}, f32[32,128]{1,0:T(8,128)S(1)}, u32[]{:S(2)}, u32[]{:S(2)}) collective-permute-start(f32[32,128]{1,0:T(8,128)S(1)} %get-tuple-element.15), channel_id=1, source_target_pairs={{0,24},{1,25},{2,26},{3,27},{4,28},{5,29},{6,30},{7,31},{8,0},{9,1... | collective-permute-start | bytes 49160 | tf_op jit(solution)/shard_map/ppermute | solution.py:401
  293.0 4.1 %collective-permute-start.17 = (f32[32,128]{1,0:T(8,128)S(1)}, f32[32,128]{1,0:T(8,128)S(1)}, u32[]{:S(2)}, u32[]{:S(2)}) collective-permute-start(f32[32,128]{1,0:T(8,128)S(1)} %get-tuple-element.15), channel_id=1, source_target_pairs={{0,16},{1,17},{2,18},{3,19},{4,20},{5,21},{6,22},{7,23},{8,24},{9,... | collective-permute-start | bytes 49160 | tf_op jit(solution)/shard_map/ppermute | solution.py:401
  297.1 6.7 %collective-permute-start.20 = (f32[4,32,128]{2,1,0:T(8,128)S(1)}, f32[4,32,128]{2,1,0:T(8,128)S(1)}, u32[]{:S(2)}, u32[]{:S(2)}) collective-permute-start(f32[4,32,128]{2,1,0:T(8,128)S(1)} %bitcast_dynamic-update-slice_fusion.4), channel_id=1, source_target_pairs={{0,4},{1,5},{2,6},{3,7},{4,0},{5,1},{6,2},{7,3},{8,12},{9,13},{10,... | collective-permute-start | bytes 196616 | tf_op jit(solution)/shard_map/ppermute | solution.py:401
  297.3 6.5 %collective-permute-start.19 = (f32[4,32,128]{2,1,0:T(8,128)S(1)}, f32[4,32,128]{2,1,0:T(8,128)S(1)}, u32[]{:S(2)}, u32[]{:S(2)}) collective-permute-start(f32[4,32,128]{2,1,0:T(8,128)S(1)} %bitcast_dynamic-update-slice_fusion.4), channel_id=1, source_target_pairs={{0,6},{1,7},{2,0},{3,1},{4,2},{5,3},{6,4},{7,5},{8,14},{9,15},{10,... | collective-permute-start | bytes 196616 | tf_op jit(solution)/shard_map/ppermute | solution.py:401
  299.4 4.3 %collective-permute-start.18 = (f32[4,32,128]{2,1,0:T(8,128)S(1)}, f32[4,32,128]{2,1,0:T(8,128)S(1)}, u32[]{:S(2)}, u32[]{:S(2)}) collective-permute-start(f32[4,32,128]{2,1,0:T(8,128)S(1)} %bitcast_dynamic-update-slice_fusion.4), channel_id=1, source_target_pairs={{0,2},{1,3},{2,4},{3,5},{4,6},{5,7},{6,0},{7,1},{8,10},{9,11},{10,... | collective-permute-start | bytes 196616 | tf_op jit(solution)/shard_map/ppermute | solution.py:401
  303.8 6.8 %collective-permute-start.21 = (f32[2,2,128,128]{3,2,1,0:T(8,128)S(1)}, f32[2,2,128,128]{3,2,1,0:T(8,128)S(1)}, u32[]{:S(2)}, u32[]{:S(2)}) collective-permute-start(f32[2,2,128,128]{3,2,1,0:T(8,128)S(1)} %bitcast.115), channel_id=1, source_target_pairs={{0,1},{1,0},{2,3},{3,2},{4,5},{5,4},{6,7},{7,6},{8,9},{9,8},{10,11... | collective-permute-start | bytes 786440 | tf_op jit(solution)/shard_map/ppermute | solution.py:493
Sparse Core Ops, SparseCore 0:
  21.9 31.7 all-gather.1

commit v2 on v1

v2 whole, which is shorter than its diff:
```python
import functools
import math

import jax
import jax.numpy as jnp
import ml_dtypes
import numpy as np
from jax import lax
from jax.experimental import pallas as pl
from jax.experimental.pallas import tpu as pltpu
from jax.sharding import PartitionSpec as P

SIDE = 256
HALF = 128
TILE = 64
MODES = 4
PATS = 4
N_SCAN = 32
N_GRP = 4
BAND_ROWS = 32
GROUPS = 5
PROBE_STEP = 0.03125
OBJ_ROWS = 2 * GROUPS * 8
PRB_ROWS = 64
SEND_ROWS = OBJ_ROWS + PRB_ROWS
WEAK = 0.1
F32 = jnp.float32
BF16 = jnp.bfloat16


def row_of_position():
    return np.array([64 * r + 2 * q + h for r in range(2) for h in range(2) for q in range(32)])


def split_table(table):
    high = table.astype(ml_dtypes.bfloat16)
    low = (table - high.astype(np.float64)).astype(ml_dtypes.bfloat16)
    return high, low


def dft_tables():
    j = np.arange(HALF)[None, :]

    def real_form(n, odd):
        angle = 2.0 * math.pi * ((n[:, None] * (2 * j + odd)) % SIDE) / SIDE
        c, s = np.cos(angle) / 16.0, np.sin(angle) / 16.0
        return np.block([[c, -s], [s, c]])

    lanes = np.arange(HALF)
    rows = row_of_position()
    right, left = [], []
    for odd in (0, 1):
        for table in (real_form(lanes, odd), real_form(lanes, odd).T):
            high, low = split_table(table)
            right.append(np.concatenate([high, low], axis=0))
        for table in (real_form(rows, odd).T, real_form(rows, odd)):
            high, low = split_table(table)
            left.append(np.concatenate([high, low], axis=1))
    return np.stack(right), np.stack(left)


def split(x):
    high = x.astype(BF16)
    return high, (x - high.astype(F32)).astype(BF16)


def product(first, second):
    return jnp.dot(first, second, preferred_element_type=F32)


def from_right(pair, at, table, fast):
    high = pair[at, 0]
    if fast:
        return product(high, table[:SIDE])
    return product(high, table[:SIDE]) + product(high, table[SIDE:]) + product(pair[at, 1], table[:SIDE])


def from_left(table, pair, at, fast):
    high = pair[at, 0]
    if fast:
        return product(table[:, :SIDE], high)
    return product(table[:, :SIDE], high) + product(table[:, SIDE:], high) + product(table[:, :SIDE], pair[at, 1])


CHUNK = 16


def chunks(count):
    return [slice(c * CHUNK, (c + 1) * CHUNK) for c in range(count // CHUNK)]


def woven(matrix_tasks, vector_tasks):
    total, done = len(vector_tasks), 0
    for i, task in enumerate(matrix_tasks):
        task()
        upto = total * (i + 1) // len(matrix_tasks)
        for piece in vector_tasks[done:upto]:
            piece()
        done = upto
    if not matrix_tasks:
        for piece in vector_tasks:
            piece()


def gradients(strip, probe, amp, right, left, work, fast):
    sgrad, pgrad, weight, strength = work["sgrad"], work["pgrad"], work["weight"], work["strength"]
    lhs, rhs, far, mid, res, bright = (work[n] for n in ("lhs", "rhs", "far", "mid", "res", "bright"))
    sgrad[...] = jnp.zeros_like(sgrad)
    pgrad[...] = jnp.zeros_like(pgrad)
    weight[...] = jnp.zeros_like(weight)

    def put_split(ref, at, rows, x):
        if fast:
            ref[at, 0, rows, :] = x.astype(BF16)
        else:
            ref[at, 0, rows, :], ref[at, 1, rows, :] = split(x)

    def one_pattern(p, carry):
        def exit_rows(k):
            def piece(rh, rows):
                full = slice(rh * HALF + rows.start, rh * HALF + rows.stop)
                wave = []
                for u in range(2):
                    o_re, o_im = strip[0, p + u, full, :], strip[1, p + u, full, :]
                    p_re, p_im = probe[k, rh, 0, u, rows, :], probe[k, rh, 1, u, rows, :]
                    wave.append((p_re * o_re - p_im * o_im, p_re * o_im + p_im * o_re))
                put_split(
                    lhs, 2 * (k % 2), full,
                    jnp.concatenate([wave[0][0] + wave[1][0], wave[0][1] + wave[1][1]], axis=1),
                )
                put_split(
                    lhs, 2 * (k % 2) + 1, full,
                    jnp.concatenate([wave[0][0] - wave[1][0], wave[0][1] - wave[1][1]], axis=1),
                )

            return [functools.partial(piece, rh, rows) for rh in range(2) for rows in chunks(HALF)]

        def right_dots(k, back):
            def one(eo):
                at = 2 * (k % 2) + eo
                res[at] = from_right(lhs, at, right[2 * eo + back], fast)

            return [functools.partial(one, eo) for eo in range(2)]

        def fold_rows(k):
            def piece(rows):
                low = slice(HALF + rows.start, HALF + rows.stop)
                at = 2 * (k % 2)
                e_top, e_low, o_top, o_low = res[at, rows, :], res[at, low, :], res[at + 1, rows, :], res[at + 1, low, :]
                for eo in range(2):
                    e = e_top + e_low if eo == 0 else e_top - e_low
                    o = o_top + o_low if eo == 0 else o_top - o_low
                    put_split(rhs, at + eo, rows, jnp.concatenate([e[:, :HALF], o[:, :HALF]], axis=1))
                    put_split(rhs, at + eo, low, jnp.concatenate([e[:, HALF:], o[:, HALF:]], axis=1))

            return [functools.partial(piece, rows) for rows in chunks(HALF)]

        def left_dots(k, back):
            def one(eo):
                at = 2 * (k % 2) + eo
                if back:
                    mid[at] = from_left(left[2 * eo + 1], rhs, at, fast)
                else:
                    far[k, eo] = from_left(left[2 * eo], rhs, at, fast)

            return [functools.partial(one, eo) for eo in range(2)]

        def power_rows(k):
            def piece(eo, rows):
                low = slice(HALF + rows.start, HALF + rows.stop)
                w_re, w_im = far[k, eo, rows, :], far[k, eo, low, :]
                power = w_re * w_re + w_im * w_im
                if k > 0:
                    power = bright[eo, rows, :] + power
                if k == MODES - 1:
                    power = amp[p, eo, rows, :] * lax.rsqrt(power + 1.0)
                bright[eo, rows, :] = power

            return [functools.partial(piece, eo, rows) for eo in range(2) for rows in chunks(HALF)]

        def cut_rows(k):
            def piece(eo, rows):
                low = slice(HALF + rows.start, HALF + rows.stop)
                scale = bright[eo, rows, :]
                put_split(rhs, 2 * (k % 2) + eo, rows, far[k, eo, rows, :] * scale)
                put_split(rhs, 2 * (k % 2) + eo, low, far[k, eo, low, :] * scale)

            return [functools.partial(piece, eo, rows) for eo in range(2) for rows in chunks(HALF)]

        def spread_rows(k):
            def piece(rows):
                low = slice(HALF + rows.start, HALF + rows.stop)
                at = 2 * (k % 2)
                for rh, full in enumerate((rows, low)):
                    if rh == 0:
                        w_re, w_im = mid[at, rows, :] + mid[at + 1, rows, :], mid[at, low, :] + mid[at + 1, low, :]
                    else:
                        w_re, w_im = mid[at, rows, :] - mid[at + 1, rows, :], mid[at, low, :] - mid[at + 1, low, :]
                    put_split(lhs, at, full, jnp.concatenate([w_re[:, :HALF], w_im[:, :HALF]], axis=1))
                    put_split(lhs, at + 1, full, jnp.concatenate([w_re[:, HALF:], w_im[:, HALF:]], axis=1))

            return [functools.partial(piece, rows) for rows in chunks(HALF)]

        def gradient_rows(k):
            def piece(rh, rows):
                full = slice(rh * HALF + rows.start, rh * HALF + rows.stop)
                at = 2 * (k % 2)
                even, odd = res[at, full, :], res[at + 1, full, :]
                for u in range(2):
                    psi = even + odd if u == 0 else even - odd
                    s_re, s_im = psi[:, :HALF], psi[:, HALF:]
                    o_re, o_im = strip[0, p + u, full, :], strip[1, p + u, full, :]
                    p_re, p_im = probe[k, rh, 0, u, rows, :], probe[k, rh, 1, u, rows, :]
                    g_re, g_im = p_re * s_re + p_im * s_im, p_re * s_im - p_im * s_re
                    if k == 0:
                        power = strength[rh, u, rows, :]
                        g_re, g_im = g_re - power * o_re, g_im - power * o_im
                    sgrad[0, p + u, full, :] -= g_re
                    sgrad[1, p + u, full, :] -= g_im
                    pgrad[rh, k, 0, u, rows, :] -= o_re * s_re + o_im * s_im
                    pgrad[rh, k, 1, u, rows, :] -= o_re * s_im - o_im * s_re
                    if k == 0:
                        weight[rh, u, rows, :] += o_re * o_re + o_im * o_im

            return [functools.partial(piece, rh, rows) for rh in range(2) for rows in chunks(HALF)]

        woven([], exit_rows(0))
        woven(right_dots(0, 0), exit_rows(1))
        woven(right_dots(1, 0), fold_rows(0))
        woven(left_dots(0, 0), exit_rows(2))
        woven(right_dots(2, 0), fold_rows(1) + power_rows(0))
        woven(left_dots(1, 0), exit_rows(3))
        woven(right_dots(3, 0), fold_rows(2) + power_rows(1))
        woven(left_dots(2, 0), fold_rows(3))
        woven(left_dots(3, 0), power_rows(2))
        woven([], power_rows(3) + cut_rows(0))
        woven(left_dots(0, 1), cut_rows(1))
        woven(left_dots(1, 1), spread_rows(0))
        woven(right_dots(0, 1), cut_rows(2))
        woven(left_dots(2, 1), spread_rows(1) + gradient_rows(0))
        woven(right_dots(1, 1), cut_rows(3))
        woven(left_dots(3, 1), spread_rows(2) + gradient_rows(1))
        woven(right_dots(2, 1), spread_rows(3))
        woven(right_dots(3, 1), gradient_rows(2))
        woven([], gradient_rows(3))
        return carry

    lax.fori_loop(0, PATS, one_pattern, 0)


WORK = {
    "sgrad": pltpu.VMEM((2, GROUPS, SIDE, HALF), F32),
    "pgrad": pltpu.VMEM((2, MODES, 2, 2, HALF, HALF), F32),
    "weight": pltpu.VMEM((2, 2, HALF, HALF), F32),
    "strength": pltpu.VMEM((2, 2, HALF, HALF), F32),
    "lhs": pltpu.VMEM((4, 2, SIDE, SIDE), BF16),
    "rhs": pltpu.VMEM((4, 2, SIDE, SIDE), BF16),
    "far": pltpu.VMEM((MODES, 2, SIDE, SIDE), F32),
    "mid": pltpu.VMEM((4, SIDE, SIDE), F32),
    "res": pltpu.VMEM((4, SIDE, SIDE), F32),
    "bright": pltpu.VMEM((2, HALF, SIDE), F32),
    "right": pltpu.VMEM((4, 2 * SIDE, SIDE), BF16),
    "left": pltpu.VMEM((4, SIDE, 2 * SIDE), BF16),
    "sems": pltpu.SemaphoreType.DMA((2,)),
}


def hand_over(info, probe, pgrad, weight, kept, given, turned):
    mine = info[2]
    for k in range(MODES):
        mode = (k + info[5]) & 3 if turned else k
        for block in range(4):
            at = (block + info[6]) & 3 if turned else block
            c, u = (at >> 1, at & 1) if turned else (block // 2, block % 2)
            for ref, rh in ((kept, mine), (given, 1 - mine)):
                ref[k, block // 2, block % 2] = pgrad[rh, mode, c, u] + weight[rh, u] * probe[mode, rh, c, u]


def probe_strength(probe, strength):
    most = None
    for rh in range(2):
        for u in range(2):
            for rows in chunks(HALF):
                power = 0.0
                for k in range(MODES):
                    p_re, p_im = probe[k, rh, 0, u, rows, :], probe[k, rh, 1, u, rows, :]
                    power = power + (p_re * p_re + p_im * p_im)
                strength[rh, u, rows, :] = power
                most = power if most is None else jnp.maximum(most, power)
    return jnp.max(most) + 1e-6


def weak_data(strip, strength, energy):
    weak = None
    for p in range(PATS):
        total = 0.0
        for rh in range(2):
            for u in range(2):
                for rows in chunks(HALF):
                    full = slice(rh * HALF + rows.start, rh * HALF + rows.stop)
                    o_re, o_im = strip[0, p + u, full, :], strip[1, p + u, full, :]
                    total = total + strength[rh, u, rows, :] * (o_re * o_re + o_im * o_im)
        small = energy[0, p] < WEAK * WEAK * jnp.sum(total)
        weak = small if weak is None else jnp.logical_and(weak, small)
    return weak


def swap_halves(first, second):
    lane = lax.broadcasted_iota(jnp.int32, first.shape, 1)
    low = lane < TILE
    return (
        jnp.where(low, first, pltpu.roll(second, TILE, 1)),
        jnp.where(low, pltpu.roll(first, TILE, 1), second),
    )


def slot_of(info, perm, r, c):
    row, col = info[0] + r, info[1] + c
    return perm[((row & 7) << 2) + (col & 3)] * 3 + c // 4


def chunk_of(info, r, h, block):
    return (((info[0] + r) & 3) << 3) + h * 4 + block


def start_tables(right_in, left_in, work):
    copies = [
        pltpu.make_async_copy(right_in, work["right"], work["sems"].at[0]),
        pltpu.make_async_copy(left_in, work["left"], work["sems"].at[1]),
    ]
    for copy in copies:
        copy.start()
    return copies


def first_kernel(
    info, perm, tiles, probe, amp, right_in, left_in, strip, send, kept, given, peak, *scratch
):
    work = dict(zip(WORK, scratch))
    sgrad, pgrad, weight = work["sgrad"], work["pgrad"], work["weight"]
    copies = start_tables(right_in, left_in, work)
    for r in range(4):
        for g in range(GROUPS):
            a, b = slot_of(info, perm, r, 2 * g), slot_of(info, perm, r, 2 * g + 1)
            for c in range(2):
                one = tiles[a, pl.ds(c, 32, stride=2), :]
                two = tiles[b, pl.ds(c, 32, stride=2), :]
                top, low = swap_halves(one, two)
                strip[c, g, 64 * r : 64 * r + 32, :] = top
                strip[c, g, 64 * r + 32 : 64 * r + 64, :] = low
    peak[0, 0] = probe_strength(probe, work["strength"])
    for copy in copies:
        copy.wait()
    gradients(strip, probe, amp, work["right"], work["left"], work, False)
    hand_over(info, probe, pgrad, weight, kept, given, False)
    for r in range(4):
        for h in range(2):
            for block in range(4):
                at = chunk_of(info, r, h, block)
                start = 64 * r + 32 * h + 8 * block
                for c in range(2):
                    for g in range(GROUPS):
                        line = (c * GROUPS + g) * 8
                        send[at, line : line + 8, :] = sgrad[c, g, start : start + 8, :]


def second_kernel(
    info, perm, peak, energy, old_strip, first_send, total, other, old_probe, amp, right_in, left_in,
    moved, kept_out, given_out, out_tiles, kept, given, out_sems, strip, probe, *scratch
):
    work = dict(zip(WORK, scratch))
    sgrad, pgrad, weight = work["sgrad"], work["pgrad"], work["weight"]
    copies = start_tables(right_in, left_in, work)
    inverse = 1.0 / peak[0, 0]
    for r in range(4):
        for h in range(2):
            for block in range(4):
                at = chunk_of(info, r, h, block)
                start = 64 * r + 32 * h + 8 * block
                for c in range(2):
                    for g in range(GROUPS):
                        line = (c * GROUPS + g) * 8
                        strip[c, g, start : start + 8, :] = (
                            old_strip[c, g, start : start + 8, :] - total[at, line : line + 8, :] * inverse
                        )
    mine = info[2]
    for k in range(MODES):
        for c in range(2):
            for u in range(2):
                for part in range(2):
                    piece = ((k * 2 + c) * 2 + u) * 2 + part
                    rows = slice(part * 64, part * 64 + 64)
                    probe[k, mine, c, u, rows, :] = (
                        old_probe[k, mine, c, u, rows, :] - total[piece, OBJ_ROWS:, :] * PROBE_STEP
                    )
                    probe[k, 1 - mine, c, u, rows, :] = (
                        old_probe[k, 1 - mine, c, u, rows, :] - other[piece] * PROBE_STEP
                    )
    inverse_now = 1.0 / probe_strength(probe, work["strength"])
    weak = weak_data(strip, work["strength"], energy)
    for copy in copies:
        copy.wait()

    @pl.when(weak)
    def _():
        gradients(strip, probe, amp, work["right"], work["left"], work, True)

    @pl.when(jnp.logical_not(weak))
    def _():
        gradients(strip, probe, amp, work["right"], work["left"], work, False)

    hand_over(info, probe, pgrad, weight, kept, given, True)
    out_copies = [
        pltpu.make_async_copy(given, given_out, out_sems.at[0]),
        pltpu.make_async_copy(kept, kept_out, out_sems.at[1]),
    ]
    for copy in out_copies:
        copy.start()
    for r in range(4):
        for g in range(GROUPS):
            a, b = slot_of(info, perm, r, 2 * g), slot_of(info, perm, r, 2 * g + 1)
            for c in range(2):
                lines = []
                for h in range(2):
                    start = 64 * r + 32 * h
                    line = (c * GROUPS + g) * 8
                    before = jnp.concatenate(
                        [first_send[chunk_of(info, r, h, block), line : line + 8, :] for block in range(4)], axis=0
                    )
                    lines.append(sgrad[c, g, start : start + 32, :] * inverse_now + before * inverse)
                one, two = swap_halves(lines[0], lines[1])
                out_tiles[r, 2 * g, pl.ds(c, 32, stride=2), :] = one
                out_tiles[r, 2 * g + 1, pl.ds(c, 32, stride=2), :] = two
            for col, at in ((2 * g, a), (2 * g + 1, b)):
                pltpu.make_async_copy(out_tiles.at[r, col], moved.at[at], out_sems.at[2]).start()
    for copy in out_copies:
        copy.wait()
    pltpu.make_async_copy(out_tiles, out_tiles, out_sems.at[2]).wait()


def spot_of(spots, t):
    return (spots[t, 0] >> 6) & (BAND_ROWS - 1), spots[t, 1] >> 6


def served_slot(spots, info, t, k):
    row, col = spot_of(spots, t)
    cls = info[4]
    r = ((cls >> 2) - row) & 7
    c = (((cls & 3) - col) & 3) + 4 * k
    valid = jnp.logical_and(r < 4, c < 2 * GROUPS)
    slot = (((row + r) >> 3) << 4) + ((col + c) >> 2)
    return valid, jnp.where(valid, slot, 0)


def pack_kernel(spots, info, tiles, out, sem):
    def one(t, carry):
        for k in range(3):
            valid, slot = served_slot(spots, info, t, k)
            pltpu.make_async_copy(tiles.at[slot], out.at[t * 3 + k], sem).start()
        return carry

    lax.fori_loop(0, N_SCAN, one, 0)
    pltpu.make_async_copy(out, out, sem).wait()


def unpack_kernel(spots, info, tiles, arrived, out):
    out[...] = tiles[...]

    def one(t, carry):
        for k in range(3):
            valid, slot = served_slot(spots, info, t, k)

            @pl.when(valid)
            def _():
                out[slot] -= arrived[t * 3 + k]

        return carry

    lax.fori_loop(0, N_SCAN, one, 0)


def owner_kernel(spots, info, arrived, out, band):
    band[...] = jnp.zeros_like(band)
    rho = info[3] >> 3

    def place(t):
        row, col = spot_of(spots, t)
        r = row + ((rho - row) & 3)
        return r >> 2, col >> 1

    def add(t, carry):
        tr, lg = place(t)
        for c in range(2):
            for g in range(GROUPS):
                line = (c * GROUPS + g) * 8
                band[tr, c, lg + g] += arrived[t, line : line + 8, :]
        return carry

    def give(t, carry):
        tr, lg = place(t)
        for c in range(2):
            for g in range(GROUPS):
                line = (c * GROUPS + g) * 8
                out[t, line : line + 8, :] = band[tr, c, lg + g]
        return carry

    lax.fori_loop(0, N_SCAN, add, 0)
    lax.fori_loop(0, N_SCAN, give, 0)


def chip_sums_kernel(arrived, out, rows, sem):
    copy = pltpu.make_async_copy(arrived.at[:, pl.ds(OBJ_ROWS, PRB_ROWS), :], rows, sem)
    copy.start()
    copy.wait()
    for core in range(2):
        for line in range(0, PRB_ROWS, 16):
            total = rows[core, line : line + 16, :]
            for chip in range(1, N_SCAN // 2):
                total = total + rows[2 * chip + core, line : line + 16, :]
            out[core, line : line + 16, :] = total


def finish_kernel(info, base, half, other_half, out, rows):
    for place, ref in ((0, half), (1, other_half)):
        rh = info[2] if place == 0 else 1 - info[2]
        for turn in range(4):
            at = (info[6] - turn) & 3
            c, u = at >> 1, at & 1
            for r in range(2):
                for h in range(2):
                    lines = slice(64 * r + 32 * h, 64 * r + 32 * h + 32)
                    new = base[rh, c, u, lines, :] - ref[turn, lines, :] * PROBE_STEP
                    rows[c, u, pl.ds(rh * HALF + (64 * r + h), 32, stride=2), :] = new
    for c in range(2):
        for u in range(2):
            out[0, c, :, u * HALF : (u + 1) * HALF] = rows[c, u]


def amplitude_kernel(amp, shuffle, out, energy, moved):
    for p in range(PATS):
        x = amp[p]
        energy[0, p] = jnp.sum(x * x)
        first = x.astype(BF16)
        rest = x - first.astype(F32)
        second = rest.astype(BF16)
        third = (rest - second.astype(F32)).astype(BF16)
        total = None
        for piece in (third, second, first):
            part = jnp.dot(piece, shuffle[...], preferred_element_type=F32)
            total = part if total is None else total + part
        for half in range(2):
            moved[half] = total[:, half * HALF : (half + 1) * HALF]
            for eo in range(2):
                out[p, eo, :, half * HALF : (half + 1) * HALF] = moved[half, pl.ds(eo, HALF, stride=2), :]


SMEM = pl.BlockSpec(memory_space=pltpu.SMEM)
VMEM = pl.BlockSpec(memory_space=pltpu.VMEM)
ANY = pl.BlockSpec(memory_space=pl.ANY)
HBM = pl.BlockSpec(memory_space=pltpu.HBM)


def kernel(body, outs, ins, scratch=(), out_specs=None, name=None, limit=20, cost=None):
    return pl.pallas_call(
        body,
        out_shape=outs,
        in_specs=ins,
        out_specs=out_specs if out_specs is not None else jax.tree.map(lambda _: VMEM, outs),
        scratch_shapes=list(scratch),
        compiler_params=pltpu.CompilerParams(vmem_limit_bytes=limit * 1024 * 1024),
        name=name,
        cost_estimate=None if cost is None else pl.CostEstimate(flops=0, bytes_accessed=cost, transcendentals=0),
    )


def shaped(*shape, dtype=F32):
    return jax.ShapeDtypeStruct(shape, dtype)


def shift(n, k):
    return [(i, (i + k) % n) for i in range(n)]


def shift_y(k):
    return [(i, (i & ~6) | ((((i >> 1) & 3) + k) % 4) << 1) for i in range(N_SCAN)]


def shift_z(k):
    return [(i, (i + 8 * k) % N_SCAN) for i in range(N_SCAN)]


SWAP = [(i, i ^ 1) for i in range(N_SCAN)]


def exchange(x):
    return lax.all_to_all(x, "scan", split_axis=0, concat_axis=0, tiled=True)


def sum_turned(parts, axis, perm_of):
    near, far, middle = (lax.ppermute(parts[k], axis, perm_of(k)) for k in (1, 3, 2))
    return (parts[0] + middle) + (near + far)


def sum_all(x, axis, perm_of):
    near, far, middle = (lax.ppermute(x, axis, perm_of(k)) for k in (1, 3, 2))
    return (x + middle) + (near + far)


def gather_rows(x, at, axis, perm_of):
    stacked = jnp.zeros((4,) + x.shape, x.dtype)
    stacked = lax.dynamic_update_index_in_dim(stacked, x, at, 0)
    for k in (1, 3, 2):
        got = lax.ppermute(x, axis, perm_of(k))
        stacked = lax.dynamic_update_index_in_dim(stacked, got, (at - k) % 4, 0)
    return stacked


def in_order(core, mine, theirs, axis):
    return jnp.where(core == 0, jnp.stack([mine, theirs], axis), jnp.stack([theirs, mine], axis))


def body(amplitude, positions, owner_perm, object_tiles, probe):
    band = lax.axis_index("grp")
    me = lax.axis_index("scan")
    core, y_at = me % 2, me // 2 % 4
    right_np, left_np = dft_tables()
    right, left = jnp.asarray(right_np), jnp.asarray(left_np)
    shuffle_np = np.zeros((SIDE, SIDE), np.float32)
    for m in range(SIDE):
        shuffle_np[m, m // 2 + HALF * (m % 2)] = 1.0
    shuffle = jnp.asarray(shuffle_np.astype(ml_dtypes.bfloat16))

    spots = exchange(jnp.broadcast_to(positions[:1, None], (N_SCAN, 1, 2))).reshape(N_SCAN, 2)
    perm = lax.dynamic_index_in_dim(owner_perm, band, 0, keepdims=False)
    cls = jnp.sum(jnp.where(perm == me, jnp.arange(N_SCAN, dtype=jnp.int32), 0))
    spot = positions[0] // TILE
    info = jnp.stack([spot[0] % BAND_ROWS, spot[1], core, me, cls, band, y_at]).astype(jnp.int32)

    tiles = object_tiles.reshape(TILE, 2, 32, HALF).transpose(0, 2, 1, 3).reshape(TILE, TILE, HALF)
    packed = kernel(
        pack_kernel,
        shaped(96, TILE, HALF),
        [SMEM, SMEM, HBM],
        [pltpu.SemaphoreType.DMA],
        out_specs=HBM,
        name="pack",
    )(spots, info, tiles)
    arrived = exchange(packed)

    own = probe.reshape(2, 2, 2, 32, 2, 2, HALF).transpose(1, 0, 5, 2, 4, 3, 6).reshape(2, 2, 2, HALF, HALF)
    part = gather_rows(lax.dynamic_index_in_dim(own, core, 0, keepdims=False), band, "grp", lambda k: shift(N_GRP, k))
    modes = in_order(core, part, lax.ppermute(part, "scan", SWAP), 1)
    amp, energy = kernel(
        amplitude_kernel,
        (shaped(PATS, 2, HALF, SIDE), shaped(1, PATS)),
        [VMEM, VMEM],
        [pltpu.VMEM((2, SIDE, HALF), F32)],
        out_specs=(VMEM, SMEM),
        name="spread",
    )(amplitude, shuffle)

    scratch = list(WORK.values())
    strip, send, kept, given, peak = kernel(
        first_kernel,
        (
            shaped(2, GROUPS, SIDE, HALF),
            shaped(N_SCAN, SEND_ROWS, HALF),
            shaped(MODES, 2, 2, HALF, HALF),
            shaped(MODES, 2, 2, HALF, HALF),
            shaped(1, 1),
        ),
        [SMEM, SMEM] + [VMEM] * 3 + [HBM] * 2,
        scratch,
        out_specs=(VMEM, VMEM, VMEM, VMEM, SMEM),
        name="first",
        limit=30,
    )(info, perm, arrived, modes, amp, right, left)

    chip = (kept + lax.ppermute(given, "scan", SWAP)).reshape(N_SCAN, PRB_ROWS, HALF)
    send = lax.dynamic_update_slice(send, chip, (0, OBJ_ROWS, 0))
    got = exchange(send)
    both = kernel(
        chip_sums_kernel,
        shaped(2, PRB_ROWS, HALF),
        [ANY],
        [pltpu.VMEM((N_SCAN, PRB_ROWS, HALF), F32), pltpu.SemaphoreType.DMA],
        name="sums",
    )(got)
    summed = sum_all(both, "grp", lambda k: shift(N_GRP, k))
    totals = kernel(
        owner_kernel,
        shaped(N_SCAN, SEND_ROWS, HALF),
        [SMEM, SMEM, VMEM],
        [pltpu.VMEM((8, 2, 32, 8, HALF), F32)],
        name="owner",
    )(spots, info, got)
    answer = jnp.broadcast_to(summed[None], (16, 2, PRB_ROWS, HALF)).reshape(N_SCAN, PRB_ROWS, HALF)
    total = exchange(lax.dynamic_update_slice(totals, answer, (0, OBJ_ROWS, 0)))
    other = lax.ppermute(total[:, OBJ_ROWS:], "scan", SWAP)

    moved, kept, given = kernel(
        second_kernel,
        (shaped(96, TILE, HALF), shaped(MODES, 2, 2, HALF, HALF), shaped(MODES, 2, 2, HALF, HALF)),
        [SMEM, SMEM, SMEM, SMEM] + [VMEM] * 6 + [HBM] * 2,
        [
            pltpu.VMEM((4, 2 * GROUPS, TILE, HALF), F32),
            pltpu.VMEM((MODES, 2, 2, HALF, HALF), F32),
            pltpu.VMEM((MODES, 2, 2, HALF, HALF), F32),
            pltpu.SemaphoreType.DMA((3,)),
            pltpu.VMEM((2, GROUPS, SIDE, HALF), F32),
            pltpu.VMEM((MODES, 2, 2, 2, HALF, HALF), F32),
        ]
        + scratch,
        out_specs=(HBM, HBM, HBM),
        name="second",
        limit=47,
    )(info, perm, peak, energy, strip, send, total, other, modes, amp, right, left)
    returned = exchange(moved)

    theirs = lax.ppermute(given, "scan", SWAP).reshape(4, 4, HALF, HALF)
    kept = kept.reshape(4, 4, HALF, HALF)
    mine = sum_turned([kept[k] + theirs[k] for k in range(4)], "grp", lambda k: shift(N_GRP, k))
    mine = sum_turned([mine[k] for k in range(4)], "scan", shift_y)
    mine = sum_all(mine, "scan", shift_z)
    object_new = kernel(
        unpack_kernel,
        shaped(TILE, TILE, HALF),
        [SMEM, SMEM, VMEM, VMEM],
        name="unpack",
        cost=8 * 1024 * 1024,
    )(spots, info, tiles, returned)
    mine, object_new = lax.optimization_barrier((mine, object_new))
    half = jnp.stack([mine] + [lax.ppermute(mine, "scan", shift_y(k)) for k in (1, 2, 3)])
    other_half = lax.ppermute(half, "scan", SWAP)

    half_one = total[:, OBJ_ROWS:].reshape(MODES, 2, 2, HALF, HALF)
    half_one = lax.dynamic_index_in_dim(half_one, band, 0, keepdims=False)
    half_two = lax.dynamic_index_in_dim(other.reshape(MODES, 2, 2, HALF, HALF), band, 0, keepdims=False)
    base = own - in_order(core, half_one, half_two, 0) * PROBE_STEP
    probe_out = kernel(
        finish_kernel,
        shaped(1, 2, SIDE, SIDE),
        [SMEM, VMEM, VMEM, VMEM],
        [pltpu.VMEM((2, 2, SIDE, HALF), F32)],
        name="finish",
    )(info, base, half, other_half)

    object_out = object_new.reshape(TILE, 32, 2, HALF).transpose(0, 2, 1, 3).reshape(TILE, 2, TILE * TILE)
    return object_out, probe_out


def solution(mesh):
    in_specs = (
        P(("grp", "scan"), None, None),
        P(("grp", "scan"), None),
        P(),
        P(("grp", "scan"), None, None),
        P("grp", None, None, None),
    )
    out_specs = (P(("grp", "scan"), None, None), P("grp", None, None, None))
    return jax.shard_map(body, mesh=mesh, in_specs=in_specs, out_specs=out_specs, check_vma=False)
```

time: 328 us -> 272 us (0.83)
  Pallas kernels: 76.7 us -> 50.5 us
  waiting for transfers between devices: 97.3 us -> 74.8 us
  between operations: 14.5 us -> 2.81 us
  local copies, waits for them, and re-layouts: 11.5 us -> 16.5 us
    all_to_all x3, waiting for transfers between devices: 40.6 us -> 17.9 us  [exchange(): return lax.all_to_all(x, 'scan', split_axis=0, concat_axis=0, tiled=True)]
    pallas_call x5 -> x7, Pallas kernels: 69.1 us -> 46.8 us  [the longest x1 22.3 us: body(): kernel(first_kernel, (shaped(2, GROUPS, SIDE, HALF), shaped(N_SCAN, SEND_...]
    unnamed x12 -> x44, local copies, waits for them, and re-layouts: 1.46 us -> 8.66 us
    pallas_call x1, Pallas kernels: 7.61 us -> 3.69 us  [body(): kernel(unpack_kernel, shaped(TILE, TILE, HALF), [SMEM, SMEM, VMEM, VMEM],...]
    ppermute x15 -> x19, starting transfers between devices: 23.3 us -> 26.7 us  [the longest x6 8.76 us: sum_all(): near, far, middle = (lax.ppermute(x, axis, perm_of(k)) for k in (1, 3, 2))]
    ppermute x6 -> x3, waiting for transfers between devices: 8.35 us -> 10.5 us  [gather_rows(): got = lax.ppermute(x, axis, perm_of(k))]
    ppermute x15 -> x19, waiting for transfers between devices: 45.8 us -> 43.9 us  [the longest x6 29.2 us: sum_turned(): lax.ppermute(parts[k], axis, perm_of(k))]
  transfers between devices with their start and end apart: 26 -> 26, of which waited for: 16 -> 20; matrix products, arithmetic and copies ran while one was open for 2% -> 4% of each run, Pallas kernels for 3% -> 1%
where the time goes in v2:
time: 272 us; the launch traced here: 271 us
  waiting for transfers between devices  74.8 us (28%)
  blocking collectives  70.3 us (26%)
  Pallas kernels  50.5 us (19%)
  starting transfers between devices  50.3 us (18%)
  local copies, waits for them, and re-layouts  16.5 us (6%)
  other arithmetic  5.67 us (2%)
  between operations  2.81 us (1%)
    all_to_all x2, blocking collectives, exchange(): return lax.all_to_all(x, 'scan', split_axis=0, concat_axis=0, tiled=True)  70.3 us
    ppermute x6, waiting for transfers between devices, sum_turned(): lax.ppermute(parts[k], axis, perm_of(k))  29.2 us
    pallas_call x1, Pallas kernels, body(): kernel(first_kernel, (shaped(2, GROUPS, SIDE, HALF), shaped(N_SCAN, SEND_...  22.3 us
    all_to_all x3, starting transfers between devices, exchange(): return lax.all_to_all(x, 'scan', split_axis=0, concat_axis=0, tiled=True)  19.2 us
    all_to_all x3, waiting for transfers between devices, exchange(): return lax.all_to_all(x, 'scan', split_axis=0, concat_axis=0, tiled=True)  17.9 us
    pallas_call x1, Pallas kernels, body(): kernel(second_kernel, (shaped(96, TILE, HALF), shaped(MODES, 2, 2, HALF,...  17.5 us
    ppermute x3, waiting for transfers between devices, gather_rows(): got = lax.ppermute(x, axis, perm_of(k))  10.5 us
    ppermute x6, starting transfers between devices, sum_all(): near, far, middle = (lax.ppermute(x, axis, perm_of(k)) for k in (1, 3, 2))  8.76 us
  transfers between devices with their start and end apart: 26, of which 20 were waited for; matrix products, arithmetic and copies ran while one was open for 4% of the time, Pallas kernels for 1%

profile of v2, /device:TPU:1, one launch (start us, length us, event | category | flops | bytes accessed | tf_op | source)
XLA Modules:
  0.0 270.8 jit_solution(9673635119161999240)
XLA Ops:
  0.6 0.8 slice_reduce_fusion
  1.4 0.6 broadcast_in_dim.31
  2.0 9.6 %all-to-all-start = ((s32[32,1,2]{2,1,0:T(1,128)}), s32[32,1,2]{2,1,0:T(1,128)S(1)}, u32[]{:S(2)}, u32[]{:S(2)}) async-start(s32[32,1,2]{2,1,0:T(1,128)} %broadcast_in_dim.31), calls=%async_computation | async-start | bytes 32768 | tf_op jit(solution)/shard_map/all_to_all | solution.py:596
  11.7 0.6 fusion.8
  14.0 1.3 fusion.5
  15.3 1.3 stack.66.info
  16.6 1.9 all-to-all-done
  18.5 1.6 copy-done.2
  20.1 2.5 pack.1
  22.6 5.7 %all-to-all-start.1 = ((f32[96,64,128]{2,1,0:T(8,128)}), f32[96,64,128]{2,1,0:T(8,128)}, u32[]{:S(2)}, u32[]{:S(2)}) async-start(f32[96,64,128]{2,1,0:T(8,128)} %pack.1), calls=%async_computation.1 | async-start | bytes 6291456 | tf_op jit(solution)/shard_map/all_to_all | solution.py:596
  28.3 0.3 reshape.66
  28.8 0.7 dynamic-slice_bitcast_fusion
  29.5 1.2 collective-permute-start
  30.8 1.5 collective-permute-start.1
  32.2 1.5 collective-permute-start.2
  33.8 4.9 %collective-permute-done = f32[2,2,128,128]{3,2,1,0:T(8,128)} collective-permute-done((f32[2,2,128,128]{3,2,1,0:T(8,128)}, f32[2,2,128,128]{3,2,1,0:T(8,128)}, u32[]{:S(2)}, u32[]{:S(2)}) %collective-permute-start) | collective-permute-done | bytes 262176 | tf_op jit(solution)/shard_map/ppermute | solution.py:613
  38.7 1.0 bitcast_dynamic-update-slice_fusion.2
  39.7 5.6 %collective-permute-done.2 = f32[2,2,128,128]{3,2,1,0:T(8,128)S(1)} collective-permute-done((f32[2,2,128,128]{3,2,1,0:T(8,128)}, f32[2,2,128,128]{3,2,1,0:T(8,128)S(1)}, u32[]{:S(2)}, u32[]{:S(2)}) %collective-permute-start.2) | collective-permute-done | bytes 262176 | tf_op jit(solution)/shard_map/ppermute | solution.py:613
  45.3 1.1 collective-permute-start.3
  46.4 1.2 spread.1
  47.6 1.0 copy-done.7
  48.8 2.7 maximum_select_fusion.probe.old_probe
  51.5 16.0 %all-to-all-done.1.tiles = f32[96,64,128]{2,1,0:T(8,128)} async-done(((f32[96,64,128]{2,1,0:T(8,128)}), f32[96,64,128]{2,1,0:T(8,128)}, u32[]{:S(2)}, u32[]{:S(2)}) %all-to-all-start.1) | async-done | bytes 3145760 | tf_op jit(solution)/shard_map/all_to_all | solution.py:596
  67.5 1.2 copy-done.5
  68.7 1.2 copy-done.8
  70.0 22.3 %first.1 = (f32[2,5,256,128]{3,2,1,0:T(8,128)S(1)}, f32[32,144,128]{2,1,0:T(8,128)S(1)}, f32[4,2,2,128,128]{4,3,2,1,0:T(8,128)S(1)}, f32[4,2,2,128,128]{4,3,2,1,0:T(8,128)S(1)}, f32[1,1]{1,0:T(1,128)}) custom-call(s32[7]{0:T(128)S(1)} %stack.66.info, s32[32]{0:T(128)S(1)} %get-tuple-element.27.perm, f32[96,64,128]{2,1,0:T(8,128)} %all-to-all-done.1.tiles, ...), custom_call_target="tpu_custom_call" | custom-call | tf_op jit(solution)/shard_map/first/pallas_call | solution.py:663
  92.3 2.9 %collective-permute-start.4 = (f32[4,2,2,128,128]{4,3,2,1,0:T(8,128)S(1)}, f32[4,2,2,128,128]{4,3,2,1,0:T(8,128)S(1)}, u32[]{:S(2)}, u32[]{:S(2)}) collective-permute-start(f32[4,2,2,128,128]{4,3,2,1,0:T(8,128)S(1)} %get-tuple-element.20), channel_id=1, source_target_pairs={{0,1},{1,0},{2,3},{3,2},{4,5},{5,4},{6,7},{7,6},{8,9},{9,8},{10,11... | collective-permute-start | bytes 3145736 | tf_op jit(solution)/shard_map/ppermute | solution.py:679
  95.2 2.3 collective-permute-done.4
  97.7 34.6 %all_to_all.25.arrived = f32[32,144,128]{2,1,0:T(8,128)S(1)} all-to-all(f32[32,144,128]{2,1,0:T(8,128)S(1)} %constant_dynamic-update-slice_fusion.1.first_send), channel_id=1, replica_groups=mesh['grp'=4,'scan'=32] {'scan'}, dimensions={0} | all-to-all | bytes 4718592 | tf_op jit(solution)/shard_map/all_to_all | solution.py:596
  132.4 2.5 collective-permute-start.7
  135.0 1.7 collective-permute-start.5
  136.7 1.7 owner.1
  138.5 2.7 collective-permute-done.6
  141.4 35.7 %all_to_all.26.total = f32[32,144,128]{2,1,0:T(8,128)S(1)} all-to-all(f32[32,144,128]{2,1,0:T(8,128)S(1)} %constant_dynamic-update-slice_fusion), channel_id=1, replica_groups=mesh['grp'=4,'scan'=32] {'scan'}, dimensions={0} | all-to-all | bytes 4718592 | tf_op jit(solution)/shard_map/all_to_all | solution.py:596
  177.5 2.5 collective-permute-done.8.other
  180.0 17.5 %second.1 = (f32[96,64,128]{2,1,0:T(8,128)}, f32[4,2,2,128,128]{4,3,2,1,0:T(8,128)S(1)}, f32[4,2,2,128,128]{4,3,2,1,0:T(8,128)S(1)}) custom-call(s32[7]{0:T(128)S(1)} %stack.66.info, s32[32]{0:T(128)S(1)} %get-tuple-element.27.perm, f32[1,1]{1,0:T(1,128)} %get-tuple-element.15.peak, f32[1,4]{1,0:T(1,128)S(1)} %get-tuple-element.16.energy, ...), custom_call_target="tpu_custom_call" | custom-call | tf_op jit(solution)/shard_map/second/pallas_call | solution.py:701
  197.5 1.0 copy-done.12
  198.5 1.0 copy-done.15
  199.5 3.9 %all-to-all-start.4 = ((f32[96,64,128]{2,1,0:T(8,128)}), f32[96,64,128]{2,1,0:T(8,128)S(1)}, u32[]{:S(2)}, u32[]{:S(2)}) async-start(f32[96,64,128]{2,1,0:T(8,128)} %get-tuple-element.23), calls=%async_computation.4 | async-start | bytes 6291456 | tf_op jit(solution)/shard_map/all_to_all | solution.py:596
  203.4 0.4 collective-permute-start.9
  203.8 2.5 collective-permute-done.9
  206.3 1.4 slice_add_fusion
  207.8 2.7 collective-permute-start.12
  210.4 0.8 collective-permute-start.10
  211.2 5.3 %collective-permute-done.11 = f32[4,128,128]{2,1,0:T(8,128)S(1)} collective-permute-done((f32[4,128,128]{2,1,0:T(8,128)S(1)}, f32[4,128,128]{2,1,0:T(8,128)S(1)}, u32[]{:S(2)}, u32[]{:S(2)}) %collective-permute-start.11) | collective-permute-done | bytes 262176 | tf_op jit(solution)/shard_map/ppermute | solution.py:600
  216.5 6.4 %collective-permute-done.10 = f32[4,128,128]{2,1,0:T(8,128)S(1)} collective-permute-done((f32[4,128,128]{2,1,0:T(8,128)S(1)}, f32[4,128,128]{2,1,0:T(8,128)S(1)}, u32[]{:S(2)}, u32[]{:S(2)}) %collective-permute-start.10) | collective-permute-done | bytes 262176 | tf_op jit(solution)/shard_map/ppermute | solution.py:600
  223.0 2.7 collective-permute-start.15
  225.7 1.7 collective-permute-start.13
  227.4 13.6 %collective-permute-done.15 = f32[128,128]{1,0:T(8,128)S(1)} collective-permute-done((f32[128,128]{1,0:T(8,128)S(1)}, f32[128,128]{1,0:T(8,128)S(1)}, u32[]{:S(2)}, u32[]{:S(2)}) %collective-permute-start.15) | collective-permute-done | bytes 65568 | tf_op jit(solution)/shard_map/ppermute | solution.py:600
  241.0 1.1 collective-permute-done.14
  242.1 2.7 %collective-permute-done.13 = f32[128,128]{1,0:T(8,128)S(1)} collective-permute-done((f32[128,128]{1,0:T(8,128)S(1)}, f32[128,128]{1,0:T(8,128)S(1)}, u32[]{:S(2)}, u32[]{:S(2)}) %collective-permute-start.13) | collective-permute-done | bytes 65568 | tf_op jit(solution)/shard_map/ppermute | solution.py:600
  244.9 3.2 %collective-permute-start.18 = (f32[128,128]{1,0:T(8,128)S(1)}, f32[128,128]{1,0:T(8,128)S(1)}, u32[]{:S(2)}, u32[]{:S(2)}) collective-permute-start(f32[128,128]{1,0:T(8,128)S(1)} %fusion.4), channel_id=1, source_target_pairs={{0,24},{1,25},{2,26},{3,27},{4,28},{5,29},{6,30},{7,31},{8,0},{9,1... | collective-permute-start | bytes 196616 | tf_op jit(solution)/shard_map/ppermute | solution.py:605
  248.1 1.3 collective-permute-start.16
  249.5 3.7 %collective-permute-done.17 = f32[128,128]{1,0:T(8,128)S(1)} collective-permute-done((f32[128,128]{1,0:T(8,128)S(1)}, f32[128,128]{1,0:T(8,128)S(1)}, u32[]{:S(2)}, u32[]{:S(2)}) %collective-permute-start.17) | collective-permute-done | bytes 65568 | tf_op jit(solution)/shard_map/ppermute | solution.py:605
  253.2 1.6 copy-done.3
  254.8 3.7 %unpack.1 = f32[64,64,128]{2,1,0:T(8,128)} custom-call(s32[32,2]{1,0:T(8,128)S(1)} %bitcast.69, s32[7]{0:T(128)S(1)} %stack.66.info, f32[64,64,128]{2,1,0:T(8,128)S(1)} %bitcast.65, f32[96,64,128]{2,1,0:T(8,128)S(1)} %all-to-all-done.4.arrived), custom_call_target="tpu_custom_call" | custom-call | bytes 8388608 | tf_op jit(solution)/shard_map/unpack/pallas_call | solution.py:725
  258.5 1.3 collective-permute-start.20
  259.9 1.0 constant_dynamic-slice_fusion.1
  260.9 0.7 collective-permute-done.21
  261.6 1.5 collective-permute-done.20
  263.1 1.0 collective-permute-done.19
  264.2 4.1 %collective-permute-start.22 = (f32[4,128,128]{2,1,0:T(8,128)S(1)}, f32[4,128,128]{2,1,0:T(8,128)S(1)}, u32[]{:S(2)}, u32[]{:S(2)}) collective-permute-start(f32[4,128,128]{2,1,0:T(8,128)S(1)} %pad_maximum_fusion.half), channel_id=1, source_target_pairs={{0,1},{1,0},{2,3},{3,2},{4,5},{5,4},{6,7},{7,6},{8,9},{9,8},{10,11... | collective-permute-start | bytes 786440 | tf_op jit(solution)/shard_map/ppermute | solution.py:734
  268.2 1.0 constant_dynamic-slice_fusion
  269.4 1.4 finish.1
  (71 shorter events, 2.0 us)
Async XLA Ops:
  2.0 16.5 %all-to-all-start = ((s32[32,1,2]{2,1,0:T(1,128)}), s32[32,1,2]{2,1,0:T(1,128)S(1)}, u32[]{:S(2)}, u32[]{:S(2)}) async-start(s32[32,1,2]{2,1,0:T(1,128)} %broadcast_in_dim.31), calls=%async_computation | async-start | bytes 32768 | tf_op jit(solution)/shard_map/all_to_all | solution.py:596
  18.5 1.6 copy-start.2
  22.6 5.7 %copy-start.21 = (f32[1,2,256,256]{3,2,1,0:T(8,128)S(1)}, f32[1,2,256,256]{3,2,1,0:T(8,128)}, u32[]{:S(2)}) copy-start(f32[1,2,256,256]{3,2,1,0:T(8,128)} %param.12) | copy-start | bytes 1572868
  22.6 44.9 %all-to-all-start.1 = ((f32[96,64,128]{2,1,0:T(8,128)}), f32[96,64,128]{2,1,0:T(8,128)}, u32[]{:S(2)}, u32[]{:S(2)}) async-start(f32[96,64,128]{2,1,0:T(8,128)} %pack.1), calls=%async_computation.1 | async-start | bytes 6291456 | tf_op jit(solution)/shard_map/all_to_all | solution.py:596
  28.6 17.8 %copy-start.13 = (f32[4,256,256]{2,1,0:T(8,128)S(1)}, f32[4,256,256]{2,1,0:T(8,128)}, u32[]{:S(2)}) copy-start(f32[4,256,256]{2,1,0:T(8,128)} %amp.1) | copy-start | bytes 3145732
  28.6 17.8 %copy-start.14 = (bf16[256,256]{1,0:T(8,128)(2,1)S(1)}, bf16[256,256]{1,0:T(8,128)(2,1)}, u32[]{:S(2)}) copy-start(bf16[256,256]{1,0:T(8,128)(2,1)} %constant.124.clone.shuffle) | copy-start | bytes 393220
  28.7 20.1 %copy-start.18 = (f32[2,2,2,32,2,2,128]{6,3,4,2,5,0,1:T(8,128)}, f32[2,2,2,32,2,2,128]{6,3,4,2,5,0,1:T(8,128)S(1)}, u32[]{:S(2)}) copy-start(f32[2,2,2,32,2,2,128]{6,3,4,2,5,0,1:T(8,128)S(1)} %copy.19) | copy-start | bytes 1572868
  29.5 9.1 %collective-permute-start = (f32[2,2,128,128]{3,2,1,0:T(8,128)}, f32[2,2,128,128]{3,2,1,0:T(8,128)}, u32[]{:S(2)}, u32[]{:S(2)}) collective-permute-start(f32[2,2,128,128]{3,2,1,0:T(8,128)} %get-tuple-element.32), channel_id=1, source_target_pairs={{0,32},{32,64},{64,96},{96,0},{1,33},{33,65},{65,97},{97,1},{2,34}... | collective-permute-start | bytes 786440 | tf_op jit(solution)/shard_map/ppermute | solution.py:613
  30.8 8.9 %collective-permute-start.1 = (f32[2,2,128,128]{3,2,1,0:T(8,128)}, f32[2,2,128,128]{3,2,1,0:T(8,128)S(1)}, u32[]{:S(2)}, u32[]{:S(2)}) collective-permute-start(f32[2,2,128,128]{3,2,1,0:T(8,128)} %get-tuple-element.32), channel_id=1, source_target_pairs={{0,96},{32,0},{64,32},{96,64},{1,97},{33,1},{65,33},{97,65},{2,98}... | collective-permute-start | bytes 786440 | tf_op jit(solution)/shard_map/ppermute | solution.py:613
  32.2 13.1 %collective-permute-start.2 = (f32[2,2,128,128]{3,2,1,0:T(8,128)}, f32[2,2,128,128]{3,2,1,0:T(8,128)S(1)}, u32[]{:S(2)}, u32[]{:S(2)}) collective-permute-start(f32[2,2,128,128]{3,2,1,0:T(8,128)} %get-tuple-element.32), channel_id=1, source_target_pairs={{0,64},{32,96},{64,0},{96,32},{1,65},{33,97},{65,1},{97,33},{2,66}... | collective-permute-start | bytes 786440 | tf_op jit(solution)/shard_map/ppermute | solution.py:613
  45.3 3.5 %copy-start.17 = (f32[4,2,2,128,128]{4,3,2,1,0:T(8,128)}, f32[4,2,2,128,128]{4,3,2,1,0:T(8,128)S(1)}, u32[]{:S(2)}) copy-start(f32[4,2,2,128,128]{4,3,2,1,0:T(8,128)S(1)} %bitcast_dynamic-update-slice_fusion) | copy-start | bytes 3145732
  45.3 3.5 %collective-permute-start.3 = (f32[4,2,2,128,128]{4,3,2,1,0:T(8,128)S(1)}, f32[4,2,2,128,128]{4,3,2,1,0:T(8,128)}, u32[]{:S(2)}, u32[]{:S(2)}) collective-permute-start(f32[4,2,2,128,128]{4,3,2,1,0:T(8,128)S(1)} %bitcast_dynamic-update-slice_fusion), channel_id=1, source_target_pairs={{0,1},{1,0},{2,3},{3,2},{4,5},{5,4},{6,7},{7,6},{8,9},{9,8},{10,11... | collective-permute-start | bytes 3145736 | tf_op jit(solution)/shard_map/ppermute | solution.py:652
  47.6 1.0 copy-start.7
  48.6 18.9 %copy-start.4 = (bf16[4,256,512]{2,1,0:T(8,128)(2,1)S(1)}, bf16[4,256,512]{2,1,0:T(8,128)(2,1)}, u32[]{:S(2)}) copy-start(bf16[4,256,512]{2,1,0:T(8,128)(2,1)} %constant.123.clone.left_in) | copy-start | bytes 3145732
  51.5 40.8 %copy-start = (f32[4,2,2,2,128,128]{5,4,3,2,1,0:T(8,128)}, f32[4,2,2,2,128,128]{5,4,3,2,1,0:T(8,128)S(1)}, u32[]{:S(2)}) copy-start(f32[4,2,2,2,128,128]{5,4,3,2,1,0:T(8,128)S(1)} %maximum_select_fusion.probe.old_probe) | copy-start | bytes 6291460
  67.5 1.2 copy-start.5
  68.7 1.2 copy-start.8
  92.3 5.4 %copy-start.11 = (f32[2,5,256,128]{3,2,1,0:T(8,128)}, f32[2,5,256,128]{3,2,1,0:T(8,128)S(1)}, u32[]{:S(2)}) copy-start(f32[2,5,256,128]{3,2,1,0:T(8,128)S(1)} %get-tuple-element.17.old_strip) | copy-start | bytes 3932164
  92.3 5.2 %collective-permute-start.4 = (f32[4,2,2,128,128]{4,3,2,1,0:T(8,128)S(1)}, f32[4,2,2,128,128]{4,3,2,1,0:T(8,128)S(1)}, u32[]{:S(2)}, u32[]{:S(2)}) collective-permute-start(f32[4,2,2,128,128]{4,3,2,1,0:T(8,128)S(1)} %get-tuple-element.20), channel_id=1, source_target_pairs={{0,1},{1,0},{2,3},{3,2},{4,5},{5,4},{6,7},{7,6},{8,9},{9,8},{10,11... | collective-permute-start | bytes 3145736 | tf_op jit(solution)/shard_map/ppermute | solution.py:679
  97.7 34.6 %copy-start.1 = (f32[32,144,128]{2,1,0:T(8,128)}, f32[32,144,128]{2,1,0:T(8,128)S(1)}, u32[]{:S(2)}) copy-start(f32[32,144,128]{2,1,0:T(8,128)S(1)} %constant_dynamic-update-slice_fusion.1.first_send) | copy-start | bytes 7077892
  132.4 6.0 %collective-permute-start.7 = (f32[2,64,128]{2,1,0:T(8,128)S(1)}, f32[2,64,128]{2,1,0:T(8,128)S(1)}, u32[]{:S(2)}, u32[]{:S(2)}) collective-permute-start(f32[2,64,128]{2,1,0:T(8,128)S(1)} %sums.1), channel_id=1, source_target_pairs={{0,96},{32,0},{64,32},{96,64},{1,97},{33,1},{65,33},{97,65},{2,98}... | collective-permute-start | bytes 196616 | tf_op jit(solution)/shard_map/ppermute | solution.py:605
  135.0 6.1 %collective-permute-start.6 = (f32[2,64,128]{2,1,0:T(8,128)S(1)}, f32[2,64,128]{2,1,0:T(8,128)S(1)}, u32[]{:S(2)}, u32[]{:S(2)}) collective-permute-start(f32[2,64,128]{2,1,0:T(8,128)S(1)} %sums.1), channel_id=1, source_target_pairs={{0,32},{32,64},{64,96},{96,0},{1,33},{33,65},{65,97},{97,1},{2,34}... | collective-permute-start | bytes 196616 | tf_op jit(solution)/shard_map/ppermute | solution.py:605
  135.0 6.1 %collective-permute-start.5 = (f32[2,64,128]{2,1,0:T(8,128)S(1)}, f32[2,64,128]{2,1,0:T(8,128)S(1)}, u32[]{:S(2)}, u32[]{:S(2)}) collective-permute-start(f32[2,64,128]{2,1,0:T(8,128)S(1)} %sums.1), channel_id=1, source_target_pairs={{0,64},{32,96},{64,0},{96,32},{1,65},{33,97},{65,1},{97,33},{2,66}... | collective-permute-start | bytes 196616 | tf_op jit(solution)/shard_map/ppermute | solution.py:605
  141.3 38.6 %copy-start.6 = (bf16[4,512,256]{2,1,0:T(8,128)(2,1)S(1)}, bf16[4,512,256]{2,1,0:T(8,128)(2,1)}, u32[]{:S(2)}) copy-start(bf16[4,512,256]{2,1,0:T(8,128)(2,1)} %constant.122.clone.right_in) | copy-start | bytes 3145732
  141.4 38.6 %copy-start.9 = (f32[4,2,128,256]{3,2,1,0:T(8,128)S(1)}, f32[4,2,128,256]{3,2,1,0:T(8,128)}, u32[]{:S(2)}) copy-start(f32[4,2,128,256]{3,2,1,0:T(8,128)} %copy-done.7) | copy-start | bytes 3145732
  177.1 2.9 %copy-start.16 = (f32[32,144,128]{2,1,0:T(8,128)}, f32[32,144,128]{2,1,0:T(8,128)S(1)}, u32[]{:S(2)}) copy-start(f32[32,144,128]{2,1,0:T(8,128)S(1)} %all_to_all.26.total) | copy-start | bytes 7077892
  177.2 2.8 %copy-start.20 = (f32[32,64,128]{2,1,0:T(8,128)}, f32[32,64,128]{2,1,0:T(8,128)S(1)}, u32[]{:S(2)}) copy-start(f32[32,64,128]{2,1,0:T(8,128)S(1)} %slice.74) | copy-start | bytes 3145732
  177.2 2.7 %collective-permute-start.8 = (f32[32,64,128]{2,1,0:T(8,128)S(1)}, f32[32,64,128]{2,1,0:T(8,128)S(1)}, u32[]{:S(2)}, u32[]{:S(2)}) collective-permute-start(f32[32,64,128]{2,1,0:T(8,128)S(1)} %slice.74), channel_id=1, source_target_pairs={{0,1},{1,0},{2,3},{3,2},{4,5},{5,4},{6,7},{7,6},{8,9},{9,8},{10,11... | collective-permute-start | bytes 3145736 | tf_op jit(solution)/shard_map/ppermute | solution.py:699
  180.0 17.5 %copy-start.10 = (f32[32,64,128]{2,1,0:T(8,128)}, f32[32,64,128]{2,1,0:T(8,128)S(1)}, u32[]{:S(2)}) copy-start(f32[32,64,128]{2,1,0:T(8,128)S(1)} %collective-permute-done.8.other) | copy-start | bytes 3145732
  197.5 1.0 copy-start.12
  198.5 1.0 copy-start.15
  199.5 53.7 %all-to-all-start.4 = ((f32[96,64,128]{2,1,0:T(8,128)}), f32[96,64,128]{2,1,0:T(8,128)S(1)}, u32[]{:S(2)}, u32[]{:S(2)}) async-start(f32[96,64,128]{2,1,0:T(8,128)} %get-tuple-element.23), calls=%async_computation.4 | async-start | bytes 6291456 | tf_op jit(solution)/shard_map/all_to_all | solution.py:596
  203.4 3.0 %collective-permute-start.9 = (f32[4,2,2,128,128]{4,3,2,1,0:T(8,128)}, f32[4,2,2,128,128]{4,3,2,1,0:T(8,128)S(1)}, u32[]{:S(2)}, u32[]{:S(2)}) collective-permute-start(f32[4,2,2,128,128]{4,3,2,1,0:T(8,128)} %copy-done.15), channel_id=1, source_target_pairs={{0,1},{1,0},{2,3},{3,2},{4,5},{5,4},{6,7},{7,6},{8,9},{9,8},{10,11... | collective-permute-start | bytes 3145736 | tf_op jit(solution)/shard_map/ppermute | solution.py:720
  207.7 8.8 %collective-permute-start.11 = (f32[4,128,128]{2,1,0:T(8,128)S(1)}, f32[4,128,128]{2,1,0:T(8,128)S(1)}, u32[]{:S(2)}, u32[]{:S(2)}) collective-permute-start(f32[4,128,128]{2,1,0:T(8,128)S(1)} %bitcast.78), channel_id=1, source_target_pairs={{0,32},{32,64},{64,96},{96,0},{1,33},{33,65},{65,97},{97,1},{2,34}... | collective-permute-start | bytes 786440 | tf_op jit(solution)/shard_map/ppermute | solution.py:600
  207.8 8.7 %collective-permute-start.12 = (f32[4,128,128]{2,1,0:T(8,128)S(1)}, f32[4,128,128]{2,1,0:T(8,128)S(1)}, u32[]{:S(2)}, u32[]{:S(2)}) collective-permute-start(f32[4,128,128]{2,1,0:T(8,128)S(1)} %bitcast.77), channel_id=1, source_target_pairs={{0,96},{32,0},{64,32},{96,64},{1,97},{33,1},{65,33},{97,65},{2,98}... | collective-permute-start | bytes 786440 | tf_op jit(solution)/shard_map/ppermute | solution.py:600
  210.4 12.4 %collective-permute-start.10 = (f32[4,128,128]{2,1,0:T(8,128)S(1)}, f32[4,128,128]{2,1,0:T(8,128)S(1)}, u32[]{:S(2)}, u32[]{:S(2)}) collective-permute-start(f32[4,128,128]{2,1,0:T(8,128)S(1)} %bitcast.76), channel_id=1, source_target_pairs={{0,64},{32,96},{64,0},{96,32},{1,65},{33,97},{65,1},{97,33},{2,66}... | collective-permute-start | bytes 786440 | tf_op jit(solution)/shard_map/ppermute | solution.py:600
  223.0 18.1 %collective-permute-start.15 = (f32[128,128]{1,0:T(8,128)S(1)}, f32[128,128]{1,0:T(8,128)S(1)}, u32[]{:S(2)}, u32[]{:S(2)}) collective-permute-start(f32[128,128]{1,0:T(8,128)S(1)} %get-tuple-element.34), channel_id=1, source_target_pairs={{0,6},{1,7},{2,0},{3,1},{4,2},{5,3},{6,4},{7,5},{8,14},{9,15},{10,... | collective-permute-start | bytes 196616 | tf_op jit(solution)/shard_map/ppermute | solution.py:600
  225.7 16.5 %collective-permute-start.14 = (f32[128,128]{1,0:T(8,128)S(1)}, f32[128,128]{1,0:T(8,128)S(1)}, u32[]{:S(2)}, u32[]{:S(2)}) collective-permute-start(f32[128,128]{1,0:T(8,128)S(1)} %get-tuple-element.35), channel_id=1, source_target_pairs={{0,2},{1,3},{2,4},{3,5},{4,6},{5,7},{6,0},{7,1},{8,10},{9,11},{10,... | collective-permute-start | bytes 196616 | tf_op jit(solution)/shard_map/ppermute | solution.py:600
  225.7 19.2 %collective-permute-start.13 = (f32[128,128]{1,0:T(8,128)S(1)}, f32[128,128]{1,0:T(8,128)S(1)}, u32[]{:S(2)}, u32[]{:S(2)}) collective-permute-start(f32[128,128]{1,0:T(8,128)S(1)} %get-tuple-element.36), channel_id=1, source_target_pairs={{0,4},{1,5},{2,6},{3,7},{4,0},{5,1},{6,2},{7,3},{8,12},{9,13},{10,... | collective-permute-start | bytes 196616 | tf_op jit(solution)/shard_map/ppermute | solution.py:600
  244.9 4.6 %collective-permute-start.18 = (f32[128,128]{1,0:T(8,128)S(1)}, f32[128,128]{1,0:T(8,128)S(1)}, u32[]{:S(2)}, u32[]{:S(2)}) collective-permute-start(f32[128,128]{1,0:T(8,128)S(1)} %fusion.4), channel_id=1, source_target_pairs={{0,24},{1,25},{2,26},{3,27},{4,28},{5,29},{6,30},{7,31},{8,0},{9,1... | collective-permute-start | bytes 196616 | tf_op jit(solution)/shard_map/ppermute | solution.py:605
  248.1 5.0 %collective-permute-start.17 = (f32[128,128]{1,0:T(8,128)S(1)}, f32[128,128]{1,0:T(8,128)S(1)}, u32[]{:S(2)}, u32[]{:S(2)}) collective-permute-start(f32[128,128]{1,0:T(8,128)S(1)} %fusion.4), channel_id=1, source_target_pairs={{0,8},{1,9},{2,10},{3,11},{4,12},{5,13},{6,14},{7,15},{8,16},{9,17... | collective-permute-start | bytes 196616 | tf_op jit(solution)/shard_map/ppermute | solution.py:605
  248.1 5.0 %collective-permute-start.16 = (f32[128,128]{1,0:T(8,128)S(1)}, f32[128,128]{1,0:T(8,128)S(1)}, u32[]{:S(2)}, u32[]{:S(2)}) collective-permute-start(f32[128,128]{1,0:T(8,128)S(1)} %fusion.4), channel_id=1, source_target_pairs={{0,16},{1,17},{2,18},{3,19},{4,20},{5,21},{6,22},{7,23},{8,24},{9,... | collective-permute-start | bytes 196616 | tf_op jit(solution)/shard_map/ppermute | solution.py:605
  253.2 1.6 copy-start.3
  254.8 14.4 %copy-start.19 = (f32[2,2,2,32,2,2,128]{6,3,4,2,5,0,1:T(8,128)S(1)}, f32[2,2,2,32,2,2,128]{6,3,4,2,5,0,1:T(8,128)}, u32[]{:S(2)}) copy-start(f32[2,2,2,32,2,2,128]{6,3,4,2,5,0,1:T(8,128)} %copy-done.18) | copy-start | bytes 1572868
  258.5 3.1 %collective-permute-start.21 = (f32[128,128]{1,0:T(8,128)S(1)}, f32[128,128]{1,0:T(8,128)S(1)}, u32[]{:S(2)}, u32[]{:S(2)}) collective-permute-start(f32[128,128]{1,0:T(8,128)S(1)} %add_add_fusion), channel_id=1, source_target_pairs={{0,6},{1,7},{2,0},{3,1},{4,2},{5,3},{6,4},{7,5},{8,14},{9,15},{10,... | collective-permute-start | bytes 196616 | tf_op jit(solution)/shard_map/ppermute | solution.py:733
  258.5 4.6 %collective-permute-start.20 = (f32[128,128]{1,0:T(8,128)S(1)}, f32[128,128]{1,0:T(8,128)S(1)}, u32[]{:S(2)}, u32[]{:S(2)}) collective-permute-start(f32[128,128]{1,0:T(8,128)S(1)} %add_add_fusion), channel_id=1, source_target_pairs={{0,4},{1,5},{2,6},{3,7},{4,0},{5,1},{6,2},{7,3},{8,12},{9,13},{10,... | collective-permute-start | bytes 196616 | tf_op jit(solution)/shard_map/ppermute | solution.py:733
  259.8 4.3 %collective-permute-start.19 = (f32[128,128]{1,0:T(8,128)S(1)}, f32[128,128]{1,0:T(8,128)S(1)}, u32[]{:S(2)}, u32[]{:S(2)}) collective-permute-start(f32[128,128]{1,0:T(8,128)S(1)} %add_add_fusion), channel_id=1, source_target_pairs={{0,2},{1,3},{2,4},{3,5},{4,6},{5,7},{6,0},{7,1},{8,10},{9,11},{10,... | collective-permute-start | bytes 196616 | tf_op jit(solution)/shard_map/ppermute | solution.py:733
  264.2 5.2 %collective-permute-start.22 = (f32[4,128,128]{2,1,0:T(8,128)S(1)}, f32[4,128,128]{2,1,0:T(8,128)S(1)}, u32[]{:S(2)}, u32[]{:S(2)}) collective-permute-start(f32[4,128,128]{2,1,0:T(8,128)S(1)} %pad_maximum_fusion.half), channel_id=1, source_target_pairs={{0,1},{1,0},{2,3},{3,2},{4,5},{5,4},{6,7},{7,6},{8,9},{9,8},{10,11... | collective-permute-start | bytes 786440 | tf_op jit(solution)/shard_map/ppermute | solution.py:734

commit v3 on v2

--- a/solution.py
+++ b/solution.py
@@ -261,7 +261,8 @@
     "bright": pltpu.VMEM((2, HALF, SIDE), F32),
     "right": pltpu.VMEM((4, 2 * SIDE, SIDE), BF16),
     "left": pltpu.VMEM((4, SIDE, 2 * SIDE), BF16),
-    "sems": pltpu.SemaphoreType.DMA((2,)),
+    "needed": pltpu.VMEM((4, 2 * GROUPS, TILE, HALF), F32),
+    "sems": pltpu.SemaphoreType.DMA((3,)),
 }
 
 
@@ -338,17 +339,21 @@
 ):
     work = dict(zip(WORK, scratch))
     sgrad, pgrad, weight = work["sgrad"], work["pgrad"], work["weight"]
+    needed, sem = work["needed"], work["sems"].at[2]
+    for r in range(4):
+        for c in range(2 * GROUPS):
+            pltpu.make_async_copy(tiles.at[slot_of(info, perm, r, c)], needed.at[r, c], sem).start()
     copies = start_tables(right_in, left_in, work)
+    peak[0, 0] = probe_strength(probe, work["strength"])
+    pltpu.make_async_copy(needed, needed, sem).wait()
     for r in range(4):
         for g in range(GROUPS):
-            a, b = slot_of(info, perm, r, 2 * g), slot_of(info, perm, r, 2 * g + 1)
             for c in range(2):
-                one = tiles[a, pl.ds(c, 32, stride=2), :]
-                two = tiles[b, pl.ds(c, 32, stride=2), :]
+                one = needed[r, 2 * g, pl.ds(c, 32, stride=2), :]
+                two = needed[r, 2 * g + 1, pl.ds(c, 32, stride=2), :]
                 top, low = swap_halves(one, two)
                 strip[c, g, 64 * r : 64 * r + 32, :] = top
                 strip[c, g, 64 * r + 32 : 64 * r + 64, :] = low
-    peak[0, 0] = probe_strength(probe, work["strength"])
     for copy in copies:
         copy.wait()
     gradients(strip, probe, amp, work["right"], work["left"], work, False)
@@ -365,13 +370,19 @@
 
 
 def second_kernel(
-    info, perm, peak, energy, old_strip, first_send, total, other, old_probe, amp, right_in, left_in,
-    moved, kept_out, given_out, out_tiles, kept, given, out_sems, strip, probe, *scratch
+    info, perm, peak, energy, old_strip, first_in, total_in, other_in, old_probe, amp, right_in, left_in,
+    moved, kept_out, given_out, kept, given, out_sems, strip, probe, first_send, total, other, in_sems, *scratch
 ):
     work = dict(zip(WORK, scratch))
-    sgrad, pgrad, weight = work["sgrad"], work["pgrad"], work["weight"]
+    sgrad, pgrad, weight, out_tiles = work["sgrad"], work["pgrad"], work["weight"], work["needed"]
+    pairs = ((old_strip, strip), (total_in, total), (old_probe, probe), (other_in, other), (first_in, first_send))
+    come = [pltpu.make_async_copy(a, b, in_sems.at[i]) for i, (a, b) in enumerate(pairs)]
+    for copy in come:
+        copy.start()
     copies = start_tables(right_in, left_in, work)
     inverse = 1.0 / peak[0, 0]
+    come[0].wait()
+    come[1].wait()
     for r in range(4):
         for h in range(2):
             for block in range(4):
@@ -380,22 +391,18 @@
                 for c in range(2):
                     for g in range(GROUPS):
                         line = (c * GROUPS + g) * 8
-                        strip[c, g, start : start + 8, :] = (
-                            old_strip[c, g, start : start + 8, :] - total[at, line : line + 8, :] * inverse
-                        )
+                        strip[c, g, start : start + 8, :] -= total[at, line : line + 8, :] * inverse
     mine = info[2]
+    come[2].wait()
+    come[3].wait()
     for k in range(MODES):
         for c in range(2):
             for u in range(2):
                 for part in range(2):
                     piece = ((k * 2 + c) * 2 + u) * 2 + part
                     rows = slice(part * 64, part * 64 + 64)
-                    probe[k, mine, c, u, rows, :] = (
-                        old_probe[k, mine, c, u, rows, :] - total[piece, OBJ_ROWS:, :] * PROBE_STEP
-                    )
-                    probe[k, 1 - mine, c, u, rows, :] = (
-                        old_probe[k, 1 - mine, c, u, rows, :] - other[piece] * PROBE_STEP
-                    )
+                    probe[k, mine, c, u, rows, :] -= total[piece, OBJ_ROWS:, :] * PROBE_STEP
+                    probe[k, 1 - mine, c, u, rows, :] -= other[piece] * PROBE_STEP
     inverse_now = 1.0 / probe_strength(probe, work["strength"])
     weak = weak_data(strip, work["strength"], energy)
     for copy in copies:
@@ -416,6 +423,7 @@
     ]
     for copy in out_copies:
         copy.start()
+    come[4].wait()
     for r in range(4):
         for g in range(GROUPS):
             a, b = slot_of(info, perm, r, 2 * g), slot_of(info, perm, r, 2 * g + 1)
@@ -442,9 +450,12 @@
     return (spots[t, 0] >> 6) & (BAND_ROWS - 1), spots[t, 1] >> 6
 
 
-def served_slot(spots, info, t, k):
+def own_class(info, perm):
+    return lax.fori_loop(0, N_SCAN, lambda i, found: jnp.where(perm[i] == info[3], i, found), 0)
+
+
+def served_slot(spots, cls, t, k):
     row, col = spot_of(spots, t)
-    cls = info[4]
     r = ((cls >> 2) - row) & 7
     c = (((cls & 3) - col) & 3) + 4 * k
     valid = jnp.logical_and(r < 4, c < 2 * GROUPS)
@@ -452,10 +463,12 @@
     return valid, jnp.where(valid, slot, 0)
 
 
-def pack_kernel(spots, info, tiles, out, sem):
+def pack_kernel(spots, info, perm, tiles, out, sem):
+    cls = own_class(info, perm)
+
     def one(t, carry):
         for k in range(3):
-            valid, slot = served_slot(spots, info, t, k)
+            _, slot = served_slot(spots, cls, t, k)
             pltpu.make_async_copy(tiles.at[slot], out.at[t * 3 + k], sem).start()
         return carry
 
@@ -463,20 +476,35 @@
     pltpu.make_async_copy(out, out, sem).wait()
 
 
-def unpack_kernel(spots, info, tiles, arrived, out):
-    out[...] = tiles[...]
+PARTS = 4
+
+
+def unpack_kernel(spots, info, perm, tiles, arrived, out, total, came, sems):
+    cls = own_class(info, perm)
+    step = N_SCAN // PARTS
+    held = total.at[pl.ds(0, TILE)]
+    pltpu.make_async_copy(tiles, held, sems.at[PARTS]).start()
+    parts = []
+    for part in range(PARTS):
+        rows = pl.ds(part * step * 3, step * 3)
+        parts.append(pltpu.make_async_copy(arrived.at[rows], came.at[rows], sems.at[part]))
+        parts[-1].start()
+    pltpu.make_async_copy(tiles, held, sems.at[PARTS]).wait()
+    total[TILE] = jnp.zeros((TILE, HALF), F32)
 
     def one(t, carry):
         for k in range(3):
-            valid, slot = served_slot(spots, info, t, k)
-
-            @pl.when(valid)
-            def _():
-                out[slot] -= arrived[t * 3 + k]
-
+            valid, slot = served_slot(spots, cls, t, k)
+            at = jnp.where(valid, slot, TILE)
+            total[at] -= came[t * 3 + k]
         return carry
 
-    lax.fori_loop(0, N_SCAN, one, 0)
+    for part in range(PARTS):
+        parts[part].wait()
+        lax.fori_loop(part * step, (part + 1) * step, one, 0)
+    last = pltpu.make_async_copy(held, out, sems.at[PARTS])
+    last.start()
+    last.wait()
 
 
 def owner_kernel(spots, info, arrived, out, band):
@@ -632,19 +660,18 @@
 
     spots = exchange(jnp.broadcast_to(positions[:1, None], (N_SCAN, 1, 2))).reshape(N_SCAN, 2)
     perm = lax.dynamic_index_in_dim(owner_perm, band, 0, keepdims=False)
-    cls = jnp.sum(jnp.where(perm == me, jnp.arange(N_SCAN, dtype=jnp.int32), 0))
     spot = positions[0] // TILE
-    info = jnp.stack([spot[0] % BAND_ROWS, spot[1], core, me, cls, band, y_at]).astype(jnp.int32)
+    info = jnp.stack([spot[0] % BAND_ROWS, spot[1], core, me, me, band, y_at]).astype(jnp.int32)
 
     tiles = object_tiles.reshape(TILE, 2, 32, HALF).transpose(0, 2, 1, 3).reshape(TILE, TILE, HALF)
     packed = kernel(
         pack_kernel,
         shaped(96, TILE, HALF),
-        [SMEM, SMEM, HBM],
+        [SMEM, SMEM, SMEM, HBM],
         [pltpu.SemaphoreType.DMA],
         out_specs=HBM,
         name="pack",
-    )(spots, info, tiles)
+    )(spots, info, perm, tiles)
     arrived = exchange(packed)
 
     own = probe.reshape(2, 2, 2, 32, 2, 2, HALF).transpose(1, 0, 5, 2, 4, 3, 6).reshape(2, 2, 2, HALF, HALF)
@@ -669,7 +696,7 @@
             shaped(MODES, 2, 2, HALF, HALF),
             shaped(1, 1),
         ),
-        [SMEM, SMEM] + [VMEM] * 3 + [HBM] * 2,
+        [SMEM, SMEM, HBM, VMEM, VMEM, HBM, HBM],
         scratch,
         out_specs=(VMEM, VMEM, VMEM, VMEM, SMEM),
         name="first",
@@ -701,19 +728,22 @@
     moved, kept, given = kernel(
         second_kernel,
         (shaped(96, TILE, HALF), shaped(MODES, 2, 2, HALF, HALF), shaped(MODES, 2, 2, HALF, HALF)),
-        [SMEM, SMEM, SMEM, SMEM] + [VMEM] * 6 + [HBM] * 2,
+        [SMEM, SMEM, SMEM, SMEM] + [HBM] * 5 + [VMEM] + [HBM] * 2,
         [
-            pltpu.VMEM((4, 2 * GROUPS, TILE, HALF), F32),
             pltpu.VMEM((MODES, 2, 2, HALF, HALF), F32),
             pltpu.VMEM((MODES, 2, 2, HALF, HALF), F32),
             pltpu.SemaphoreType.DMA((3,)),
             pltpu.VMEM((2, GROUPS, SIDE, HALF), F32),
             pltpu.VMEM((MODES, 2, 2, 2, HALF, HALF), F32),
+            pltpu.VMEM((N_SCAN, SEND_ROWS, HALF), F32),
+            pltpu.VMEM((N_SCAN, SEND_ROWS, HALF), F32),
+            pltpu.VMEM((N_SCAN, PRB_ROWS, HALF), F32),
+            pltpu.SemaphoreType.DMA((5,)),
         ]
         + scratch,
         out_specs=(HBM, HBM, HBM),
         name="second",
-        limit=47,
+        limit=48,
     )(info, perm, peak, energy, strip, send, total, other, modes, amp, right, left)
     returned = exchange(moved)
 
@@ -725,12 +755,20 @@
     object_new = kernel(
         unpack_kernel,
         shaped(TILE, TILE, HALF),
-        [SMEM, SMEM, VMEM, VMEM],
+        [SMEM, SMEM, SMEM, HBM, HBM],
+        [
+            pltpu.VMEM((TILE + 1, TILE, HALF), F32),
+            pltpu.VMEM((96, TILE, HALF), F32),
+            pltpu.SemaphoreType.DMA((PARTS + 1,)),
+        ],
+        out_specs=HBM,
         name="unpack",
+        limit=58,
         cost=8 * 1024 * 1024,
-    )(spots, info, tiles, returned)
-    mine, object_new = lax.optimization_barrier((mine, object_new))
-    half = jnp.stack([mine] + [lax.ppermute(mine, "scan", shift_y(k)) for k in (1, 2, 3)])
+    )(spots, info, perm, tiles, returned)
+    turns = [lax.ppermute(mine, "scan", shift_y(k)) for k in (1, 2, 3)]
+    turns, object_new = lax.optimization_barrier((turns, object_new))
+    half = jnp.stack([mine] + turns)
     other_half = lax.ppermute(half, "scan", SWAP)
 
     half_one = total[:, OBJ_ROWS:].reshape(MODES, 2, 2, HALF, HALF)

time: 272 us -> 264 us (0.971)
  local copies, waits for them, and re-layouts: 16.5 us -> 13.5 us
  other arithmetic: 5.67 us -> 2.91 us
    unnamed x44, local copies, waits for them, and re-layouts: 8.66 us -> 5.13 us
    ppermute x3, waiting for transfers between devices: 3.22 us -> 0.01 us  [body(): turns = [lax.ppermute(mine, 'scan', shift_y(k)) for k in (1, 2, 3)]]
  transfers between devices with their start and end apart: 26 -> 26, of which waited for: 20 -> 17; matrix products, arithmetic and copies ran while one was open for 4% -> 4% of each run, Pallas kernels for 1% -> 3%
where the time goes in v3:
time: 264 us
  waiting for transfers between devices  73.6 us (28%)
  blocking collectives  70.3 us (27%)
  Pallas kernels  50.6 us (19%)
  starting transfers between devices  49.6 us (19%)
  local copies, waits for them, and re-layouts  13.5 us (5%)
  between operations  3.01 us (1%)
  other arithmetic  2.91 us (1%)
    all_to_all x2, blocking collectives, exchange(): return lax.all_to_all(x, 'scan', split_axis=0, concat_axis=0, tiled=True)  70.3 us
    ppermute x6, waiting for transfers between devices, sum_turned(): lax.ppermute(parts[k], axis, perm_of(k))  30.5 us
    pallas_call x1, Pallas kernels, body(): kernel(first_kernel, (shaped(2, GROUPS, SIDE, HALF), shaped(N_SCAN, SEND_...  21.5 us
    all_to_all x3, starting transfers between devices, exchange(): return lax.all_to_all(x, 'scan', split_axis=0, concat_axis=0, tiled=True)  19.5 us
    all_to_all x3, waiting for transfers between devices, exchange(): return lax.all_to_all(x, 'scan', split_axis=0, concat_axis=0, tiled=True)  18.4 us
    pallas_call x1, Pallas kernels, body(): kernel(second_kernel, (shaped(96, TILE, HALF), shaped(MODES, 2, 2, HALF,...  16.3 us
    ppermute x3, waiting for transfers between devices, gather_rows(): got = lax.ppermute(x, axis, perm_of(k))  9.74 us
    ppermute x6, starting transfers between devices, sum_all(): near, far, middle = (lax.ppermute(x, axis, perm_of(k)) for k in (1, 3, 2))  8.63 us
  transfers between devices with their start and end apart: 26, of which 17 were waited for; matrix products, arithmetic and copies ran while one was open for 4% of the time, Pallas kernels for 3%

profile of v3, /device:TPU:1, one launch (start us, length us, event | category | flops | bytes accessed | tf_op | source)
XLA Modules:
  0.0 263.6 jit_solution(8350794848663115648)
XLA Ops:
  0.6 0.8 slice_reduce_fusion
  1.4 0.6 broadcast_in_dim.26
  2.1 9.6 %all-to-all-start = ((s32[32,1,2]{2,1,0:T(1,128)}), s32[32,1,2]{2,1,0:T(1,128)S(1)}, u32[]{:S(2)}, u32[]{:S(2)}) async-start(s32[32,1,2]{2,1,0:T(1,128)} %broadcast_in_dim.26), calls=%async_computation | async-start | bytes 32768 | tf_op jit(solution)/shard_map/all_to_all | solution.py:624
  11.7 0.6 fusion.6
  14.2 0.7 stack.63.info
  14.9 3.6 %all-to-all-done = s32[32,1,2]{2,1,0:T(1,128)S(1)} async-done(((s32[32,1,2]{2,1,0:T(1,128)}), s32[32,1,2]{2,1,0:T(1,128)S(1)}, u32[]{:S(2)}, u32[]{:S(2)}) %all-to-all-start) | async-done | bytes 288 | tf_op jit(solution)/shard_map/all_to_all | solution.py:624
  18.5 1.6 copy-done.3
  20.1 2.9 %pack.1 = f32[96,64,128]{2,1,0:T(8,128)} custom-call(s32[32,2]{1,0:T(8,128)S(1)} %bitcast.65, s32[7]{0:T(128)S(1)} %stack.63.info, s32[32]{0:T(128)S(1)} %fusion.5.perm, f32[64,64,128]{2,1,0:T(8,128)S(1)} %bitcast.63), custom_call_target="tpu_custom_call" | custom-call | tf_op jit(solution)/shard_map/pack/pallas_call | solution.py:667
  23.0 5.2 %all-to-all-start.1 = ((f32[96,64,128]{2,1,0:T(8,128)}), f32[96,64,128]{2,1,0:T(8,128)}, u32[]{:S(2)}, u32[]{:S(2)}) async-start(f32[96,64,128]{2,1,0:T(8,128)} %pack.1), calls=%async_computation.1 | async-start | bytes 6291456 | tf_op jit(solution)/shard_map/all_to_all | solution.py:624
  28.3 0.3 reshape.66
  28.6 1.1 broadcast_in_dim.27
  29.7 0.7 dynamic-slice_bitcast_fusion
  30.5 1.2 collective-permute-start
  31.7 1.5 collective-permute-start.1
  33.1 1.5 collective-permute-start.2
  34.7 4.6 %collective-permute-done = f32[2,2,128,128]{3,2,1,0:T(8,128)S(1)} collective-permute-done((f32[2,2,128,128]{3,2,1,0:T(8,128)S(1)}, f32[2,2,128,128]{3,2,1,0:T(8,128)S(1)}, u32[]{:S(2)}, u32[]{:S(2)}) %collective-permute-start) | collective-permute-done | bytes 262176 | tf_op jit(solution)/shard_map/ppermute | solution.py:641
  39.2 0.7 bitcast_dynamic-update-slice_fusion.2
  40.0 0.7 bitcast_dynamic-update-slice_fusion.1
  40.7 5.2 %collective-permute-done.2 = f32[2,2,128,128]{3,2,1,0:T(8,128)S(1)} collective-permute-done((f32[2,2,128,128]{3,2,1,0:T(8,128)S(1)}, f32[2,2,128,128]{3,2,1,0:T(8,128)S(1)}, u32[]{:S(2)}, u32[]{:S(2)}) %collective-permute-start.2) | collective-permute-done | bytes 262176 | tf_op jit(solution)/shard_map/ppermute | solution.py:641
  45.8 0.7 bitcast_dynamic-update-slice_fusion
  46.6 1.1 collective-permute-start.3
  47.7 1.2 spread.1
  48.9 1.0 copy-done.7
  49.9 0.4 collective-permute-done.3
  50.3 2.4 maximum_select_fusion.probe.old_probe
  52.8 14.8 %all-to-all-done.1.tiles = f32[96,64,128]{2,1,0:T(8,128)} async-done(((f32[96,64,128]{2,1,0:T(8,128)}), f32[96,64,128]{2,1,0:T(8,128)}, u32[]{:S(2)}, u32[]{:S(2)}) %all-to-all-start.1) | async-done | bytes 3145760 | tf_op jit(solution)/shard_map/all_to_all | solution.py:624
  67.6 1.2 copy-done.5
  68.8 1.2 copy-done.8
  70.0 21.5 %first.1 = (f32[2,5,256,128]{3,2,1,0:T(8,128)S(1)}, f32[32,144,128]{2,1,0:T(8,128)S(1)}, f32[4,2,2,128,128]{4,3,2,1,0:T(8,128)S(1)}, f32[4,2,2,128,128]{4,3,2,1,0:T(8,128)S(1)}, f32[1,1]{1,0:T(1,128)}) custom-call(s32[7]{0:T(128)S(1)} %stack.63.info, s32[32]{0:T(128)S(1)} %fusion.5.perm, f32[96,64,128]{2,1,0:T(8,128)} %all-to-all-done.1.tiles, ...), custom_call_target="tpu_custom_call" | custom-call | tf_op jit(solution)/shard_map/first/pallas_call | solution.py:690
  91.5 2.9 %collective-permute-start.4 = (f32[4,2,2,128,128]{4,3,2,1,0:T(8,128)S(1)}, f32[4,2,2,128,128]{4,3,2,1,0:T(8,128)S(1)}, u32[]{:S(2)}, u32[]{:S(2)}) collective-permute-start(f32[4,2,2,128,128]{4,3,2,1,0:T(8,128)S(1)} %get-tuple-element.22), channel_id=1, source_target_pairs={{0,1},{1,0},{2,3},{3,2},{4,5},{5,4},{6,7},{7,6},{8,9},{9,8},{10,11... | collective-permute-start | bytes 3145736 | tf_op jit(solution)/shard_map/ppermute | solution.py:706
  94.5 2.3 collective-permute-done.4
  96.8 0.1 add.120
  97.0 34.6 %all_to_all.25.arrived = f32[32,144,128]{2,1,0:T(8,128)S(1)} all-to-all(f32[32,144,128]{2,1,0:T(8,128)S(1)} %constant_dynamic-update-slice_fusion.1.first_in), channel_id=1, replica_groups=mesh['grp'=4,'scan'=32] {'scan'}, dimensions={0} | all-to-all | bytes 4718592 | tf_op jit(solution)/shard_map/all_to_all | solution.py:624
  131.6 0.1 sums.1
  131.7 2.5 collective-permute-start.7
  134.3 1.7 collective-permute-start.5
  136.0 1.7 owner.1
  137.8 2.6 %collective-permute-done.6 = f32[2,64,128]{2,1,0:T(8,128)S(1)} collective-permute-done((f32[2,64,128]{2,1,0:T(8,128)S(1)}, f32[2,64,128]{2,1,0:T(8,128)S(1)}, u32[]{:S(2)}, u32[]{:S(2)}) %collective-permute-start.6) | collective-permute-done | bytes 65568 | tf_op jit(solution)/shard_map/ppermute | solution.py:633
  140.7 35.7 %all_to_all.26.total_in = f32[32,144,128]{2,1,0:T(8,128)S(1)} all-to-all(f32[32,144,128]{2,1,0:T(8,128)S(1)} %constant_dynamic-update-slice_fusion), channel_id=1, replica_groups=mesh['grp'=4,'scan'=32] {'scan'}, dimensions={0} | all-to-all | bytes 4718592 | tf_op jit(solution)/shard_map/all_to_all | solution.py:624
  176.5 0.3 collective-permute-start.8
  176.8 2.5 collective-permute-done.8.other_in
  179.3 16.3 %second.1 = (f32[96,64,128]{2,1,0:T(8,128)}, f32[4,2,2,128,128]{4,3,2,1,0:T(8,128)S(1)}, f32[4,2,2,128,128]{4,3,2,1,0:T(8,128)S(1)}) custom-call(s32[7]{0:T(128)S(1)} %stack.63.info, s32[32]{0:T(128)S(1)} %fusion.5.perm, f32[1,1]{1,0:T(1,128)} %get-tuple-element.17.peak, f32[1,4]{1,0:T(1,128)S(1)} %get-tuple-element.18.energy, ...), custom_call_target="tpu_custom_call" | custom-call | tf_op jit(solution)/shard_map/second/pallas_call | solution.py:728
  195.6 4.6 %all-to-all-start.4 = ((f32[96,64,128]{2,1,0:T(8,128)}), f32[96,64,128]{2,1,0:T(8,128)}, u32[]{:S(2)}, u32[]{:S(2)}) async-start(f32[96,64,128]{2,1,0:T(8,128)} %get-tuple-element.25), calls=%async_computation.4 | async-start | bytes 6291456 | tf_op jit(solution)/shard_map/all_to_all | solution.py:624
  200.2 0.5 collective-permute-start.9
  200.7 2.3 collective-permute-done.9
  203.0 0.1 slice_add_fusion
  203.2 2.7 %collective-permute-start.12 = (f32[4,128,128]{2,1,0:T(8,128)S(1)}, f32[4,128,128]{2,1,0:T(8,128)S(1)}, u32[]{:S(2)}, u32[]{:S(2)}) collective-permute-start(f32[4,128,128]{2,1,0:T(8,128)S(1)} %bitcast.74), channel_id=1, source_target_pairs={{0,96},{32,0},{64,32},{96,64},{1,97},{33,1},{65,33},{97,65},{2,98}... | collective-permute-start | bytes 786440 | tf_op jit(solution)/shard_map/ppermute | solution.py:628
  205.9 0.7 collective-permute-start.10
  206.6 5.5 %collective-permute-done.11 = f32[4,128,128]{2,1,0:T(8,128)S(1)} collective-permute-done((f32[4,128,128]{2,1,0:T(8,128)S(1)}, f32[4,128,128]{2,1,0:T(8,128)S(1)}, u32[]{:S(2)}, u32[]{:S(2)}) %collective-permute-start.11) | collective-permute-done | bytes 262176 | tf_op jit(solution)/shard_map/ppermute | solution.py:628
  212.0 6.3 %collective-permute-done.10 = f32[4,128,128]{2,1,0:T(8,128)S(1)} collective-permute-done((f32[4,128,128]{2,1,0:T(8,128)S(1)}, f32[4,128,128]{2,1,0:T(8,128)S(1)}, u32[]{:S(2)}, u32[]{:S(2)}) %collective-permute-start.10) | collective-permute-done | bytes 262176 | tf_op jit(solution)/shard_map/ppermute | solution.py:628
  218.4 2.9 %collective-permute-start.15 = (f32[128,128]{1,0:T(8,128)S(1)}, f32[128,128]{1,0:T(8,128)S(1)}, u32[]{:S(2)}, u32[]{:S(2)}) collective-permute-start(f32[128,128]{1,0:T(8,128)S(1)} %get-tuple-element.36), channel_id=1, source_target_pairs={{0,6},{1,7},{2,0},{3,1},{4,2},{5,3},{6,4},{7,5},{8,14},{9,15},{10,... | collective-permute-start | bytes 196616 | tf_op jit(solution)/shard_map/ppermute | solution.py:628
  221.3 1.7 collective-permute-start.13
  223.1 14.8 %collective-permute-done.15 = f32[128,128]{1,0:T(8,128)S(1)} collective-permute-done((f32[128,128]{1,0:T(8,128)S(1)}, f32[128,128]{1,0:T(8,128)S(1)}, u32[]{:S(2)}, u32[]{:S(2)}) %collective-permute-start.15) | collective-permute-done | bytes 65568 | tf_op jit(solution)/shard_map/ppermute | solution.py:628
  237.8 1.1 collective-permute-done.14
  238.9 2.9 %collective-permute-done.13 = f32[128,128]{1,0:T(8,128)S(1)} collective-permute-done((f32[128,128]{1,0:T(8,128)S(1)}, f32[128,128]{1,0:T(8,128)S(1)}, u32[]{:S(2)}, u32[]{:S(2)}) %collective-permute-start.13) | collective-permute-done | bytes 65568 | tf_op jit(solution)/shard_map/ppermute | solution.py:628
  241.8 3.1 %collective-permute-start.18 = (f32[128,128]{1,0:T(8,128)S(1)}, f32[128,128]{1,0:T(8,128)S(1)}, u32[]{:S(2)}, u32[]{:S(2)}) collective-permute-start(f32[128,128]{1,0:T(8,128)S(1)} %fusion.4), channel_id=1, source_target_pairs={{0,24},{1,25},{2,26},{3,27},{4,28},{5,29},{6,30},{7,31},{8,0},{9,1... | collective-permute-start | bytes 196616 | tf_op jit(solution)/shard_map/ppermute | solution.py:633
  244.9 1.3 collective-permute-start.16
  246.3 3.7 %collective-permute-done.17 = f32[128,128]{1,0:T(8,128)S(1)} collective-permute-done((f32[128,128]{1,0:T(8,128)S(1)}, f32[128,128]{1,0:T(8,128)S(1)}, u32[]{:S(2)}, u32[]{:S(2)}) %collective-permute-start.17) | collective-permute-done | bytes 65568 | tf_op jit(solution)/shard_map/ppermute | solution.py:633
  250.1 1.4 collective-permute-start.20
  251.5 1.0 constant_dynamic-slice_fusion.1
  252.5 5.4 %unpack.1 = f32[64,64,128]{2,1,0:T(8,128)} custom-call(s32[32,2]{1,0:T(8,128)} %bitcast.67, s32[7]{0:T(128)} %copy-done.14, s32[32]{0:T(128)} %copy-done.16, f32[64,64,128]{2,1,0:T(8,128)} %bitcast.62, f32[96,64,128]{2,1,0:T(8,128)} %all-to-all-done.4.arrived), custom_call_target="tpu_custom_call" | custom-call | bytes 8388608 | tf_op jit(solution)/shard_map/unpack/pallas_call | solution.py:755
  258.0 2.9 %collective-permute-start.22 = (f32[4,128,128]{2,1,0:T(8,128)S(1)}, f32[4,128,128]{2,1,0:T(8,128)S(1)}, u32[]{:S(2)}, u32[]{:S(2)}) collective-permute-start(f32[4,128,128]{2,1,0:T(8,128)S(1)} %pad_maximum_fusion.half), channel_id=1, source_target_pairs={{0,1},{1,0},{2,3},{3,2},{4,5},{5,4},{6,7},{7,6},{8,9},{9,8},{10,11... | collective-permute-start | bytes 786440 | tf_op jit(solution)/shard_map/ppermute | solution.py:772
  261.1 1.1 collective-permute-done.22.other_half
  262.1 1.4 finish.1
  (71 shorter events, 1.1 us)
Async XLA Ops:
  0.6 13.5 %copy-start = (s32[4,32]{1,0:T(4,128)S(1)}, s32[4,32]{1,0:T(4,128)}, u32[]{:S(2)}) copy-start(s32[4,32]{1,0:T(4,128)} %param.10) | copy-start | bytes 1540
  2.1 16.5 %all-to-all-start = ((s32[32,1,2]{2,1,0:T(1,128)}), s32[32,1,2]{2,1,0:T(1,128)S(1)}, u32[]{:S(2)}, u32[]{:S(2)}) async-start(s32[32,1,2]{2,1,0:T(1,128)} %broadcast_in_dim.26), calls=%async_computation | async-start | bytes 32768 | tf_op jit(solution)/shard_map/all_to_all | solution.py:624
  14.2 165.1 %copy-start.16 = (s32[32]{0:T(128)}, s32[32]{0:T(128)S(1)}, u32[]{:S(2)}) copy-start(s32[32]{0:T(128)S(1)} %fusion.5.perm) | copy-start | bytes 388
  14.9 164.3 %copy-start.14 = (s32[7]{0:T(128)}, s32[7]{0:T(128)S(1)}, u32[]{:S(2)}) copy-start(s32[7]{0:T(128)S(1)} %stack.63.info) | copy-start | bytes 88
  18.5 117.5 %copy-start.12 = (s32[32,1,2]{2,1,0:T(1,128)}, s32[32,1,2]{2,1,0:T(1,128)S(1)}, u32[]{:S(2)}) copy-start(s32[32,1,2]{2,1,0:T(1,128)S(1)} %all-to-all-done) | copy-start | bytes 772
  18.5 1.6 copy-start.3
  23.0 5.2 %copy-start.21 = (f32[1,2,256,256]{3,2,1,0:T(8,128)S(1)}, f32[1,2,256,256]{3,2,1,0:T(8,128)}, u32[]{:S(2)}) copy-start(f32[1,2,256,256]{3,2,1,0:T(8,128)} %param.12) | copy-start | bytes 1572868
  23.0 44.5 %all-to-all-start.1 = ((f32[96,64,128]{2,1,0:T(8,128)}), f32[96,64,128]{2,1,0:T(8,128)}, u32[]{:S(2)}, u32[]{:S(2)}) async-start(f32[96,64,128]{2,1,0:T(8,128)} %pack.1), calls=%async_computation.1 | async-start | bytes 6291456 | tf_op jit(solution)/shard_map/all_to_all | solution.py:624
  28.5 19.2 %copy-start.11 = (f32[4,256,256]{2,1,0:T(8,128)S(1)}, f32[4,256,256]{2,1,0:T(8,128)}, u32[]{:S(2)}) copy-start(f32[4,256,256]{2,1,0:T(8,128)} %amp.1) | copy-start | bytes 3145732
  28.5 19.2 %copy-start.13 = (bf16[256,256]{1,0:T(8,128)(2,1)S(1)}, bf16[256,256]{1,0:T(8,128)(2,1)}, u32[]{:S(2)}) copy-start(bf16[256,256]{1,0:T(8,128)(2,1)} %constant.124.clone.shuffle) | copy-start | bytes 393220
  28.6 21.7 %copy-start.18 = (f32[2,2,2,32,2,2,128]{6,3,4,2,5,0,1:T(8,128)}, f32[2,2,2,32,2,2,128]{6,3,4,2,5,0,1:T(8,128)S(1)}, u32[]{:S(2)}) copy-start(f32[2,2,2,32,2,2,128]{6,3,4,2,5,0,1:T(8,128)S(1)} %copy.19) | copy-start | bytes 1572868
  30.5 8.8 %collective-permute-start = (f32[2,2,128,128]{3,2,1,0:T(8,128)S(1)}, f32[2,2,128,128]{3,2,1,0:T(8,128)S(1)}, u32[]{:S(2)}, u32[]{:S(2)}) collective-permute-start(f32[2,2,128,128]{3,2,1,0:T(8,128)S(1)} %get-tuple-element.34), channel_id=1, source_target_pairs={{0,32},{32,64},{64,96},{96,0},{1,33},{33,65},{65,97},{97,1},{2,34}... | collective-permute-start | bytes 786440 | tf_op jit(solution)/shard_map/ppermute | solution.py:641
  31.7 8.3 %collective-permute-start.1 = (f32[2,2,128,128]{3,2,1,0:T(8,128)S(1)}, f32[2,2,128,128]{3,2,1,0:T(8,128)S(1)}, u32[]{:S(2)}, u32[]{:S(2)}) collective-permute-start(f32[2,2,128,128]{3,2,1,0:T(8,128)S(1)} %get-tuple-element.34), channel_id=1, source_target_pairs={{0,96},{32,0},{64,32},{96,64},{1,97},{33,1},{65,33},{97,65},{2,98}... | collective-permute-start | bytes 786440 | tf_op jit(solution)/shard_map/ppermute | solution.py:641
  33.1 12.7 %collective-permute-start.2 = (f32[2,2,128,128]{3,2,1,0:T(8,128)S(1)}, f32[2,2,128,128]{3,2,1,0:T(8,128)S(1)}, u32[]{:S(2)}, u32[]{:S(2)}) collective-permute-start(f32[2,2,128,128]{3,2,1,0:T(8,128)S(1)} %get-tuple-element.34), channel_id=1, source_target_pairs={{0,64},{32,96},{64,0},{96,32},{1,65},{33,97},{65,1},{97,33},{2,66}... | collective-permute-start | bytes 786440 | tf_op jit(solution)/shard_map/ppermute | solution.py:641
  46.6 3.8 %collective-permute-start.3 = (f32[4,2,2,128,128]{4,3,2,1,0:T(8,128)}, f32[4,2,2,128,128]{4,3,2,1,0:T(8,128)}, u32[]{:S(2)}, u32[]{:S(2)}) collective-permute-start(f32[4,2,2,128,128]{4,3,2,1,0:T(8,128)} %bitcast_dynamic-update-slice_fusion), channel_id=1, source_target_pairs={{0,1},{1,0},{2,3},{3,2},{4,5},{5,4},{6,7},{7,6},{8,9},{9,8},{10,11... | collective-permute-start | bytes 3145736 | tf_op jit(solution)/shard_map/ppermute | solution.py:679
  48.9 1.0 copy-start.7
  49.9 17.6 %copy-start.4 = (bf16[4,256,512]{2,1,0:T(8,128)(2,1)S(1)}, bf16[4,256,512]{2,1,0:T(8,128)(2,1)}, u32[]{:S(2)}) copy-start(bf16[4,256,512]{2,1,0:T(8,128)(2,1)} %constant.123.clone.left_in) | copy-start | bytes 3145732
  52.8 38.8 %copy-start.1 = (f32[4,2,2,2,128,128]{5,4,3,2,1,0:T(8,128)}, f32[4,2,2,2,128,128]{5,4,3,2,1,0:T(8,128)S(1)}, u32[]{:S(2)}) copy-start(f32[4,2,2,2,128,128]{5,4,3,2,1,0:T(8,128)S(1)} %maximum_select_fusion.probe.old_probe) | copy-start | bytes 6291460
  67.6 1.2 copy-start.5
  68.8 1.2 copy-start.8
  91.5 5.5 %copy-start.10 = (f32[2,5,256,128]{3,2,1,0:T(8,128)}, f32[2,5,256,128]{3,2,1,0:T(8,128)S(1)}, u32[]{:S(2)}) copy-start(f32[2,5,256,128]{3,2,1,0:T(8,128)S(1)} %get-tuple-element.19.old_strip) | copy-start | bytes 3932164
  91.5 5.2 %collective-permute-start.4 = (f32[4,2,2,128,128]{4,3,2,1,0:T(8,128)S(1)}, f32[4,2,2,128,128]{4,3,2,1,0:T(8,128)S(1)}, u32[]{:S(2)}, u32[]{:S(2)}) collective-permute-start(f32[4,2,2,128,128]{4,3,2,1,0:T(8,128)S(1)} %get-tuple-element.22), channel_id=1, source_target_pairs={{0,1},{1,0},{2,3},{3,2},{4,5},{5,4},{6,7},{7,6},{8,9},{9,8},{10,11... | collective-permute-start | bytes 3145736 | tf_op jit(solution)/shard_map/ppermute | solution.py:706
  97.0 34.6 %copy-start.2 = (f32[32,144,128]{2,1,0:T(8,128)}, f32[32,144,128]{2,1,0:T(8,128)S(1)}, u32[]{:S(2)}) copy-start(f32[32,144,128]{2,1,0:T(8,128)S(1)} %constant_dynamic-update-slice_fusion.1.first_in) | copy-start | bytes 7077892
  131.7 6.0 %collective-permute-start.7 = (f32[2,64,128]{2,1,0:T(8,128)S(1)}, f32[2,64,128]{2,1,0:T(8,128)S(1)}, u32[]{:S(2)}, u32[]{:S(2)}) collective-permute-start(f32[2,64,128]{2,1,0:T(8,128)S(1)} %sums.1), channel_id=1, source_target_pairs={{0,96},{32,0},{64,32},{96,64},{1,97},{33,1},{65,33},{97,65},{2,98}... | collective-permute-start | bytes 196616 | tf_op jit(solution)/shard_map/ppermute | solution.py:633
  134.3 6.1 %collective-permute-start.6 = (f32[2,64,128]{2,1,0:T(8,128)S(1)}, f32[2,64,128]{2,1,0:T(8,128)S(1)}, u32[]{:S(2)}, u32[]{:S(2)}) collective-permute-start(f32[2,64,128]{2,1,0:T(8,128)S(1)} %sums.1), channel_id=1, source_target_pairs={{0,32},{32,64},{64,96},{96,0},{1,33},{33,65},{65,97},{97,1},{2,34}... | collective-permute-start | bytes 196616 | tf_op jit(solution)/shard_map/ppermute | solution.py:633
  134.3 6.1 %collective-permute-start.5 = (f32[2,64,128]{2,1,0:T(8,128)S(1)}, f32[2,64,128]{2,1,0:T(8,128)S(1)}, u32[]{:S(2)}, u32[]{:S(2)}) collective-permute-start(f32[2,64,128]{2,1,0:T(8,128)S(1)} %sums.1), channel_id=1, source_target_pairs={{0,64},{32,96},{64,0},{96,32},{1,65},{33,97},{65,1},{97,33},{2,66}... | collective-permute-start | bytes 196616 | tf_op jit(solution)/shard_map/ppermute | solution.py:633
  140.6 38.6 %copy-start.6 = (bf16[4,512,256]{2,1,0:T(8,128)(2,1)S(1)}, bf16[4,512,256]{2,1,0:T(8,128)(2,1)}, u32[]{:S(2)}) copy-start(bf16[4,512,256]{2,1,0:T(8,128)(2,1)} %constant.122.clone.right_in) | copy-start | bytes 3145732
  140.7 38.6 %copy-start.9 = (f32[4,2,128,256]{3,2,1,0:T(8,128)S(1)}, f32[4,2,128,256]{3,2,1,0:T(8,128)}, u32[]{:S(2)}) copy-start(f32[4,2,128,256]{3,2,1,0:T(8,128)} %copy-done.7) | copy-start | bytes 3145732
  176.4 2.9 %copy-start.17 = (f32[32,144,128]{2,1,0:T(8,128)}, f32[32,144,128]{2,1,0:T(8,128)S(1)}, u32[]{:S(2)}) copy-start(f32[32,144,128]{2,1,0:T(8,128)S(1)} %all_to_all.26.total_in) | copy-start | bytes 7077892
  176.5 2.8 %copy-start.20 = (f32[32,64,128]{2,1,0:T(8,128)}, f32[32,64,128]{2,1,0:T(8,128)S(1)}, u32[]{:S(2)}) copy-start(f32[32,64,128]{2,1,0:T(8,128)S(1)} %slice.74) | copy-start | bytes 3145732
  176.5 2.7 %collective-permute-start.8 = (f32[32,64,128]{2,1,0:T(8,128)S(1)}, f32[32,64,128]{2,1,0:T(8,128)S(1)}, u32[]{:S(2)}, u32[]{:S(2)}) collective-permute-start(f32[32,64,128]{2,1,0:T(8,128)S(1)} %slice.74), channel_id=1, source_target_pairs={{0,1},{1,0},{2,3},{3,2},{4,5},{5,4},{6,7},{7,6},{8,9},{9,8},{10,11... | collective-permute-start | bytes 3145736 | tf_op jit(solution)/shard_map/ppermute | solution.py:726
  195.6 56.9 %all-to-all-start.4 = ((f32[96,64,128]{2,1,0:T(8,128)}), f32[96,64,128]{2,1,0:T(8,128)}, u32[]{:S(2)}, u32[]{:S(2)}) async-start(f32[96,64,128]{2,1,0:T(8,128)} %get-tuple-element.25), calls=%async_computation.4 | async-start | bytes 6291456 | tf_op jit(solution)/shard_map/all_to_all | solution.py:624
  200.2 2.8 %collective-permute-start.9 = (f32[4,2,2,128,128]{4,3,2,1,0:T(8,128)S(1)}, f32[4,2,2,128,128]{4,3,2,1,0:T(8,128)S(1)}, u32[]{:S(2)}, u32[]{:S(2)}) collective-permute-start(f32[4,2,2,128,128]{4,3,2,1,0:T(8,128)S(1)} %get-tuple-element.24), channel_id=1, source_target_pairs={{0,1},{1,0},{2,3},{3,2},{4,5},{5,4},{6,7},{7,6},{8,9},{9,8},{10,11... | collective-permute-start | bytes 3145736 | tf_op jit(solution)/shard_map/ppermute | solution.py:750
  203.1 8.9 %collective-permute-start.11 = (f32[4,128,128]{2,1,0:T(8,128)S(1)}, f32[4,128,128]{2,1,0:T(8,128)S(1)}, u32[]{:S(2)}, u32[]{:S(2)}) collective-permute-start(f32[4,128,128]{2,1,0:T(8,128)S(1)} %bitcast.75), channel_id=1, source_target_pairs={{0,32},{32,64},{64,96},{96,0},{1,33},{33,65},{65,97},{97,1},{2,34}... | collective-permute-start | bytes 786440 | tf_op jit(solution)/shard_map/ppermute | solution.py:628
  203.2 8.8 %collective-permute-start.12 = (f32[4,128,128]{2,1,0:T(8,128)S(1)}, f32[4,128,128]{2,1,0:T(8,128)S(1)}, u32[]{:S(2)}, u32[]{:S(2)}) collective-permute-start(f32[4,128,128]{2,1,0:T(8,128)S(1)} %bitcast.74), channel_id=1, source_target_pairs={{0,96},{32,0},{64,32},{96,64},{1,97},{33,1},{65,33},{97,65},{2,98}... | collective-permute-start | bytes 786440 | tf_op jit(solution)/shard_map/ppermute | solution.py:628
  205.9 12.5 %collective-permute-start.10 = (f32[4,128,128]{2,1,0:T(8,128)S(1)}, f32[4,128,128]{2,1,0:T(8,128)S(1)}, u32[]{:S(2)}, u32[]{:S(2)}) collective-permute-start(f32[4,128,128]{2,1,0:T(8,128)S(1)} %bitcast.73), channel_id=1, source_target_pairs={{0,64},{32,96},{64,0},{96,32},{1,65},{33,97},{65,1},{97,33},{2,66}... | collective-permute-start | bytes 786440 | tf_op jit(solution)/shard_map/ppermute | solution.py:628
  218.4 19.4 %collective-permute-start.15 = (f32[128,128]{1,0:T(8,128)S(1)}, f32[128,128]{1,0:T(8,128)S(1)}, u32[]{:S(2)}, u32[]{:S(2)}) collective-permute-start(f32[128,128]{1,0:T(8,128)S(1)} %get-tuple-element.36), channel_id=1, source_target_pairs={{0,6},{1,7},{2,0},{3,1},{4,2},{5,3},{6,4},{7,5},{8,14},{9,15},{10,... | collective-permute-start | bytes 196616 | tf_op jit(solution)/shard_map/ppermute | solution.py:628
  221.3 17.6 %collective-permute-start.14 = (f32[128,128]{1,0:T(8,128)S(1)}, f32[128,128]{1,0:T(8,128)S(1)}, u32[]{:S(2)}, u32[]{:S(2)}) collective-permute-start(f32[128,128]{1,0:T(8,128)S(1)} %get-tuple-element.37), channel_id=1, source_target_pairs={{0,2},{1,3},{2,4},{3,5},{4,6},{5,7},{6,0},{7,1},{8,10},{9,11},{10,... | collective-permute-start | bytes 196616 | tf_op jit(solution)/shard_map/ppermute | solution.py:628
  221.3 20.5 %collective-permute-start.13 = (f32[128,128]{1,0:T(8,128)S(1)}, f32[128,128]{1,0:T(8,128)S(1)}, u32[]{:S(2)}, u32[]{:S(2)}) collective-permute-start(f32[128,128]{1,0:T(8,128)S(1)} %get-tuple-element.38), channel_id=1, source_target_pairs={{0,4},{1,5},{2,6},{3,7},{4,0},{5,1},{6,2},{7,3},{8,12},{9,13},{10,... | collective-permute-start | bytes 196616 | tf_op jit(solution)/shard_map/ppermute | solution.py:628
  241.8 4.4 %collective-permute-start.18 = (f32[128,128]{1,0:T(8,128)S(1)}, f32[128,128]{1,0:T(8,128)S(1)}, u32[]{:S(2)}, u32[]{:S(2)}) collective-permute-start(f32[128,128]{1,0:T(8,128)S(1)} %fusion.4), channel_id=1, source_target_pairs={{0,24},{1,25},{2,26},{3,27},{4,28},{5,29},{6,30},{7,31},{8,0},{9,1... | collective-permute-start | bytes 196616 | tf_op jit(solution)/shard_map/ppermute | solution.py:633
  244.9 5.0 %collective-permute-start.17 = (f32[128,128]{1,0:T(8,128)S(1)}, f32[128,128]{1,0:T(8,128)S(1)}, u32[]{:S(2)}, u32[]{:S(2)}) collective-permute-start(f32[128,128]{1,0:T(8,128)S(1)} %fusion.4), channel_id=1, source_target_pairs={{0,8},{1,9},{2,10},{3,11},{4,12},{5,13},{6,14},{7,15},{8,16},{9,17... | collective-permute-start | bytes 196616 | tf_op jit(solution)/shard_map/ppermute | solution.py:633
  244.9 5.0 %collective-permute-start.16 = (f32[128,128]{1,0:T(8,128)S(1)}, f32[128,128]{1,0:T(8,128)S(1)}, u32[]{:S(2)}, u32[]{:S(2)}) collective-permute-start(f32[128,128]{1,0:T(8,128)S(1)} %fusion.4), channel_id=1, source_target_pairs={{0,16},{1,17},{2,18},{3,19},{4,20},{5,21},{6,22},{7,23},{8,24},{9,... | collective-permute-start | bytes 196616 | tf_op jit(solution)/shard_map/ppermute | solution.py:633
  250.0 8.0 %collective-permute-start.21 = (f32[128,128]{1,0:T(8,128)S(1)}, f32[128,128]{1,0:T(8,128)S(1)}, u32[]{:S(2)}, u32[]{:S(2)}) collective-permute-start(f32[128,128]{1,0:T(8,128)S(1)} %add_add_fusion), channel_id=1, source_target_pairs={{0,6},{1,7},{2,0},{3,1},{4,2},{5,3},{6,4},{7,5},{8,14},{9,15},{10,... | collective-permute-start | bytes 196616 | tf_op jit(solution)/shard_map/ppermute | solution.py:769
  250.1 7.9 %collective-permute-start.20 = (f32[128,128]{1,0:T(8,128)S(1)}, f32[128,128]{1,0:T(8,128)S(1)}, u32[]{:S(2)}, u32[]{:S(2)}) collective-permute-start(f32[128,128]{1,0:T(8,128)S(1)} %add_add_fusion), channel_id=1, source_target_pairs={{0,4},{1,5},{2,6},{3,7},{4,0},{5,1},{6,2},{7,3},{8,12},{9,13},{10,... | collective-permute-start | bytes 196616 | tf_op jit(solution)/shard_map/ppermute | solution.py:769
  251.4 6.6 %collective-permute-start.19 = (f32[128,128]{1,0:T(8,128)S(1)}, f32[128,128]{1,0:T(8,128)S(1)}, u32[]{:S(2)}, u32[]{:S(2)}) collective-permute-start(f32[128,128]{1,0:T(8,128)S(1)} %add_add_fusion), channel_id=1, source_target_pairs={{0,2},{1,3},{2,4},{3,5},{4,6},{5,7},{6,0},{7,1},{8,10},{9,11},{10,... | collective-permute-start | bytes 196616 | tf_op jit(solution)/shard_map/ppermute | solution.py:769
  252.5 8.5 %copy-start.19 = (f32[2,2,2,32,2,2,128]{6,3,4,2,5,0,1:T(8,128)S(1)}, f32[2,2,2,32,2,2,128]{6,3,4,2,5,0,1:T(8,128)}, u32[]{:S(2)}) copy-start(f32[2,2,2,32,2,2,128]{6,3,4,2,5,0,1:T(8,128)} %copy-done.18) | copy-start | bytes 1572868
  258.0 4.2 %copy-start.15 = (s32[7]{0:T(128)S(1)}, s32[7]{0:T(128)}, u32[]{:S(2)}) copy-start(s32[7]{0:T(128)} %copy-done.14) | copy-start | bytes 88
  258.0 4.1 %collective-permute-start.22 = (f32[4,128,128]{2,1,0:T(8,128)S(1)}, f32[4,128,128]{2,1,0:T(8,128)S(1)}, u32[]{:S(2)}, u32[]{:S(2)}) collective-permute-start(f32[4,128,128]{2,1,0:T(8,128)S(1)} %pad_maximum_fusion.half), channel_id=1, source_target_pairs={{0,1},{1,0},{2,3},{3,2},{4,5},{5,4},{6,7},{7,6},{8,9},{9,8},{10,11... | collective-permute-start | bytes 786440 | tf_op jit(solution)/shard_map/ppermute | solution.py:772

commit v4 on v3

--- a/solution.py
+++ b/solution.py
@@ -105,10 +105,6 @@
 def gradients(strip, probe, amp, right, left, work, fast):
     sgrad, pgrad, weight, strength = work["sgrad"], work["pgrad"], work["weight"], work["strength"]
     lhs, rhs, far, mid, res, bright = (work[n] for n in ("lhs", "rhs", "far", "mid", "res", "bright"))
-    sgrad[...] = jnp.zeros_like(sgrad)
-    pgrad[...] = jnp.zeros_like(pgrad)
-    weight[...] = jnp.zeros_like(weight)
-
     def put_split(ref, at, rows, x):
         if fast:
             ref[at, 0, rows, :] = x.astype(BF16)
@@ -262,7 +258,7 @@
     "right": pltpu.VMEM((4, 2 * SIDE, SIDE), BF16),
     "left": pltpu.VMEM((4, SIDE, 2 * SIDE), BF16),
     "needed": pltpu.VMEM((4, 2 * GROUPS, TILE, HALF), F32),
-    "sems": pltpu.SemaphoreType.DMA((3,)),
+    "sems": pltpu.SemaphoreType.DMA((4,)),
 }
 
 
@@ -324,6 +320,11 @@
     return (((info[0] + r) & 3) << 3) + h * 4 + block
 
 
+def clear(work):
+    for name in ("sgrad", "pgrad", "weight"):
+        work[name][...] = jnp.zeros_like(work[name])
+
+
 def start_tables(right_in, left_in, work):
     copies = [
         pltpu.make_async_copy(right_in, work["right"], work["sems"].at[0]),
@@ -335,7 +336,7 @@
 
 
 def first_kernel(
-    info, perm, tiles, probe, amp, right_in, left_in, strip, send, kept, given, peak, *scratch
+    info, perm, tiles, probe, amp_in, right_in, left_in, strip, send, kept, given, peak, amp, *scratch
 ):
     work = dict(zip(WORK, scratch))
     sgrad, pgrad, weight = work["sgrad"], work["pgrad"], work["weight"]
@@ -344,6 +345,9 @@
         for c in range(2 * GROUPS):
             pltpu.make_async_copy(tiles.at[slot_of(info, perm, r, c)], needed.at[r, c], sem).start()
     copies = start_tables(right_in, left_in, work)
+    copies.append(pltpu.make_async_copy(amp_in, amp, work["sems"].at[3]))
+    copies[-1].start()
+    clear(work)
     peak[0, 0] = probe_strength(probe, work["strength"])
     pltpu.make_async_copy(needed, needed, sem).wait()
     for r in range(4):
@@ -380,6 +384,7 @@
     for copy in come:
         copy.start()
     copies = start_tables(right_in, left_in, work)
+    clear(work)
     inverse = 1.0 / peak[0, 0]
     come[0].wait()
     come[1].wait()
@@ -480,7 +485,6 @@
 
 
 def unpack_kernel(spots, info, perm, tiles, arrived, out, total, came, sems):
-    cls = own_class(info, perm)
     step = N_SCAN // PARTS
     held = total.at[pl.ds(0, TILE)]
     pltpu.make_async_copy(tiles, held, sems.at[PARTS]).start()
@@ -489,8 +493,9 @@
         rows = pl.ds(part * step * 3, step * 3)
         parts.append(pltpu.make_async_copy(arrived.at[rows], came.at[rows], sems.at[part]))
         parts[-1].start()
+    cls = own_class(info, perm)
+    total[TILE] = jnp.zeros((TILE, HALF), F32)
     pltpu.make_async_copy(tiles, held, sems.at[PARTS]).wait()
-    total[TILE] = jnp.zeros((TILE, HALF), F32)
 
     def one(t, carry):
         for k in range(3):
@@ -696,11 +701,11 @@
             shaped(MODES, 2, 2, HALF, HALF),
             shaped(1, 1),
         ),
-        [SMEM, SMEM, HBM, VMEM, VMEM, HBM, HBM],
-        scratch,
+        [SMEM, SMEM, HBM, VMEM, HBM, HBM, HBM],
+        [pltpu.VMEM((PATS, 2, HALF, SIDE), F32)] + scratch,
         out_specs=(VMEM, VMEM, VMEM, VMEM, SMEM),
         name="first",
-        limit=30,
+        limit=38,
     )(info, perm, arrived, modes, amp, right, left)
 
     chip = (kept + lax.ppermute(given, "scan", SWAP)).reshape(N_SCAN, PRB_ROWS, HALF)

time: 264 us -> 263 us (level)
  no operation moved by 1% of the time
where the time goes in v4:
time: 263 us; the launch traced here: 262 us
  waiting for transfers between devices  73.8 us (28%)
  blocking collectives  70.3 us (27%)
  starting transfers between devices  49.4 us (19%)
  Pallas kernels  49.4 us (19%)
  local copies, waits for them, and re-layouts  13.5 us (5%)
  between operations  3.01 us (1%)
  other arithmetic  2.92 us (1%)
    all_to_all x2, blocking collectives, exchange(): return lax.all_to_all(x, 'scan', split_axis=0, concat_axis=0, tiled=True)  70.3 us
    ppermute x6, waiting for transfers between devices, sum_turned(): lax.ppermute(parts[k], axis, perm_of(k))  30.7 us
    pallas_call x1, Pallas kernels, body(): kernel(first_kernel, (shaped(2, GROUPS, SIDE, HALF), shaped(N_SCAN, SEND_...  20.9 us
    all_to_all x3, starting transfers between devices, exchange(): return lax.all_to_all(x, 'scan', split_axis=0, concat_axis=0, tiled=True)  19.4 us
    all_to_all x3, waiting for transfers between devices, exchange(): return lax.all_to_all(x, 'scan', split_axis=0, concat_axis=0, tiled=True)  18.4 us
    pallas_call x1, Pallas kernels, body(): kernel(second_kernel, (shaped(96, TILE, HALF), shaped(MODES, 2, 2, HALF,...  16.1 us
    ppermute x3, waiting for transfers between devices, gather_rows(): got = lax.ppermute(x, axis, perm_of(k))  9.74 us
    ppermute x6, starting transfers between devices, sum_all(): near, far, middle = (lax.ppermute(x, axis, perm_of(k)) for k in (1, 3, 2))  8.66 us
  transfers between devices with their start and end apart: 26, of which 17 were waited for; matrix products, arithmetic and copies ran while one was open for 4% of the time, Pallas kernels for 3%

profile of v4, /device:TPU:1, one launch (start us, length us, event | category | flops | bytes accessed | tf_op | source)
XLA Modules:
  0.0 262.4 jit_solution(2778278314610998393)
XLA Ops:
  0.6 0.8 slice_reduce_fusion
  1.4 0.6 broadcast_in_dim.26
  2.1 9.6 %all-to-all-start = ((s32[32,1,2]{2,1,0:T(1,128)}), s32[32,1,2]{2,1,0:T(1,128)S(1)}, u32[]{:S(2)}, u32[]{:S(2)}) async-start(s32[32,1,2]{2,1,0:T(1,128)} %broadcast_in_dim.26), calls=%async_computation | async-start | bytes 32768 | tf_op jit(solution)/shard_map/all_to_all | solution.py:629
  11.7 0.6 fusion.6
  14.2 0.7 stack.63.info
  14.9 3.6 %all-to-all-done = s32[32,1,2]{2,1,0:T(1,128)S(1)} async-done(((s32[32,1,2]{2,1,0:T(1,128)}), s32[32,1,2]{2,1,0:T(1,128)S(1)}, u32[]{:S(2)}, u32[]{:S(2)}) %all-to-all-start) | async-done | bytes 288 | tf_op jit(solution)/shard_map/all_to_all | solution.py:629
  18.5 1.6 copy-done.3
  20.1 2.9 %pack.1 = f32[96,64,128]{2,1,0:T(8,128)} custom-call(s32[32,2]{1,0:T(8,128)S(1)} %bitcast.65, s32[7]{0:T(128)S(1)} %stack.63.info, s32[32]{0:T(128)S(1)} %fusion.5.perm, f32[64,64,128]{2,1,0:T(8,128)S(1)} %bitcast.63), custom_call_target="tpu_custom_call" | custom-call | tf_op jit(solution)/shard_map/pack/pallas_call | solution.py:672
  23.0 5.2 %all-to-all-start.1 = ((f32[96,64,128]{2,1,0:T(8,128)}), f32[96,64,128]{2,1,0:T(8,128)}, u32[]{:S(2)}, u32[]{:S(2)}) async-start(f32[96,64,128]{2,1,0:T(8,128)} %pack.1), calls=%async_computation.1 | async-start | bytes 6291456 | tf_op jit(solution)/shard_map/all_to_all | solution.py:629
  28.3 0.3 reshape.66
  28.6 1.1 broadcast_in_dim.27
  29.7 0.7 dynamic-slice_bitcast_fusion
  30.5 1.2 collective-permute-start
  31.7 1.5 collective-permute-start.1
  33.1 1.5 collective-permute-start.2
  34.7 4.6 %collective-permute-done = f32[2,2,128,128]{3,2,1,0:T(8,128)S(1)} collective-permute-done((f32[2,2,128,128]{3,2,1,0:T(8,128)S(1)}, f32[2,2,128,128]{3,2,1,0:T(8,128)S(1)}, u32[]{:S(2)}, u32[]{:S(2)}) %collective-permute-start) | collective-permute-done | bytes 262176 | tf_op jit(solution)/shard_map/ppermute | solution.py:646
  39.2 0.7 bitcast_dynamic-update-slice_fusion.2
  40.0 0.7 bitcast_dynamic-update-slice_fusion.1
  40.7 5.2 %collective-permute-done.2 = f32[2,2,128,128]{3,2,1,0:T(8,128)S(1)} collective-permute-done((f32[2,2,128,128]{3,2,1,0:T(8,128)S(1)}, f32[2,2,128,128]{3,2,1,0:T(8,128)S(1)}, u32[]{:S(2)}, u32[]{:S(2)}) %collective-permute-start.2) | collective-permute-done | bytes 262176 | tf_op jit(solution)/shard_map/ppermute | solution.py:646
  45.8 0.7 bitcast_dynamic-update-slice_fusion
  46.6 1.1 collective-permute-start.3
  47.7 1.2 spread.1
  48.9 1.0 copy-done.7
  49.9 0.4 collective-permute-done.3
  50.3 2.4 maximum_select_fusion.probe.old_probe
  52.8 14.8 %all-to-all-done.1.tiles = f32[96,64,128]{2,1,0:T(8,128)} async-done(((f32[96,64,128]{2,1,0:T(8,128)}), f32[96,64,128]{2,1,0:T(8,128)}, u32[]{:S(2)}, u32[]{:S(2)}) %all-to-all-start.1) | async-done | bytes 3145760 | tf_op jit(solution)/shard_map/all_to_all | solution.py:629
  67.6 1.2 copy-done.5
  68.8 1.2 copy-done.8
  70.0 20.9 %first.1 = (f32[2,5,256,128]{3,2,1,0:T(8,128)S(1)}, f32[32,144,128]{2,1,0:T(8,128)S(1)}, f32[4,2,2,128,128]{4,3,2,1,0:T(8,128)S(1)}, f32[4,2,2,128,128]{4,3,2,1,0:T(8,128)S(1)}, f32[1,1]{1,0:T(1,128)}) custom-call(s32[7]{0:T(128)S(1)} %stack.63.info, s32[32]{0:T(128)S(1)} %fusion.5.perm, f32[96,64,128]{2,1,0:T(8,128)} %all-to-all-done.1.tiles, ...), custom_call_target="tpu_custom_call" | custom-call | tf_op jit(solution)/shard_map/first/pallas_call | solution.py:695
  90.9 2.9 %collective-permute-start.4 = (f32[4,2,2,128,128]{4,3,2,1,0:T(8,128)S(1)}, f32[4,2,2,128,128]{4,3,2,1,0:T(8,128)S(1)}, u32[]{:S(2)}, u32[]{:S(2)}) collective-permute-start(f32[4,2,2,128,128]{4,3,2,1,0:T(8,128)S(1)} %get-tuple-element.22), channel_id=1, source_target_pairs={{0,1},{1,0},{2,3},{3,2},{4,5},{5,4},{6,7},{7,6},{8,9},{9,8},{10,11... | collective-permute-start | bytes 3145736 | tf_op jit(solution)/shard_map/ppermute | solution.py:711
  93.9 2.3 collective-permute-done.4
  96.2 0.2 add.120
  96.4 34.6 %all_to_all.25.arrived = f32[32,144,128]{2,1,0:T(8,128)S(1)} all-to-all(f32[32,144,128]{2,1,0:T(8,128)S(1)} %constant_dynamic-update-slice_fusion.1.first_in), channel_id=1, replica_groups=mesh['grp'=4,'scan'=32] {'scan'}, dimensions={0} | all-to-all | bytes 4718592 | tf_op jit(solution)/shard_map/all_to_all | solution.py:629
  131.0 0.1 sums.1
  131.2 2.6 collective-permute-start.7
  133.7 1.7 collective-permute-start.5
  135.5 1.7 owner.1
  137.2 2.6 %collective-permute-done.6 = f32[2,64,128]{2,1,0:T(8,128)S(1)} collective-permute-done((f32[2,64,128]{2,1,0:T(8,128)S(1)}, f32[2,64,128]{2,1,0:T(8,128)S(1)}, u32[]{:S(2)}, u32[]{:S(2)}) %collective-permute-start.6) | collective-permute-done | bytes 65568 | tf_op jit(solution)/shard_map/ppermute | solution.py:638
  140.1 35.7 %all_to_all.26.total_in = f32[32,144,128]{2,1,0:T(8,128)S(1)} all-to-all(f32[32,144,128]{2,1,0:T(8,128)S(1)} %constant_dynamic-update-slice_fusion), channel_id=1, replica_groups=mesh['grp'=4,'scan'=32] {'scan'}, dimensions={0} | all-to-all | bytes 4718592 | tf_op jit(solution)/shard_map/all_to_all | solution.py:629
  175.9 0.3 collective-permute-start.8
  176.2 2.5 collective-permute-done.8.other_in
  178.7 16.1 %second.1 = (f32[96,64,128]{2,1,0:T(8,128)}, f32[4,2,2,128,128]{4,3,2,1,0:T(8,128)S(1)}, f32[4,2,2,128,128]{4,3,2,1,0:T(8,128)S(1)}) custom-call(s32[7]{0:T(128)S(1)} %stack.63.info, s32[32]{0:T(128)S(1)} %fusion.5.perm, f32[1,1]{1,0:T(1,128)} %get-tuple-element.17.peak, f32[1,4]{1,0:T(1,128)S(1)} %get-tuple-element.18.energy, ...), custom_call_target="tpu_custom_call" | custom-call | tf_op jit(solution)/shard_map/second/pallas_call | solution.py:733
  194.8 4.6 %all-to-all-start.4 = ((f32[96,64,128]{2,1,0:T(8,128)}), f32[96,64,128]{2,1,0:T(8,128)}, u32[]{:S(2)}, u32[]{:S(2)}) async-start(f32[96,64,128]{2,1,0:T(8,128)} %get-tuple-element.25), calls=%async_computation.4 | async-start | bytes 6291456 | tf_op jit(solution)/shard_map/all_to_all | solution.py:629
  199.4 0.4 collective-permute-start.9
  199.9 2.3 collective-permute-done.9
  202.2 0.1 slice_add_fusion
  202.4 2.7 %collective-permute-start.12 = (f32[4,128,128]{2,1,0:T(8,128)S(1)}, f32[4,128,128]{2,1,0:T(8,128)S(1)}, u32[]{:S(2)}, u32[]{:S(2)}) collective-permute-start(f32[4,128,128]{2,1,0:T(8,128)S(1)} %bitcast.74), channel_id=1, source_target_pairs={{0,96},{32,0},{64,32},{96,64},{1,97},{33,1},{65,33},{97,65},{2,98}... | collective-permute-start | bytes 786440 | tf_op jit(solution)/shard_map/ppermute | solution.py:633
  205.1 0.7 collective-permute-start.10
  205.7 5.5 %collective-permute-done.11 = f32[4,128,128]{2,1,0:T(8,128)S(1)} collective-permute-done((f32[4,128,128]{2,1,0:T(8,128)S(1)}, f32[4,128,128]{2,1,0:T(8,128)S(1)}, u32[]{:S(2)}, u32[]{:S(2)}) %collective-permute-start.11) | collective-permute-done | bytes 262176 | tf_op jit(solution)/shard_map/ppermute | solution.py:633
  211.2 6.3 %collective-permute-done.10 = f32[4,128,128]{2,1,0:T(8,128)S(1)} collective-permute-done((f32[4,128,128]{2,1,0:T(8,128)S(1)}, f32[4,128,128]{2,1,0:T(8,128)S(1)}, u32[]{:S(2)}, u32[]{:S(2)}) %collective-permute-start.10) | collective-permute-done | bytes 262176 | tf_op jit(solution)/shard_map/ppermute | solution.py:633
  217.6 2.7 %collective-permute-start.15 = (f32[128,128]{1,0:T(8,128)S(1)}, f32[128,128]{1,0:T(8,128)S(1)}, u32[]{:S(2)}, u32[]{:S(2)}) collective-permute-start(f32[128,128]{1,0:T(8,128)S(1)} %get-tuple-element.36), channel_id=1, source_target_pairs={{0,6},{1,7},{2,0},{3,1},{4,2},{5,3},{6,4},{7,5},{8,14},{9,15},{10,... | collective-permute-start | bytes 196616 | tf_op jit(solution)/shard_map/ppermute | solution.py:633
  220.3 1.7 collective-permute-start.13
  222.0 14.9 %collective-permute-done.15 = f32[128,128]{1,0:T(8,128)S(1)} collective-permute-done((f32[128,128]{1,0:T(8,128)S(1)}, f32[128,128]{1,0:T(8,128)S(1)}, u32[]{:S(2)}, u32[]{:S(2)}) %collective-permute-start.15) | collective-permute-done | bytes 65568 | tf_op jit(solution)/shard_map/ppermute | solution.py:633
  237.0 1.1 collective-permute-done.14
  238.1 2.9 %collective-permute-done.13 = f32[128,128]{1,0:T(8,128)S(1)} collective-permute-done((f32[128,128]{1,0:T(8,128)S(1)}, f32[128,128]{1,0:T(8,128)S(1)}, u32[]{:S(2)}, u32[]{:S(2)}) %collective-permute-start.13) | collective-permute-done | bytes 65568 | tf_op jit(solution)/shard_map/ppermute | solution.py:633
  241.0 3.1 %collective-permute-start.18 = (f32[128,128]{1,0:T(8,128)S(1)}, f32[128,128]{1,0:T(8,128)S(1)}, u32[]{:S(2)}, u32[]{:S(2)}) collective-permute-start(f32[128,128]{1,0:T(8,128)S(1)} %fusion.4), channel_id=1, source_target_pairs={{0,24},{1,25},{2,26},{3,27},{4,28},{5,29},{6,30},{7,31},{8,0},{9,1... | collective-permute-start | bytes 196616 | tf_op jit(solution)/shard_map/ppermute | solution.py:638
  244.1 1.3 collective-permute-start.16
  245.4 3.7 %collective-permute-done.17 = f32[128,128]{1,0:T(8,128)S(1)} collective-permute-done((f32[128,128]{1,0:T(8,128)S(1)}, f32[128,128]{1,0:T(8,128)S(1)}, u32[]{:S(2)}, u32[]{:S(2)}) %collective-permute-start.17) | collective-permute-done | bytes 65568 | tf_op jit(solution)/shard_map/ppermute | solution.py:638
  249.2 1.4 collective-permute-start.20
  250.7 1.0 constant_dynamic-slice_fusion.1
  251.7 5.1 %unpack.1 = f32[64,64,128]{2,1,0:T(8,128)} custom-call(s32[32,2]{1,0:T(8,128)} %bitcast.67, s32[7]{0:T(128)} %copy-done.14, s32[32]{0:T(128)} %copy-done.16, f32[64,64,128]{2,1,0:T(8,128)} %bitcast.62, f32[96,64,128]{2,1,0:T(8,128)} %all-to-all-done.4.arrived), custom_call_target="tpu_custom_call" | custom-call | bytes 8388608 | tf_op jit(solution)/shard_map/unpack/pallas_call | solution.py:760
  256.8 2.9 %collective-permute-start.22 = (f32[4,128,128]{2,1,0:T(8,128)S(1)}, f32[4,128,128]{2,1,0:T(8,128)S(1)}, u32[]{:S(2)}, u32[]{:S(2)}) collective-permute-start(f32[4,128,128]{2,1,0:T(8,128)S(1)} %pad_maximum_fusion.half), channel_id=1, source_target_pairs={{0,1},{1,0},{2,3},{3,2},{4,5},{5,4},{6,7},{7,6},{8,9},{9,8},{10,11... | collective-permute-start | bytes 786440 | tf_op jit(solution)/shard_map/ppermute | solution.py:777
  259.9 1.1 collective-permute-done.22.other_half
  260.9 1.4 finish.1
  (71 shorter events, 1.1 us)
Async XLA Ops:
  0.6 13.5 %copy-start = (s32[4,32]{1,0:T(4,128)S(1)}, s32[4,32]{1,0:T(4,128)}, u32[]{:S(2)}) copy-start(s32[4,32]{1,0:T(4,128)} %param.10) | copy-start | bytes 1540
  2.1 16.5 %all-to-all-start = ((s32[32,1,2]{2,1,0:T(1,128)}), s32[32,1,2]{2,1,0:T(1,128)S(1)}, u32[]{:S(2)}, u32[]{:S(2)}) async-start(s32[32,1,2]{2,1,0:T(1,128)} %broadcast_in_dim.26), calls=%async_computation | async-start | bytes 32768 | tf_op jit(solution)/shard_map/all_to_all | solution.py:629
  14.2 164.5 %copy-start.16 = (s32[32]{0:T(128)}, s32[32]{0:T(128)S(1)}, u32[]{:S(2)}) copy-start(s32[32]{0:T(128)S(1)} %fusion.5.perm) | copy-start | bytes 388
  14.9 163.8 %copy-start.14 = (s32[7]{0:T(128)}, s32[7]{0:T(128)S(1)}, u32[]{:S(2)}) copy-start(s32[7]{0:T(128)S(1)} %stack.63.info) | copy-start | bytes 88
  18.5 116.9 %copy-start.12 = (s32[32,1,2]{2,1,0:T(1,128)}, s32[32,1,2]{2,1,0:T(1,128)S(1)}, u32[]{:S(2)}) copy-start(s32[32,1,2]{2,1,0:T(1,128)S(1)} %all-to-all-done) | copy-start | bytes 772
  18.5 1.6 copy-start.3
  23.0 5.2 %copy-start.21 = (f32[1,2,256,256]{3,2,1,0:T(8,128)S(1)}, f32[1,2,256,256]{3,2,1,0:T(8,128)}, u32[]{:S(2)}) copy-start(f32[1,2,256,256]{3,2,1,0:T(8,128)} %param.12) | copy-start | bytes 1572868
  23.0 44.5 %all-to-all-start.1 = ((f32[96,64,128]{2,1,0:T(8,128)}), f32[96,64,128]{2,1,0:T(8,128)}, u32[]{:S(2)}, u32[]{:S(2)}) async-start(f32[96,64,128]{2,1,0:T(8,128)} %pack.1), calls=%async_computation.1 | async-start | bytes 6291456 | tf_op jit(solution)/shard_map/all_to_all | solution.py:629
  28.5 19.2 %copy-start.11 = (f32[4,256,256]{2,1,0:T(8,128)S(1)}, f32[4,256,256]{2,1,0:T(8,128)}, u32[]{:S(2)}) copy-start(f32[4,256,256]{2,1,0:T(8,128)} %amp.1) | copy-start | bytes 3145732
  28.5 19.2 %copy-start.13 = (bf16[256,256]{1,0:T(8,128)(2,1)S(1)}, bf16[256,256]{1,0:T(8,128)(2,1)}, u32[]{:S(2)}) copy-start(bf16[256,256]{1,0:T(8,128)(2,1)} %constant.124.clone.shuffle) | copy-start | bytes 393220
  28.6 21.7 %copy-start.18 = (f32[2,2,2,32,2,2,128]{6,3,4,2,5,0,1:T(8,128)}, f32[2,2,2,32,2,2,128]{6,3,4,2,5,0,1:T(8,128)S(1)}, u32[]{:S(2)}) copy-start(f32[2,2,2,32,2,2,128]{6,3,4,2,5,0,1:T(8,128)S(1)} %copy.19) | copy-start | bytes 1572868
  30.5 8.8 %collective-permute-start = (f32[2,2,128,128]{3,2,1,0:T(8,128)S(1)}, f32[2,2,128,128]{3,2,1,0:T(8,128)S(1)}, u32[]{:S(2)}, u32[]{:S(2)}) collective-permute-start(f32[2,2,128,128]{3,2,1,0:T(8,128)S(1)} %get-tuple-element.34), channel_id=1, source_target_pairs={{0,32},{32,64},{64,96},{96,0},{1,33},{33,65},{65,97},{97,1},{2,34}... | collective-permute-start | bytes 786440 | tf_op jit(solution)/shard_map/ppermute | solution.py:646
  31.7 8.3 %collective-permute-start.1 = (f32[2,2,128,128]{3,2,1,0:T(8,128)S(1)}, f32[2,2,128,128]{3,2,1,0:T(8,128)S(1)}, u32[]{:S(2)}, u32[]{:S(2)}) collective-permute-start(f32[2,2,128,128]{3,2,1,0:T(8,128)S(1)} %get-tuple-element.34), channel_id=1, source_target_pairs={{0,96},{32,0},{64,32},{96,64},{1,97},{33,1},{65,33},{97,65},{2,98}... | collective-permute-start | bytes 786440 | tf_op jit(solution)/shard_map/ppermute | solution.py:646
  33.1 12.7 %collective-permute-start.2 = (f32[2,2,128,128]{3,2,1,0:T(8,128)S(1)}, f32[2,2,128,128]{3,2,1,0:T(8,128)S(1)}, u32[]{:S(2)}, u32[]{:S(2)}) collective-permute-start(f32[2,2,128,128]{3,2,1,0:T(8,128)S(1)} %get-tuple-element.34), channel_id=1, source_target_pairs={{0,64},{32,96},{64,0},{96,32},{1,65},{33,97},{65,1},{97,33},{2,66}... | collective-permute-start | bytes 786440 | tf_op jit(solution)/shard_map/ppermute | solution.py:646
  46.6 3.8 %collective-permute-start.3 = (f32[4,2,2,128,128]{4,3,2,1,0:T(8,128)}, f32[4,2,2,128,128]{4,3,2,1,0:T(8,128)}, u32[]{:S(2)}, u32[]{:S(2)}) collective-permute-start(f32[4,2,2,128,128]{4,3,2,1,0:T(8,128)} %bitcast_dynamic-update-slice_fusion), channel_id=1, source_target_pairs={{0,1},{1,0},{2,3},{3,2},{4,5},{5,4},{6,7},{7,6},{8,9},{9,8},{10,11... | collective-permute-start | bytes 3145736 | tf_op jit(solution)/shard_map/ppermute | solution.py:684
  48.9 1.0 copy-start.7
  49.9 17.6 %copy-start.4 = (bf16[4,256,512]{2,1,0:T(8,128)(2,1)S(1)}, bf16[4,256,512]{2,1,0:T(8,128)(2,1)}, u32[]{:S(2)}) copy-start(bf16[4,256,512]{2,1,0:T(8,128)(2,1)} %constant.123.clone.left_in) | copy-start | bytes 3145732
  52.8 38.2 %copy-start.1 = (f32[4,2,2,2,128,128]{5,4,3,2,1,0:T(8,128)}, f32[4,2,2,2,128,128]{5,4,3,2,1,0:T(8,128)S(1)}, u32[]{:S(2)}) copy-start(f32[4,2,2,2,128,128]{5,4,3,2,1,0:T(8,128)S(1)} %maximum_select_fusion.probe.old_probe) | copy-start | bytes 6291460
  67.6 1.2 copy-start.5
  68.8 1.2 copy-start.8
  90.9 5.5 %copy-start.10 = (f32[2,5,256,128]{3,2,1,0:T(8,128)}, f32[2,5,256,128]{3,2,1,0:T(8,128)S(1)}, u32[]{:S(2)}) copy-start(f32[2,5,256,128]{3,2,1,0:T(8,128)S(1)} %get-tuple-element.19.old_strip) | copy-start | bytes 3932164
  90.9 5.2 %collective-permute-start.4 = (f32[4,2,2,128,128]{4,3,2,1,0:T(8,128)S(1)}, f32[4,2,2,128,128]{4,3,2,1,0:T(8,128)S(1)}, u32[]{:S(2)}, u32[]{:S(2)}) collective-permute-start(f32[4,2,2,128,128]{4,3,2,1,0:T(8,128)S(1)} %get-tuple-element.22), channel_id=1, source_target_pairs={{0,1},{1,0},{2,3},{3,2},{4,5},{5,4},{6,7},{7,6},{8,9},{9,8},{10,11... | collective-permute-start | bytes 3145736 | tf_op jit(solution)/shard_map/ppermute | solution.py:711
  96.4 34.6 %copy-start.2 = (f32[32,144,128]{2,1,0:T(8,128)}, f32[32,144,128]{2,1,0:T(8,128)S(1)}, u32[]{:S(2)}) copy-start(f32[32,144,128]{2,1,0:T(8,128)S(1)} %constant_dynamic-update-slice_fusion.1.first_in) | copy-start | bytes 7077892
  131.2 6.0 %collective-permute-start.7 = (f32[2,64,128]{2,1,0:T(8,128)S(1)}, f32[2,64,128]{2,1,0:T(8,128)S(1)}, u32[]{:S(2)}, u32[]{:S(2)}) collective-permute-start(f32[2,64,128]{2,1,0:T(8,128)S(1)} %sums.1), channel_id=1, source_target_pairs={{0,96},{32,0},{64,32},{96,64},{1,97},{33,1},{65,33},{97,65},{2,98}... | collective-permute-start | bytes 196616 | tf_op jit(solution)/shard_map/ppermute | solution.py:638
  133.7 6.1 %collective-permute-start.6 = (f32[2,64,128]{2,1,0:T(8,128)S(1)}, f32[2,64,128]{2,1,0:T(8,128)S(1)}, u32[]{:S(2)}, u32[]{:S(2)}) collective-permute-start(f32[2,64,128]{2,1,0:T(8,128)S(1)} %sums.1), channel_id=1, source_target_pairs={{0,32},{32,64},{64,96},{96,0},{1,33},{33,65},{65,97},{97,1},{2,34}... | collective-permute-start | bytes 196616 | tf_op jit(solution)/shard_map/ppermute | solution.py:638
  133.7 6.1 %collective-permute-start.5 = (f32[2,64,128]{2,1,0:T(8,128)S(1)}, f32[2,64,128]{2,1,0:T(8,128)S(1)}, u32[]{:S(2)}, u32[]{:S(2)}) collective-permute-start(f32[2,64,128]{2,1,0:T(8,128)S(1)} %sums.1), channel_id=1, source_target_pairs={{0,64},{32,96},{64,0},{96,32},{1,65},{33,97},{65,1},{97,33},{2,66}... | collective-permute-start | bytes 196616 | tf_op jit(solution)/shard_map/ppermute | solution.py:638
  140.1 38.6 %copy-start.6 = (bf16[4,512,256]{2,1,0:T(8,128)(2,1)S(1)}, bf16[4,512,256]{2,1,0:T(8,128)(2,1)}, u32[]{:S(2)}) copy-start(bf16[4,512,256]{2,1,0:T(8,128)(2,1)} %constant.122.clone.right_in) | copy-start | bytes 3145732
  140.1 38.6 %copy-start.9 = (f32[4,2,128,256]{3,2,1,0:T(8,128)S(1)}, f32[4,2,128,256]{3,2,1,0:T(8,128)}, u32[]{:S(2)}) copy-start(f32[4,2,128,256]{3,2,1,0:T(8,128)} %copy-done.7) | copy-start | bytes 3145732
  175.8 2.9 %copy-start.17 = (f32[32,144,128]{2,1,0:T(8,128)}, f32[32,144,128]{2,1,0:T(8,128)S(1)}, u32[]{:S(2)}) copy-start(f32[32,144,128]{2,1,0:T(8,128)S(1)} %all_to_all.26.total_in) | copy-start | bytes 7077892
  175.9 2.8 %copy-start.20 = (f32[32,64,128]{2,1,0:T(8,128)}, f32[32,64,128]{2,1,0:T(8,128)S(1)}, u32[]{:S(2)}) copy-start(f32[32,64,128]{2,1,0:T(8,128)S(1)} %slice.74) | copy-start | bytes 3145732
  175.9 2.7 %collective-permute-start.8 = (f32[32,64,128]{2,1,0:T(8,128)S(1)}, f32[32,64,128]{2,1,0:T(8,128)S(1)}, u32[]{:S(2)}, u32[]{:S(2)}) collective-permute-start(f32[32,64,128]{2,1,0:T(8,128)S(1)} %slice.74), channel_id=1, source_target_pairs={{0,1},{1,0},{2,3},{3,2},{4,5},{5,4},{6,7},{7,6},{8,9},{9,8},{10,11... | collective-permute-start | bytes 3145736 | tf_op jit(solution)/shard_map/ppermute | solution.py:731
  194.8 56.9 %all-to-all-start.4 = ((f32[96,64,128]{2,1,0:T(8,128)}), f32[96,64,128]{2,1,0:T(8,128)}, u32[]{:S(2)}, u32[]{:S(2)}) async-start(f32[96,64,128]{2,1,0:T(8,128)} %get-tuple-element.25), calls=%async_computation.4 | async-start | bytes 6291456 | tf_op jit(solution)/shard_map/all_to_all | solution.py:629
  199.4 2.7 %collective-permute-start.9 = (f32[4,2,2,128,128]{4,3,2,1,0:T(8,128)S(1)}, f32[4,2,2,128,128]{4,3,2,1,0:T(8,128)S(1)}, u32[]{:S(2)}, u32[]{:S(2)}) collective-permute-start(f32[4,2,2,128,128]{4,3,2,1,0:T(8,128)S(1)} %get-tuple-element.24), channel_id=1, source_target_pairs={{0,1},{1,0},{2,3},{3,2},{4,5},{5,4},{6,7},{7,6},{8,9},{9,8},{10,11... | collective-permute-start | bytes 3145736 | tf_op jit(solution)/shard_map/ppermute | solution.py:755
  202.3 8.9 %collective-permute-start.11 = (f32[4,128,128]{2,1,0:T(8,128)S(1)}, f32[4,128,128]{2,1,0:T(8,128)S(1)}, u32[]{:S(2)}, u32[]{:S(2)}) collective-permute-start(f32[4,128,128]{2,1,0:T(8,128)S(1)} %bitcast.75), channel_id=1, source_target_pairs={{0,32},{32,64},{64,96},{96,0},{1,33},{33,65},{65,97},{97,1},{2,34}... | collective-permute-start | bytes 786440 | tf_op jit(solution)/shard_map/ppermute | solution.py:633
  202.4 8.8 %collective-permute-start.12 = (f32[4,128,128]{2,1,0:T(8,128)S(1)}, f32[4,128,128]{2,1,0:T(8,128)S(1)}, u32[]{:S(2)}, u32[]{:S(2)}) collective-permute-start(f32[4,128,128]{2,1,0:T(8,128)S(1)} %bitcast.74), channel_id=1, source_target_pairs={{0,96},{32,0},{64,32},{96,64},{1,97},{33,1},{65,33},{97,65},{2,98}... | collective-permute-start | bytes 786440 | tf_op jit(solution)/shard_map/ppermute | solution.py:633
  205.1 12.5 %collective-permute-start.10 = (f32[4,128,128]{2,1,0:T(8,128)S(1)}, f32[4,128,128]{2,1,0:T(8,128)S(1)}, u32[]{:S(2)}, u32[]{:S(2)}) collective-permute-start(f32[4,128,128]{2,1,0:T(8,128)S(1)} %bitcast.73), channel_id=1, source_target_pairs={{0,64},{32,96},{64,0},{96,32},{1,65},{33,97},{65,1},{97,33},{2,66}... | collective-permute-start | bytes 786440 | tf_op jit(solution)/shard_map/ppermute | solution.py:633
  217.6 19.4 %collective-permute-start.15 = (f32[128,128]{1,0:T(8,128)S(1)}, f32[128,128]{1,0:T(8,128)S(1)}, u32[]{:S(2)}, u32[]{:S(2)}) collective-permute-start(f32[128,128]{1,0:T(8,128)S(1)} %get-tuple-element.36), channel_id=1, source_target_pairs={{0,6},{1,7},{2,0},{3,1},{4,2},{5,3},{6,4},{7,5},{8,14},{9,15},{10,... | collective-permute-start | bytes 196616 | tf_op jit(solution)/shard_map/ppermute | solution.py:633
  220.3 17.8 %collective-permute-start.14 = (f32[128,128]{1,0:T(8,128)S(1)}, f32[128,128]{1,0:T(8,128)S(1)}, u32[]{:S(2)}, u32[]{:S(2)}) collective-permute-start(f32[128,128]{1,0:T(8,128)S(1)} %get-tuple-element.37), channel_id=1, source_target_pairs={{0,2},{1,3},{2,4},{3,5},{4,6},{5,7},{6,0},{7,1},{8,10},{9,11},{10,... | collective-permute-start | bytes 196616 | tf_op jit(solution)/shard_map/ppermute | solution.py:633
  220.3 20.7 %collective-permute-start.13 = (f32[128,128]{1,0:T(8,128)S(1)}, f32[128,128]{1,0:T(8,128)S(1)}, u32[]{:S(2)}, u32[]{:S(2)}) collective-permute-start(f32[128,128]{1,0:T(8,128)S(1)} %get-tuple-element.38), channel_id=1, source_target_pairs={{0,4},{1,5},{2,6},{3,7},{4,0},{5,1},{6,2},{7,3},{8,12},{9,13},{10,... | collective-permute-start | bytes 196616 | tf_op jit(solution)/shard_map/ppermute | solution.py:633
  241.0 4.4 %collective-permute-start.18 = (f32[128,128]{1,0:T(8,128)S(1)}, f32[128,128]{1,0:T(8,128)S(1)}, u32[]{:S(2)}, u32[]{:S(2)}) collective-permute-start(f32[128,128]{1,0:T(8,128)S(1)} %fusion.4), channel_id=1, source_target_pairs={{0,24},{1,25},{2,26},{3,27},{4,28},{5,29},{6,30},{7,31},{8,0},{9,1... | collective-permute-start | bytes 196616 | tf_op jit(solution)/shard_map/ppermute | solution.py:638
  244.1 5.0 %collective-permute-start.17 = (f32[128,128]{1,0:T(8,128)S(1)}, f32[128,128]{1,0:T(8,128)S(1)}, u32[]{:S(2)}, u32[]{:S(2)}) collective-permute-start(f32[128,128]{1,0:T(8,128)S(1)} %fusion.4), channel_id=1, source_target_pairs={{0,8},{1,9},{2,10},{3,11},{4,12},{5,13},{6,14},{7,15},{8,16},{9,17... | collective-permute-start | bytes 196616 | tf_op jit(solution)/shard_map/ppermute | solution.py:638
  244.1 5.0 %collective-permute-start.16 = (f32[128,128]{1,0:T(8,128)S(1)}, f32[128,128]{1,0:T(8,128)S(1)}, u32[]{:S(2)}, u32[]{:S(2)}) collective-permute-start(f32[128,128]{1,0:T(8,128)S(1)} %fusion.4), channel_id=1, source_target_pairs={{0,16},{1,17},{2,18},{3,19},{4,20},{5,21},{6,22},{7,23},{8,24},{9,... | collective-permute-start | bytes 196616 | tf_op jit(solution)/shard_map/ppermute | solution.py:638
  249.1 7.6 %collective-permute-start.21 = (f32[128,128]{1,0:T(8,128)S(1)}, f32[128,128]{1,0:T(8,128)S(1)}, u32[]{:S(2)}, u32[]{:S(2)}) collective-permute-start(f32[128,128]{1,0:T(8,128)S(1)} %add_add_fusion), channel_id=1, source_target_pairs={{0,6},{1,7},{2,0},{3,1},{4,2},{5,3},{6,4},{7,5},{8,14},{9,15},{10,... | collective-permute-start | bytes 196616 | tf_op jit(solution)/shard_map/ppermute | solution.py:774
  249.2 7.6 %collective-permute-start.20 = (f32[128,128]{1,0:T(8,128)S(1)}, f32[128,128]{1,0:T(8,128)S(1)}, u32[]{:S(2)}, u32[]{:S(2)}) collective-permute-start(f32[128,128]{1,0:T(8,128)S(1)} %add_add_fusion), channel_id=1, source_target_pairs={{0,4},{1,5},{2,6},{3,7},{4,0},{5,1},{6,2},{7,3},{8,12},{9,13},{10,... | collective-permute-start | bytes 196616 | tf_op jit(solution)/shard_map/ppermute | solution.py:774
  250.6 6.2 %collective-permute-start.19 = (f32[128,128]{1,0:T(8,128)S(1)}, f32[128,128]{1,0:T(8,128)S(1)}, u32[]{:S(2)}, u32[]{:S(2)}) collective-permute-start(f32[128,128]{1,0:T(8,128)S(1)} %add_add_fusion), channel_id=1, source_target_pairs={{0,2},{1,3},{2,4},{3,5},{4,6},{5,7},{6,0},{7,1},{8,10},{9,11},{10,... | collective-permute-start | bytes 196616 | tf_op jit(solution)/shard_map/ppermute | solution.py:774
  251.6 8.2 %copy-start.19 = (f32[2,2,2,32,2,2,128]{6,3,4,2,5,0,1:T(8,128)S(1)}, f32[2,2,2,32,2,2,128]{6,3,4,2,5,0,1:T(8,128)}, u32[]{:S(2)}) copy-start(f32[2,2,2,32,2,2,128]{6,3,4,2,5,0,1:T(8,128)} %copy-done.18) | copy-start | bytes 1572868
  256.8 4.2 %copy-start.15 = (s32[7]{0:T(128)S(1)}, s32[7]{0:T(128)}, u32[]{:S(2)}) copy-start(s32[7]{0:T(128)} %copy-done.14) | copy-start | bytes 88
  256.8 4.1 %collective-permute-start.22 = (f32[4,128,128]{2,1,0:T(8,128)S(1)}, f32[4,128,128]{2,1,0:T(8,128)S(1)}, u32[]{:S(2)}, u32[]{:S(2)}) collective-permute-start(f32[4,128,128]{2,1,0:T(8,128)S(1)} %pad_maximum_fusion.half), channel_id=1, source_target_pairs={{0,1},{1,0},{2,3},{3,2},{4,5},{5,4},{6,7},{7,6},{8,9},{9,8},{10,11... | collective-permute-start | bytes 786440 | tf_op jit(solution)/shard_map/ppermute | solution.py:777

commit v5 on v4

--- a/solution.py
+++ b/solution.py
@@ -102,7 +102,7 @@
             piece()
 
 
-def gradients(strip, probe, amp, right, left, work, fast):
+def gradients(strip, probe, amp, right, left, work, fast, chosen=None):
     sgrad, pgrad, weight, strength = work["sgrad"], work["pgrad"], work["weight"], work["strength"]
     lhs, rhs, far, mid, res, bright = (work[n] for n in ("lhs", "rhs", "far", "mid", "res", "bright"))
     def put_split(ref, at, rows, x):
@@ -241,7 +241,14 @@
         woven([], gradient_rows(3))
         return carry
 
-    lax.fori_loop(0, PATS, one_pattern, 0)
+    def one_chosen(p, carry):
+        @pl.when(((chosen >> p) & 1) == 1)
+        def _():
+            one_pattern(p, 0)
+
+        return carry
+
+    lax.fori_loop(0, PATS, one_pattern if chosen is None else one_chosen, 0)
 
 
 WORK = {
@@ -288,7 +295,7 @@
 
 
 def weak_data(strip, strength, energy):
-    weak = None
+    weak = 0
     for p in range(PATS):
         total = 0.0
         for rh in range(2):
@@ -298,7 +305,7 @@
                     o_re, o_im = strip[0, p + u, full, :], strip[1, p + u, full, :]
                     total = total + strength[rh, u, rows, :] * (o_re * o_re + o_im * o_im)
         small = energy[0, p] < WEAK * WEAK * jnp.sum(total)
-        weak = small if weak is None else jnp.logical_and(weak, small)
+        weak = weak + jnp.where(small, 1 << p, 0)
     return weak
 
 
@@ -413,13 +420,11 @@
     for copy in copies:
         copy.wait()
 
-    @pl.when(weak)
+    gradients(strip, probe, amp, work["right"], work["left"], work, True, weak)
+
+    @pl.when(weak != 2**PATS - 1)
     def _():
-        gradients(strip, probe, amp, work["right"], work["left"], work, True)
-
-    @pl.when(jnp.logical_not(weak))
-    def _():
-        gradients(strip, probe, amp, work["right"], work["left"], work, False)
+        gradients(strip, probe, amp, work["right"], work["left"], work, False, 2**PATS - 1 - weak)
 
     hand_over(info, probe, pgrad, weight, kept, given, True)
     out_copies = [

time: 263 us -> 263 us (level)
  no operation moved by 1% of the time
where the time goes in v5:
time: 263 us; the launch traced here: 262 us
  waiting for transfers between devices  73.8 us (28%)
  blocking collectives  70.3 us (27%)
  starting transfers between devices  49.4 us (19%)
  Pallas kernels  49.4 us (19%)
  local copies, waits for them, and re-layouts  13.5 us (5%)
  between operations  3.01 us (1%)
  other arithmetic  2.92 us (1%)
    all_to_all x2, blocking collectives, exchange(): return lax.all_to_all(x, 'scan', split_axis=0, concat_axis=0, tiled=True)  70.3 us
    ppermute x6, waiting for transfers between devices, sum_turned(): lax.ppermute(parts[k], axis, perm_of(k))  30.7 us
    pallas_call x1, Pallas kernels, body(): kernel(first_kernel, (shaped(2, GROUPS, SIDE, HALF), shaped(N_SCAN, SEND_...  20.9 us
    all_to_all x3, starting transfers between devices, exchange(): return lax.all_to_all(x, 'scan', split_axis=0, concat_axis=0, tiled=True)  19.4 us
    all_to_all x3, waiting for transfers between devices, exchange(): return lax.all_to_all(x, 'scan', split_axis=0, concat_axis=0, tiled=True)  18.4 us
    pallas_call x1, Pallas kernels, body(): kernel(second_kernel, (shaped(96, TILE, HALF), shaped(MODES, 2, 2, HALF,...  16.1 us
    ppermute x3, waiting for transfers between devices, gather_rows(): got = lax.ppermute(x, axis, perm_of(k))  9.74 us
    ppermute x6, starting transfers between devices, sum_all(): near, far, middle = (lax.ppermute(x, axis, perm_of(k)) for k in (1, 3, 2))  8.66 us
  transfers between devices with their start and end apart: 26, of which 17 were waited for; matrix products, arithmetic and copies ran while one was open for 4% of the time, Pallas kernels for 3%

profile of v5, /device:TPU:1, one launch (start us, length us, event | category | flops | bytes accessed | tf_op | source)
XLA Modules:
  0.0 262.4 jit_solution(10882904972641573931)
XLA Ops:
  0.6 0.8 slice_reduce_fusion
  1.4 0.6 broadcast_in_dim.26
  2.1 9.6 %all-to-all-start = ((s32[32,1,2]{2,1,0:T(1,128)}), s32[32,1,2]{2,1,0:T(1,128)S(1)}, u32[]{:S(2)}, u32[]{:S(2)}) async-start(s32[32,1,2]{2,1,0:T(1,128)} %broadcast_in_dim.26), calls=%async_computation | async-start | bytes 32768 | tf_op jit(solution)/shard_map/all_to_all | solution.py:634
  11.7 0.6 fusion.6
  14.2 0.7 stack.63.info
  14.9 3.6 %all-to-all-done = s32[32,1,2]{2,1,0:T(1,128)S(1)} async-done(((s32[32,1,2]{2,1,0:T(1,128)}), s32[32,1,2]{2,1,0:T(1,128)S(1)}, u32[]{:S(2)}, u32[]{:S(2)}) %all-to-all-start) | async-done | bytes 288 | tf_op jit(solution)/shard_map/all_to_all | solution.py:634
  18.5 1.6 copy-done.3
  20.1 2.9 %pack.1 = f32[96,64,128]{2,1,0:T(8,128)} custom-call(s32[32,2]{1,0:T(8,128)S(1)} %bitcast.65, s32[7]{0:T(128)S(1)} %stack.63.info, s32[32]{0:T(128)S(1)} %fusion.5.perm, f32[64,64,128]{2,1,0:T(8,128)S(1)} %bitcast.63), custom_call_target="tpu_custom_call" | custom-call | tf_op jit(solution)/shard_map/pack/pallas_call | solution.py:677
  23.0 5.2 %all-to-all-start.1 = ((f32[96,64,128]{2,1,0:T(8,128)}), f32[96,64,128]{2,1,0:T(8,128)}, u32[]{:S(2)}, u32[]{:S(2)}) async-start(f32[96,64,128]{2,1,0:T(8,128)} %pack.1), calls=%async_computation.1 | async-start | bytes 6291456 | tf_op jit(solution)/shard_map/all_to_all | solution.py:634
  28.3 0.3 reshape.66
  28.6 1.1 broadcast_in_dim.27
  29.7 0.7 dynamic-slice_bitcast_fusion
  30.5 1.2 collective-permute-start
  31.7 1.5 collective-permute-start.1
  33.1 1.5 collective-permute-start.2
  34.7 4.6 %collective-permute-done = f32[2,2,128,128]{3,2,1,0:T(8,128)S(1)} collective-permute-done((f32[2,2,128,128]{3,2,1,0:T(8,128)S(1)}, f32[2,2,128,128]{3,2,1,0:T(8,128)S(1)}, u32[]{:S(2)}, u32[]{:S(2)}) %collective-permute-start) | collective-permute-done | bytes 262176 | tf_op jit(solution)/shard_map/ppermute | solution.py:651
  39.2 0.7 bitcast_dynamic-update-slice_fusion.2
  40.0 0.7 bitcast_dynamic-update-slice_fusion.1
  40.7 5.2 %collective-permute-done.2 = f32[2,2,128,128]{3,2,1,0:T(8,128)S(1)} collective-permute-done((f32[2,2,128,128]{3,2,1,0:T(8,128)S(1)}, f32[2,2,128,128]{3,2,1,0:T(8,128)S(1)}, u32[]{:S(2)}, u32[]{:S(2)}) %collective-permute-start.2) | collective-permute-done | bytes 262176 | tf_op jit(solution)/shard_map/ppermute | solution.py:651
  45.8 0.7 bitcast_dynamic-update-slice_fusion
  46.6 1.1 collective-permute-start.3
  47.7 1.2 spread.1
  48.9 1.0 copy-done.7
  49.9 0.4 collective-permute-done.3
  50.3 2.4 maximum_select_fusion.probe.old_probe
  52.8 14.8 %all-to-all-done.1.tiles = f32[96,64,128]{2,1,0:T(8,128)} async-done(((f32[96,64,128]{2,1,0:T(8,128)}), f32[96,64,128]{2,1,0:T(8,128)}, u32[]{:S(2)}, u32[]{:S(2)}) %all-to-all-start.1) | async-done | bytes 3145760 | tf_op jit(solution)/shard_map/all_to_all | solution.py:634
  67.6 1.2 copy-done.5
  68.8 1.2 copy-done.8
  70.0 20.9 %first.1 = (f32[2,5,256,128]{3,2,1,0:T(8,128)S(1)}, f32[32,144,128]{2,1,0:T(8,128)S(1)}, f32[4,2,2,128,128]{4,3,2,1,0:T(8,128)S(1)}, f32[4,2,2,128,128]{4,3,2,1,0:T(8,128)S(1)}, f32[1,1]{1,0:T(1,128)}) custom-call(s32[7]{0:T(128)S(1)} %stack.63.info, s32[32]{0:T(128)S(1)} %fusion.5.perm, f32[96,64,128]{2,1,0:T(8,128)} %all-to-all-done.1.tiles, ...), custom_call_target="tpu_custom_call" | custom-call | tf_op jit(solution)/shard_map/first/pallas_call | solution.py:700
  90.9 2.9 %collective-permute-start.4 = (f32[4,2,2,128,128]{4,3,2,1,0:T(8,128)S(1)}, f32[4,2,2,128,128]{4,3,2,1,0:T(8,128)S(1)}, u32[]{:S(2)}, u32[]{:S(2)}) collective-permute-start(f32[4,2,2,128,128]{4,3,2,1,0:T(8,128)S(1)} %get-tuple-element.22), channel_id=1, source_target_pairs={{0,1},{1,0},{2,3},{3,2},{4,5},{5,4},{6,7},{7,6},{8,9},{9,8},{10,11... | collective-permute-start | bytes 3145736 | tf_op jit(solution)/shard_map/ppermute | solution.py:716
  93.9 2.3 collective-permute-done.4
  96.2 0.2 add.120
  96.4 34.6 %all_to_all.25.arrived = f32[32,144,128]{2,1,0:T(8,128)S(1)} all-to-all(f32[32,144,128]{2,1,0:T(8,128)S(1)} %constant_dynamic-update-slice_fusion.1.first_in), channel_id=1, replica_groups=mesh['grp'=4,'scan'=32] {'scan'}, dimensions={0} | all-to-all | bytes 4718592 | tf_op jit(solution)/shard_map/all_to_all | solution.py:634
  131.0 0.1 sums.1
  131.2 2.6 collective-permute-start.7
  133.7 1.7 collective-permute-start.5
  135.5 1.7 owner.1
  137.2 2.6 %collective-permute-done.6 = f32[2,64,128]{2,1,0:T(8,128)S(1)} collective-permute-done((f32[2,64,128]{2,1,0:T(8,128)S(1)}, f32[2,64,128]{2,1,0:T(8,128)S(1)}, u32[]{:S(2)}, u32[]{:S(2)}) %collective-permute-start.6) | collective-permute-done | bytes 65568 | tf_op jit(solution)/shard_map/ppermute | solution.py:643
  140.1 35.7 %all_to_all.26.total_in = f32[32,144,128]{2,1,0:T(8,128)S(1)} all-to-all(f32[32,144,128]{2,1,0:T(8,128)S(1)} %constant_dynamic-update-slice_fusion), channel_id=1, replica_groups=mesh['grp'=4,'scan'=32] {'scan'}, dimensions={0} | all-to-all | bytes 4718592 | tf_op jit(solution)/shard_map/all_to_all | solution.py:634
  175.9 0.3 collective-permute-start.8
  176.2 2.5 collective-permute-done.8.other_in
  178.7 16.1 %second.1 = (f32[96,64,128]{2,1,0:T(8,128)}, f32[4,2,2,128,128]{4,3,2,1,0:T(8,128)S(1)}, f32[4,2,2,128,128]{4,3,2,1,0:T(8,128)S(1)}) custom-call(s32[7]{0:T(128)S(1)} %stack.63.info, s32[32]{0:T(128)S(1)} %fusion.5.perm, f32[1,1]{1,0:T(1,128)} %get-tuple-element.17.peak, f32[1,4]{1,0:T(1,128)S(1)} %get-tuple-element.18.energy, ...), custom_call_target="tpu_custom_call" | custom-call | tf_op jit(solution)/shard_map/second/pallas_call | solution.py:738
  194.8 4.6 %all-to-all-start.4 = ((f32[96,64,128]{2,1,0:T(8,128)}), f32[96,64,128]{2,1,0:T(8,128)}, u32[]{:S(2)}, u32[]{:S(2)}) async-start(f32[96,64,128]{2,1,0:T(8,128)} %get-tuple-element.25), calls=%async_computation.4 | async-start | bytes 6291456 | tf_op jit(solution)/shard_map/all_to_all | solution.py:634
  199.5 0.4 collective-permute-start.9
  199.9 2.3 collective-permute-done.9
  202.2 0.1 slice_add_fusion
  202.4 2.7 %collective-permute-start.12 = (f32[4,128,128]{2,1,0:T(8,128)S(1)}, f32[4,128,128]{2,1,0:T(8,128)S(1)}, u32[]{:S(2)}, u32[]{:S(2)}) collective-permute-start(f32[4,128,128]{2,1,0:T(8,128)S(1)} %bitcast.74), channel_id=1, source_target_pairs={{0,96},{32,0},{64,32},{96,64},{1,97},{33,1},{65,33},{97,65},{2,98}... | collective-permute-start | bytes 786440 | tf_op jit(solution)/shard_map/ppermute | solution.py:638
  205.1 0.7 collective-permute-start.10
  205.8 5.5 %collective-permute-done.11 = f32[4,128,128]{2,1,0:T(8,128)S(1)} collective-permute-done((f32[4,128,128]{2,1,0:T(8,128)S(1)}, f32[4,128,128]{2,1,0:T(8,128)S(1)}, u32[]{:S(2)}, u32[]{:S(2)}) %collective-permute-start.11) | collective-permute-done | bytes 262176 | tf_op jit(solution)/shard_map/ppermute | solution.py:638
  211.3 6.3 %collective-permute-done.10 = f32[4,128,128]{2,1,0:T(8,128)S(1)} collective-permute-done((f32[4,128,128]{2,1,0:T(8,128)S(1)}, f32[4,128,128]{2,1,0:T(8,128)S(1)}, u32[]{:S(2)}, u32[]{:S(2)}) %collective-permute-start.10) | collective-permute-done | bytes 262176 | tf_op jit(solution)/shard_map/ppermute | solution.py:638
  217.7 2.7 %collective-permute-start.15 = (f32[128,128]{1,0:T(8,128)S(1)}, f32[128,128]{1,0:T(8,128)S(1)}, u32[]{:S(2)}, u32[]{:S(2)}) collective-permute-start(f32[128,128]{1,0:T(8,128)S(1)} %get-tuple-element.36), channel_id=1, source_target_pairs={{0,6},{1,7},{2,0},{3,1},{4,2},{5,3},{6,4},{7,5},{8,14},{9,15},{10,... | collective-permute-start | bytes 196616 | tf_op jit(solution)/shard_map/ppermute | solution.py:638
  220.3 1.7 collective-permute-start.13
  222.1 14.9 %collective-permute-done.15 = f32[128,128]{1,0:T(8,128)S(1)} collective-permute-done((f32[128,128]{1,0:T(8,128)S(1)}, f32[128,128]{1,0:T(8,128)S(1)}, u32[]{:S(2)}, u32[]{:S(2)}) %collective-permute-start.15) | collective-permute-done | bytes 65568 | tf_op jit(solution)/shard_map/ppermute | solution.py:638
  237.0 1.1 collective-permute-done.14
  238.1 2.9 %collective-permute-done.13 = f32[128,128]{1,0:T(8,128)S(1)} collective-permute-done((f32[128,128]{1,0:T(8,128)S(1)}, f32[128,128]{1,0:T(8,128)S(1)}, u32[]{:S(2)}, u32[]{:S(2)}) %collective-permute-start.13) | collective-permute-done | bytes 65568 | tf_op jit(solution)/shard_map/ppermute | solution.py:638
  241.0 3.1 %collective-permute-start.18 = (f32[128,128]{1,0:T(8,128)S(1)}, f32[128,128]{1,0:T(8,128)S(1)}, u32[]{:S(2)}, u32[]{:S(2)}) collective-permute-start(f32[128,128]{1,0:T(8,128)S(1)} %fusion.4), channel_id=1, source_target_pairs={{0,24},{1,25},{2,26},{3,27},{4,28},{5,29},{6,30},{7,31},{8,0},{9,1... | collective-permute-start | bytes 196616 | tf_op jit(solution)/shard_map/ppermute | solution.py:643
  244.1 1.3 collective-permute-start.16
  245.4 3.7 %collective-permute-done.17 = f32[128,128]{1,0:T(8,128)S(1)} collective-permute-done((f32[128,128]{1,0:T(8,128)S(1)}, f32[128,128]{1,0:T(8,128)S(1)}, u32[]{:S(2)}, u32[]{:S(2)}) %collective-permute-start.17) | collective-permute-done | bytes 65568 | tf_op jit(solution)/shard_map/ppermute | solution.py:643
  249.2 1.4 collective-permute-start.20
  250.7 1.0 constant_dynamic-slice_fusion.1
  251.7 5.1 %unpack.1 = f32[64,64,128]{2,1,0:T(8,128)} custom-call(s32[32,2]{1,0:T(8,128)} %bitcast.67, s32[7]{0:T(128)} %copy-done.14, s32[32]{0:T(128)} %copy-done.16, f32[64,64,128]{2,1,0:T(8,128)} %bitcast.62, f32[96,64,128]{2,1,0:T(8,128)} %all-to-all-done.4.arrived), custom_call_target="tpu_custom_call" | custom-call | bytes 8388608 | tf_op jit(solution)/shard_map/unpack/pallas_call | solution.py:765
  256.8 2.9 %collective-permute-start.22 = (f32[4,128,128]{2,1,0:T(8,128)S(1)}, f32[4,128,128]{2,1,0:T(8,128)S(1)}, u32[]{:S(2)}, u32[]{:S(2)}) collective-permute-start(f32[4,128,128]{2,1,0:T(8,128)S(1)} %pad_maximum_fusion.half), channel_id=1, source_target_pairs={{0,1},{1,0},{2,3},{3,2},{4,5},{5,4},{6,7},{7,6},{8,9},{9,8},{10,11... | collective-permute-start | bytes 786440 | tf_op jit(solution)/shard_map/ppermute | solution.py:782
  259.9 1.1 collective-permute-done.22.other_half
  261.0 1.4 finish.1
  (71 shorter events, 1.1 us)
Async XLA Ops:
  0.6 13.5 %copy-start = (s32[4,32]{1,0:T(4,128)S(1)}, s32[4,32]{1,0:T(4,128)}, u32[]{:S(2)}) copy-start(s32[4,32]{1,0:T(4,128)} %param.10) | copy-start | bytes 1540
  2.1 16.5 %all-to-all-start = ((s32[32,1,2]{2,1,0:T(1,128)}), s32[32,1,2]{2,1,0:T(1,128)S(1)}, u32[]{:S(2)}, u32[]{:S(2)}) async-start(s32[32,1,2]{2,1,0:T(1,128)} %broadcast_in_dim.26), calls=%async_computation | async-start | bytes 32768 | tf_op jit(solution)/shard_map/all_to_all | solution.py:634
  14.2 164.5 %copy-start.16 = (s32[32]{0:T(128)}, s32[32]{0:T(128)S(1)}, u32[]{:S(2)}) copy-start(s32[32]{0:T(128)S(1)} %fusion.5.perm) | copy-start | bytes 388
  14.9 163.8 %copy-start.14 = (s32[7]{0:T(128)}, s32[7]{0:T(128)S(1)}, u32[]{:S(2)}) copy-start(s32[7]{0:T(128)S(1)} %stack.63.info) | copy-start | bytes 88
  18.5 116.9 %copy-start.12 = (s32[32,1,2]{2,1,0:T(1,128)}, s32[32,1,2]{2,1,0:T(1,128)S(1)}, u32[]{:S(2)}) copy-start(s32[32,1,2]{2,1,0:T(1,128)S(1)} %all-to-all-done) | copy-start | bytes 772
  18.5 1.6 copy-start.3
  23.0 5.2 %copy-start.21 = (f32[1,2,256,256]{3,2,1,0:T(8,128)S(1)}, f32[1,2,256,256]{3,2,1,0:T(8,128)}, u32[]{:S(2)}) copy-start(f32[1,2,256,256]{3,2,1,0:T(8,128)} %param.12) | copy-start | bytes 1572868
  23.0 44.5 %all-to-all-start.1 = ((f32[96,64,128]{2,1,0:T(8,128)}), f32[96,64,128]{2,1,0:T(8,128)}, u32[]{:S(2)}, u32[]{:S(2)}) async-start(f32[96,64,128]{2,1,0:T(8,128)} %pack.1), calls=%async_computation.1 | async-start | bytes 6291456 | tf_op jit(solution)/shard_map/all_to_all | solution.py:634
  28.5 19.2 %copy-start.11 = (f32[4,256,256]{2,1,0:T(8,128)S(1)}, f32[4,256,256]{2,1,0:T(8,128)}, u32[]{:S(2)}) copy-start(f32[4,256,256]{2,1,0:T(8,128)} %amp.1) | copy-start | bytes 3145732
  28.5 19.2 %copy-start.13 = (bf16[256,256]{1,0:T(8,128)(2,1)S(1)}, bf16[256,256]{1,0:T(8,128)(2,1)}, u32[]{:S(2)}) copy-start(bf16[256,256]{1,0:T(8,128)(2,1)} %constant.124.clone.shuffle) | copy-start | bytes 393220
  28.6 21.7 %copy-start.18 = (f32[2,2,2,32,2,2,128]{6,3,4,2,5,0,1:T(8,128)}, f32[2,2,2,32,2,2,128]{6,3,4,2,5,0,1:T(8,128)S(1)}, u32[]{:S(2)}) copy-start(f32[2,2,2,32,2,2,128]{6,3,4,2,5,0,1:T(8,128)S(1)} %copy.19) | copy-start | bytes 1572868
  30.5 8.8 %collective-permute-start = (f32[2,2,128,128]{3,2,1,0:T(8,128)S(1)}, f32[2,2,128,128]{3,2,1,0:T(8,128)S(1)}, u32[]{:S(2)}, u32[]{:S(2)}) collective-permute-start(f32[2,2,128,128]{3,2,1,0:T(8,128)S(1)} %get-tuple-element.34), channel_id=1, source_target_pairs={{0,32},{32,64},{64,96},{96,0},{1,33},{33,65},{65,97},{97,1},{2,34}... | collective-permute-start | bytes 786440 | tf_op jit(solution)/shard_map/ppermute | solution.py:651
  31.7 8.3 %collective-permute-start.1 = (f32[2,2,128,128]{3,2,1,0:T(8,128)S(1)}, f32[2,2,128,128]{3,2,1,0:T(8,128)S(1)}, u32[]{:S(2)}, u32[]{:S(2)}) collective-permute-start(f32[2,2,128,128]{3,2,1,0:T(8,128)S(1)} %get-tuple-element.34), channel_id=1, source_target_pairs={{0,96},{32,0},{64,32},{96,64},{1,97},{33,1},{65,33},{97,65},{2,98}... | collective-permute-start | bytes 786440 | tf_op jit(solution)/shard_map/ppermute | solution.py:651
  33.1 12.7 %collective-permute-start.2 = (f32[2,2,128,128]{3,2,1,0:T(8,128)S(1)}, f32[2,2,128,128]{3,2,1,0:T(8,128)S(1)}, u32[]{:S(2)}, u32[]{:S(2)}) collective-permute-start(f32[2,2,128,128]{3,2,1,0:T(8,128)S(1)} %get-tuple-element.34), channel_id=1, source_target_pairs={{0,64},{32,96},{64,0},{96,32},{1,65},{33,97},{65,1},{97,33},{2,66}... | collective-permute-start | bytes 786440 | tf_op jit(solution)/shard_map/ppermute | solution.py:651
  46.6 3.8 %collective-permute-start.3 = (f32[4,2,2,128,128]{4,3,2,1,0:T(8,128)}, f32[4,2,2,128,128]{4,3,2,1,0:T(8,128)}, u32[]{:S(2)}, u32[]{:S(2)}) collective-permute-start(f32[4,2,2,128,128]{4,3,2,1,0:T(8,128)} %bitcast_dynamic-update-slice_fusion), channel_id=1, source_target_pairs={{0,1},{1,0},{2,3},{3,2},{4,5},{5,4},{6,7},{7,6},{8,9},{9,8},{10,11... | collective-permute-start | bytes 3145736 | tf_op jit(solution)/shard_map/ppermute | solution.py:689
  48.9 1.0 copy-start.7
  49.9 17.6 %copy-start.4 = (bf16[4,256,512]{2,1,0:T(8,128)(2,1)S(1)}, bf16[4,256,512]{2,1,0:T(8,128)(2,1)}, u32[]{:S(2)}) copy-start(bf16[4,256,512]{2,1,0:T(8,128)(2,1)} %constant.123.clone.left_in) | copy-start | bytes 3145732
  52.8 38.2 %copy-start.1 = (f32[4,2,2,2,128,128]{5,4,3,2,1,0:T(8,128)}, f32[4,2,2,2,128,128]{5,4,3,2,1,0:T(8,128)S(1)}, u32[]{:S(2)}) copy-start(f32[4,2,2,2,128,128]{5,4,3,2,1,0:T(8,128)S(1)} %maximum_select_fusion.probe.old_probe) | copy-start | bytes 6291460
  67.6 1.2 copy-start.5
  68.8 1.2 copy-start.8
  90.9 5.5 %copy-start.10 = (f32[2,5,256,128]{3,2,1,0:T(8,128)}, f32[2,5,256,128]{3,2,1,0:T(8,128)S(1)}, u32[]{:S(2)}) copy-start(f32[2,5,256,128]{3,2,1,0:T(8,128)S(1)} %get-tuple-element.19.old_strip) | copy-start | bytes 3932164
  90.9 5.2 %collective-permute-start.4 = (f32[4,2,2,128,128]{4,3,2,1,0:T(8,128)S(1)}, f32[4,2,2,128,128]{4,3,2,1,0:T(8,128)S(1)}, u32[]{:S(2)}, u32[]{:S(2)}) collective-permute-start(f32[4,2,2,128,128]{4,3,2,1,0:T(8,128)S(1)} %get-tuple-element.22), channel_id=1, source_target_pairs={{0,1},{1,0},{2,3},{3,2},{4,5},{5,4},{6,7},{7,6},{8,9},{9,8},{10,11... | collective-permute-start | bytes 3145736 | tf_op jit(solution)/shard_map/ppermute | solution.py:716
  96.4 34.6 %copy-start.2 = (f32[32,144,128]{2,1,0:T(8,128)}, f32[32,144,128]{2,1,0:T(8,128)S(1)}, u32[]{:S(2)}) copy-start(f32[32,144,128]{2,1,0:T(8,128)S(1)} %constant_dynamic-update-slice_fusion.1.first_in) | copy-start | bytes 7077892
  131.2 6.0 %collective-permute-start.7 = (f32[2,64,128]{2,1,0:T(8,128)S(1)}, f32[2,64,128]{2,1,0:T(8,128)S(1)}, u32[]{:S(2)}, u32[]{:S(2)}) collective-permute-start(f32[2,64,128]{2,1,0:T(8,128)S(1)} %sums.1), channel_id=1, source_target_pairs={{0,96},{32,0},{64,32},{96,64},{1,97},{33,1},{65,33},{97,65},{2,98}... | collective-permute-start | bytes 196616 | tf_op jit(solution)/shard_map/ppermute | solution.py:643
  133.7 6.1 %collective-permute-start.6 = (f32[2,64,128]{2,1,0:T(8,128)S(1)}, f32[2,64,128]{2,1,0:T(8,128)S(1)}, u32[]{:S(2)}, u32[]{:S(2)}) collective-permute-start(f32[2,64,128]{2,1,0:T(8,128)S(1)} %sums.1), channel_id=1, source_target_pairs={{0,32},{32,64},{64,96},{96,0},{1,33},{33,65},{65,97},{97,1},{2,34}... | collective-permute-start | bytes 196616 | tf_op jit(solution)/shard_map/ppermute | solution.py:643
  133.7 6.1 %collective-permute-start.5 = (f32[2,64,128]{2,1,0:T(8,128)S(1)}, f32[2,64,128]{2,1,0:T(8,128)S(1)}, u32[]{:S(2)}, u32[]{:S(2)}) collective-permute-start(f32[2,64,128]{2,1,0:T(8,128)S(1)} %sums.1), channel_id=1, source_target_pairs={{0,64},{32,96},{64,0},{96,32},{1,65},{33,97},{65,1},{97,33},{2,66}... | collective-permute-start | bytes 196616 | tf_op jit(solution)/shard_map/ppermute | solution.py:643
  140.1 38.6 %copy-start.6 = (bf16[4,512,256]{2,1,0:T(8,128)(2,1)S(1)}, bf16[4,512,256]{2,1,0:T(8,128)(2,1)}, u32[]{:S(2)}) copy-start(bf16[4,512,256]{2,1,0:T(8,128)(2,1)} %constant.122.clone.right_in) | copy-start | bytes 3145732
  140.1 38.6 %copy-start.9 = (f32[4,2,128,256]{3,2,1,0:T(8,128)S(1)}, f32[4,2,128,256]{3,2,1,0:T(8,128)}, u32[]{:S(2)}) copy-start(f32[4,2,128,256]{3,2,1,0:T(8,128)} %copy-done.7) | copy-start | bytes 3145732
  175.8 2.9 %copy-start.17 = (f32[32,144,128]{2,1,0:T(8,128)}, f32[32,144,128]{2,1,0:T(8,128)S(1)}, u32[]{:S(2)}) copy-start(f32[32,144,128]{2,1,0:T(8,128)S(1)} %all_to_all.26.total_in) | copy-start | bytes 7077892
  175.9 2.8 %copy-start.20 = (f32[32,64,128]{2,1,0:T(8,128)}, f32[32,64,128]{2,1,0:T(8,128)S(1)}, u32[]{:S(2)}) copy-start(f32[32,64,128]{2,1,0:T(8,128)S(1)} %slice.74) | copy-start | bytes 3145732
  175.9 2.7 %collective-permute-start.8 = (f32[32,64,128]{2,1,0:T(8,128)S(1)}, f32[32,64,128]{2,1,0:T(8,128)S(1)}, u32[]{:S(2)}, u32[]{:S(2)}) collective-permute-start(f32[32,64,128]{2,1,0:T(8,128)S(1)} %slice.74), channel_id=1, source_target_pairs={{0,1},{1,0},{2,3},{3,2},{4,5},{5,4},{6,7},{7,6},{8,9},{9,8},{10,11... | collective-permute-start | bytes 3145736 | tf_op jit(solution)/shard_map/ppermute | solution.py:736
  194.8 56.8 %all-to-all-start.4 = ((f32[96,64,128]{2,1,0:T(8,128)}), f32[96,64,128]{2,1,0:T(8,128)}, u32[]{:S(2)}, u32[]{:S(2)}) async-start(f32[96,64,128]{2,1,0:T(8,128)} %get-tuple-element.25), calls=%async_computation.4 | async-start | bytes 6291456 | tf_op jit(solution)/shard_map/all_to_all | solution.py:634
  199.5 2.7 %collective-permute-start.9 = (f32[4,2,2,128,128]{4,3,2,1,0:T(8,128)S(1)}, f32[4,2,2,128,128]{4,3,2,1,0:T(8,128)S(1)}, u32[]{:S(2)}, u32[]{:S(2)}) collective-permute-start(f32[4,2,2,128,128]{4,3,2,1,0:T(8,128)S(1)} %get-tuple-element.24), channel_id=1, source_target_pairs={{0,1},{1,0},{2,3},{3,2},{4,5},{5,4},{6,7},{7,6},{8,9},{9,8},{10,11... | collective-permute-start | bytes 3145736 | tf_op jit(solution)/shard_map/ppermute | solution.py:760
  202.3 8.9 %collective-permute-start.11 = (f32[4,128,128]{2,1,0:T(8,128)S(1)}, f32[4,128,128]{2,1,0:T(8,128)S(1)}, u32[]{:S(2)}, u32[]{:S(2)}) collective-permute-start(f32[4,128,128]{2,1,0:T(8,128)S(1)} %bitcast.75), channel_id=1, source_target_pairs={{0,32},{32,64},{64,96},{96,0},{1,33},{33,65},{65,97},{97,1},{2,34}... | collective-permute-start | bytes 786440 | tf_op jit(solution)/shard_map/ppermute | solution.py:638
  202.4 8.9 %collective-permute-start.12 = (f32[4,128,128]{2,1,0:T(8,128)S(1)}, f32[4,128,128]{2,1,0:T(8,128)S(1)}, u32[]{:S(2)}, u32[]{:S(2)}) collective-permute-start(f32[4,128,128]{2,1,0:T(8,128)S(1)} %bitcast.74), channel_id=1, source_target_pairs={{0,96},{32,0},{64,32},{96,64},{1,97},{33,1},{65,33},{97,65},{2,98}... | collective-permute-start | bytes 786440 | tf_op jit(solution)/shard_map/ppermute | solution.py:638
  205.1 12.5 %collective-permute-start.10 = (f32[4,128,128]{2,1,0:T(8,128)S(1)}, f32[4,128,128]{2,1,0:T(8,128)S(1)}, u32[]{:S(2)}, u32[]{:S(2)}) collective-permute-start(f32[4,128,128]{2,1,0:T(8,128)S(1)} %bitcast.73), channel_id=1, source_target_pairs={{0,64},{32,96},{64,0},{96,32},{1,65},{33,97},{65,1},{97,33},{2,66}... | collective-permute-start | bytes 786440 | tf_op jit(solution)/shard_map/ppermute | solution.py:638
  217.7 19.3 %collective-permute-start.15 = (f32[128,128]{1,0:T(8,128)S(1)}, f32[128,128]{1,0:T(8,128)S(1)}, u32[]{:S(2)}, u32[]{:S(2)}) collective-permute-start(f32[128,128]{1,0:T(8,128)S(1)} %get-tuple-element.36), channel_id=1, source_target_pairs={{0,6},{1,7},{2,0},{3,1},{4,2},{5,3},{6,4},{7,5},{8,14},{9,15},{10,... | collective-permute-start | bytes 196616 | tf_op jit(solution)/shard_map/ppermute | solution.py:638
  220.3 17.8 %collective-permute-start.14 = (f32[128,128]{1,0:T(8,128)S(1)}, f32[128,128]{1,0:T(8,128)S(1)}, u32[]{:S(2)}, u32[]{:S(2)}) collective-permute-start(f32[128,128]{1,0:T(8,128)S(1)} %get-tuple-element.37), channel_id=1, source_target_pairs={{0,2},{1,3},{2,4},{3,5},{4,6},{5,7},{6,0},{7,1},{8,10},{9,11},{10,... | collective-permute-start | bytes 196616 | tf_op jit(solution)/shard_map/ppermute | solution.py:638
  220.3 20.6 %collective-permute-start.13 = (f32[128,128]{1,0:T(8,128)S(1)}, f32[128,128]{1,0:T(8,128)S(1)}, u32[]{:S(2)}, u32[]{:S(2)}) collective-permute-start(f32[128,128]{1,0:T(8,128)S(1)} %get-tuple-element.38), channel_id=1, source_target_pairs={{0,4},{1,5},{2,6},{3,7},{4,0},{5,1},{6,2},{7,3},{8,12},{9,13},{10,... | collective-permute-start | bytes 196616 | tf_op jit(solution)/shard_map/ppermute | solution.py:638
  241.0 4.4 %collective-permute-start.18 = (f32[128,128]{1,0:T(8,128)S(1)}, f32[128,128]{1,0:T(8,128)S(1)}, u32[]{:S(2)}, u32[]{:S(2)}) collective-permute-start(f32[128,128]{1,0:T(8,128)S(1)} %fusion.4), channel_id=1, source_target_pairs={{0,24},{1,25},{2,26},{3,27},{4,28},{5,29},{6,30},{7,31},{8,0},{9,1... | collective-permute-start | bytes 196616 | tf_op jit(solution)/shard_map/ppermute | solution.py:643
  244.1 5.0 %collective-permute-start.17 = (f32[128,128]{1,0:T(8,128)S(1)}, f32[128,128]{1,0:T(8,128)S(1)}, u32[]{:S(2)}, u32[]{:S(2)}) collective-permute-start(f32[128,128]{1,0:T(8,128)S(1)} %fusion.4), channel_id=1, source_target_pairs={{0,8},{1,9},{2,10},{3,11},{4,12},{5,13},{6,14},{7,15},{8,16},{9,17... | collective-permute-start | bytes 196616 | tf_op jit(solution)/shard_map/ppermute | solution.py:643
  244.1 5.0 %collective-permute-start.16 = (f32[128,128]{1,0:T(8,128)S(1)}, f32[128,128]{1,0:T(8,128)S(1)}, u32[]{:S(2)}, u32[]{:S(2)}) collective-permute-start(f32[128,128]{1,0:T(8,128)S(1)} %fusion.4), channel_id=1, source_target_pairs={{0,16},{1,17},{2,18},{3,19},{4,20},{5,21},{6,22},{7,23},{8,24},{9,... | collective-permute-start | bytes 196616 | tf_op jit(solution)/shard_map/ppermute | solution.py:643
  249.1 7.6 %collective-permute-start.21 = (f32[128,128]{1,0:T(8,128)S(1)}, f32[128,128]{1,0:T(8,128)S(1)}, u32[]{:S(2)}, u32[]{:S(2)}) collective-permute-start(f32[128,128]{1,0:T(8,128)S(1)} %add_add_fusion), channel_id=1, source_target_pairs={{0,6},{1,7},{2,0},{3,1},{4,2},{5,3},{6,4},{7,5},{8,14},{9,15},{10,... | collective-permute-start | bytes 196616 | tf_op jit(solution)/shard_map/ppermute | solution.py:779
  249.2 7.6 %collective-permute-start.20 = (f32[128,128]{1,0:T(8,128)S(1)}, f32[128,128]{1,0:T(8,128)S(1)}, u32[]{:S(2)}, u32[]{:S(2)}) collective-permute-start(f32[128,128]{1,0:T(8,128)S(1)} %add_add_fusion), channel_id=1, source_target_pairs={{0,4},{1,5},{2,6},{3,7},{4,0},{5,1},{6,2},{7,3},{8,12},{9,13},{10,... | collective-permute-start | bytes 196616 | tf_op jit(solution)/shard_map/ppermute | solution.py:779
  250.6 6.2 %collective-permute-start.19 = (f32[128,128]{1,0:T(8,128)S(1)}, f32[128,128]{1,0:T(8,128)S(1)}, u32[]{:S(2)}, u32[]{:S(2)}) collective-permute-start(f32[128,128]{1,0:T(8,128)S(1)} %add_add_fusion), channel_id=1, source_target_pairs={{0,2},{1,3},{2,4},{3,5},{4,6},{5,7},{6,0},{7,1},{8,10},{9,11},{10,... | collective-permute-start | bytes 196616 | tf_op jit(solution)/shard_map/ppermute | solution.py:779
  251.7 8.2 %copy-start.19 = (f32[2,2,2,32,2,2,128]{6,3,4,2,5,0,1:T(8,128)S(1)}, f32[2,2,2,32,2,2,128]{6,3,4,2,5,0,1:T(8,128)}, u32[]{:S(2)}) copy-start(f32[2,2,2,32,2,2,128]{6,3,4,2,5,0,1:T(8,128)} %copy-done.18) | copy-start | bytes 1572868
  256.8 4.2 %copy-start.15 = (s32[7]{0:T(128)S(1)}, s32[7]{0:T(128)}, u32[]{:S(2)}) copy-start(s32[7]{0:T(128)} %copy-done.14) | copy-start | bytes 88
  256.8 4.1 %collective-permute-start.22 = (f32[4,128,128]{2,1,0:T(8,128)S(1)}, f32[4,128,128]{2,1,0:T(8,128)S(1)}, u32[]{:S(2)}, u32[]{:S(2)}) collective-permute-start(f32[4,128,128]{2,1,0:T(8,128)S(1)} %pad_maximum_fusion.half), channel_id=1, source_target_pairs={{0,1},{1,0},{2,3},{3,2},{4,5},{5,4},{6,7},{7,6},{8,9},{9,8},{10,11... | collective-permute-start | bytes 786440 | tf_op jit(solution)/shard_map/ppermute | solution.py:782
